TPU v7x, 32 devices: a whole 2x2x4 slice. The times are simulated.
32 devices in a mesh: groups: 2 (over y), sec: 4 (over z), tile: 2 (over x), xt: 2 (over core).
Axes of the slice: x: 2, y: 2, z: 4, core: 2. Of those that a mesh axis runs over, the one named last changes fastest.
Arguments:
- volume: float32 [64, 64, 1024], P(('groups', 'sec'), 'tile', 'xt'), parts along dimension 0, may hold values from -6 to 6
Outputs:
- detail_zero: float32 [64, 64, 1024], P(('groups', 'sec'), 'tile', 'xt'), parts along dimension 0
- detail_one: float32 [32, 32, 512], P(('groups', 'sec'), 'tile', 'xt'), parts along dimension 0
- coarsest: float32 [16, 16, 256], P(('groups', 'sec'), 'tile', 'xt'), parts along dimension 0
There are 2 independent parts, one for each index of `groups`. A program takes and returns all parts, laid end to end along the dimension named above; each array names one. Nothing has to cross between parts.
All inputs are finite; a program needn't handle non-finite values.
Results may differ from a plain program's by a relative error of at most 0.00002.
Values sent between devices are 32-bit elements; how exact they have to be, the bound alone decides.
No kernel may reach another device: no remote copies, remote signals or barrier semaphores. Data moves between devices by JAX's collectives and lax.ppermute only.
A program may use at most 64 MiB of HBM per device.

v0:
```python
import math

import jax
import jax.numpy as jnp
from jax import lax
from jax.sharding import PartitionSpec as P

pole_value = math.sqrt(3.0) - 2.0
PREFILTER_TAPS = [math.sqrt(3.0) * pole_value ** abs(offset) for offset in range(-3, 4)]
BINOMIAL_TAPS = [0.0625, 0.25, 0.375, 0.25, 0.0625]


def padded(cells, sides, width):
    for axis, dim in sides:
        count = lax.axis_size(axis)
        ends = count - 1
        head = lax.slice_in_dim(cells, 0, width, axis=dim)
        tail = lax.slice_in_dim(cells, cells.shape[dim] - width, cells.shape[dim], axis=dim)
        cells = jnp.concatenate(
            [
                lax.ppermute(tail, axis, [(i, (i + 1) % count) for i in range(ends)]),
                cells,
                lax.ppermute(head, axis, [((i + 1) % count, i) for i in range(ends)]),
            ],
            axis=dim,
        )
    return cells


def prefilter_valid(padded_in, along):
    length = padded_in.shape[along] - 6
    summed = PREFILTER_TAPS[0] * lax.slice_in_dim(padded_in, 0, length, axis=along)
    for offset in range(1, 7):
        summed = summed + PREFILTER_TAPS[offset] * lax.slice_in_dim(
            padded_in, offset, offset + length, axis=along
        )
    return summed


def reduce_valid(padded_in, along):
    length = padded_in.shape[along] - 4
    summed = BINOMIAL_TAPS[0] * lax.slice_in_dim(padded_in, 0, length, 2, along)
    for offset in range(1, 5):
        summed = summed + BINOMIAL_TAPS[offset] * lax.slice_in_dim(
            padded_in, offset, offset + length, 2, along
        )
    return summed


def expand_valid(padded_in, along):
    length = padded_in.shape[along] - 2
    left_side = lax.slice_in_dim(padded_in, 0, length, axis=along)
    centre = lax.slice_in_dim(padded_in, 1, length + 1, axis=along)
    right_side = lax.slice_in_dim(padded_in, 2, length + 2, axis=along)
    even_part = (left_side + 6.0 * centre + right_side) * 0.125
    odd_part = (centre + right_side) * 0.5
    paired = jnp.stack([even_part, odd_part], axis=along + 1)
    new_shape = list(centre.shape)
    new_shape[along] = 2 * length
    return paired.reshape(new_shape)


def filter_all(padded_in):
    result = padded_in
    for along in range(3):
        result = prefilter_valid(result, along)
    return result


def reduce_all(padded_in):
    result = padded_in
    for along in range(3):
        result = reduce_valid(result, along)
    return result


def expand_all(padded_in):
    result = padded_in
    for along in range(3):
        result = expand_valid(result, along)
    return result


def pad_cols(field, width):
    return jnp.pad(field, ((0, 0), (0, 0), (width, width)))


def shards(volume):
    padded_in = padded(volume, (("sec", 0), ("tile", 1), ("xt", 2)), 3)
    coeffs = filter_all(padded_in)
    reduced = reduce_all(padded(coeffs, (("sec", 0), ("tile", 1), ("xt", 2)), 2))
    half_depth, half_rows, half_cols = reduced.shape
    wide_block = lax.all_gather(reduced, "xt", axis=2, tiled=True)
    level_padded = pad_cols(padded(wide_block, (("sec", 0), ("tile", 1)), 3), 3)
    wide_coeffs = filter_all(level_padded)
    wide_coarse = reduce_all(pad_cols(padded(wide_coeffs, (("sec", 0), ("tile", 1)), 2), 2))
    coarse_padded = pad_cols(padded(wide_coarse, (("sec", 0), ("tile", 1)), 1), 1)
    wide_detail = wide_block - expand_all(coarse_padded)
    col_start = lax.axis_index("xt") * half_cols
    detail_one = lax.dynamic_slice_in_dim(wide_detail, col_start, half_cols, 2)
    coarsest = lax.dynamic_slice_in_dim(wide_coarse, col_start // 2, half_cols // 2, 2)
    level_rim = lax.dynamic_slice_in_dim(
        level_padded[2:-2, 2:-2, :], col_start + 2, half_cols + 2, 2
    )
    detail_zero = volume - expand_all(level_rim)
    return (detail_zero, detail_one, coarsest)


def solution(mesh):
    in_specs = (P(("groups", "sec"), "tile", "xt"),)
    out_specs = (
        P(("groups", "sec"), "tile", "xt"),
        P(("groups", "sec"), "tile", "xt"),
        P(("groups", "sec"), "tile", "xt"),
    )
    return jax.shard_map(shards, mesh=mesh, in_specs=in_specs, out_specs=out_specs, check_vma=False)
```

profile of v0, /device:TPU:0, one launch (start us, length us, event | category | flops | bytes accessed | tf_op | source)
XLA Modules:
  0.0 132.3 jit_solution(952248459747847886)
XLA Ops:
  1.8 4.9 %collective-permute-start = (f32[3,32,512]{2,1,0:T(8,128)S(1)}, f32[3,32,512]{2,1,0:T(8,128)S(1)}, u32[]{:S(2)}, u32[]{:S(2)}) collective-permute-start(f32[3,32,512]{2,1,0:T(8,128)S(1)} %get-tuple-element.29), channel_id=1, source_target_pairs={{0,4},{4,8},{8,12},{1,5},{5,9},{9,13},{2,6},{6,10},{10,14},{3,7},{... | collective-permute-start | bytes 589832 | tf_op jit(solution)/shard_map/ppermute | solution.py:21
  8.0 2.8 %collective-permute-done = f32[3,32,512]{2,1,0:T(8,128)S(1)} collective-permute-done((f32[3,32,512]{2,1,0:T(8,128)S(1)}, f32[3,32,512]{2,1,0:T(8,128)S(1)}, u32[]{:S(2)}, u32[]{:S(2)}) %collective-permute-start) | collective-permute-done | bytes 196640 | tf_op jit(solution)/shard_map/ppermute | solution.py:21
  10.9 4.0 %collective-permute-done.1 = f32[3,32,512]{2,1,0:T(8,128)S(1)} collective-permute-done((f32[3,32,512]{2,1,0:T(8,128)S(1)}, f32[3,32,512]{2,1,0:T(8,128)S(1)}, u32[]{:S(2)}, u32[]{:S(2)}) %collective-permute-start.1) | collective-permute-done | bytes 196640 | tf_op jit(solution)/shard_map/ppermute | solution.py:23
  16.4 4.6 %collective-permute-start.2 = (f32[14,3,512]{2,0,1:T(8,128)S(1)}, f32[14,3,512]{2,0,1:T(8,128)S(1)}, u32[]{:S(2)}, u32[]{:S(2)}) collective-permute-start(f32[14,3,512]{2,0,1:T(8,128)S(1)} %copy.127), channel_id=1, source_target_pairs={{0,2},{1,3},{4,6},{5,7},{8,10},{9,11},{12,14},{13,15},{16,18},{17,... | collective-permute-start | bytes 258056 | tf_op jit(solution)/shard_map/ppermute | solution.py:21
  21.6 1.5 %collective-permute-done.2 = f32[14,3,512]{2,0,1:T(8,128)S(1)} collective-permute-done((f32[14,3,512]{2,0,1:T(8,128)S(1)}, f32[14,3,512]{2,0,1:T(8,128)S(1)}, u32[]{:S(2)}, u32[]{:S(2)}) %collective-permute-start.2) | collective-permute-done | bytes 86048 | tf_op jit(solution)/shard_map/ppermute | solution.py:21
  26.0 2.2 %collective-permute-done.5 = f32[14,38,3]{2,1,0:T(8,128)S(1)} collective-permute-done((f32[14,38,3]{2,1,0:T(8,128)S(1)}, f32[14,38,3]{2,1,0:T(8,128)S(1)}, u32[]{:S(2)}, u32[]{:S(2)}) %collective-permute-start.5) | collective-permute-done | bytes 6416 | tf_op jit(solution)/shard_map/ppermute | solution.py:23
  30.7 3.5 %collective-permute-start.6 = (f32[2,32,512]{2,1,0:T(8,128)S(1)}, f32[2,32,512]{2,1,0:T(8,128)S(1)}, u32[]{:S(2)}, u32[]{:S(2)}) collective-permute-start(f32[2,32,512]{2,1,0:T(8,128)S(1)} %get-tuple-element.26), channel_id=1, source_target_pairs={{0,4},{4,8},{8,12},{1,5},{5,9},{9,13},{2,6},{6,10},{10,14},{3,7},{... | collective-permute-start | bytes 393224 | tf_op jit(solution)/shard_map/ppermute | solution.py:21
  35.5 1.7 %collective-permute-done.6 = f32[2,32,512]{2,1,0:T(8,128)S(1)} collective-permute-done((f32[2,32,512]{2,1,0:T(8,128)S(1)}, f32[2,32,512]{2,1,0:T(8,128)S(1)}, u32[]{:S(2)}, u32[]{:S(2)}) %collective-permute-start.6) | collective-permute-done | bytes 131104 | tf_op jit(solution)/shard_map/ppermute | solution.py:21
  37.2 4.1 %collective-permute-done.7 = f32[2,32,512]{2,1,0:T(8,128)S(1)} collective-permute-done((f32[2,32,512]{2,1,0:T(8,128)S(1)}, f32[2,32,512]{2,1,0:T(8,128)S(1)}, u32[]{:S(2)}, u32[]{:S(2)}) %collective-permute-start.7) | collective-permute-done | bytes 131104 | tf_op jit(solution)/shard_map/ppermute | solution.py:23
  41.4 4.3 %collective-permute-start.8 = (f32[12,2,512]{2,1,0:T(2,128)S(1)}, f32[12,2,512]{2,1,0:T(2,128)S(1)}, u32[]{:S(2)}, u32[]{:S(2)}) collective-permute-start(f32[12,2,512]{2,1,0:T(2,128)S(1)} %get-tuple-element.24), channel_id=1, source_target_pairs={{0,2},{1,3},{4,6},{5,7},{8,10},{9,11},{12,14},{13,15},{16,18},{17,... | collective-permute-start | bytes 147464 | tf_op jit(solution)/shard_map/ppermute | solution.py:21
  47.4 4.3 %collective-permute-done.9 = f32[12,2,512]{2,1,0:T(2,128)S(1)} collective-permute-done((f32[12,2,512]{2,1,0:T(2,128)S(1)}, f32[12,2,512]{2,1,0:T(2,128)S(1)}, u32[]{:S(2)}, u32[]{:S(2)}) %collective-permute-start.9) | collective-permute-done | bytes 49184 | tf_op jit(solution)/shard_map/ppermute | solution.py:23
  54.6 1.9 %collective-permute-done.11 = f32[12,36,2]{2,1,0:T(8,128)S(1)} collective-permute-done((f32[12,36,2]{2,1,0:T(8,128)S(1)}, f32[12,36,2]{2,1,0:T(8,128)S(1)}, u32[]{:S(2)}, u32[]{:S(2)}) %collective-permute-start.11) | collective-permute-done | bytes 3488 | tf_op jit(solution)/shard_map/ppermute | solution.py:23
  58.0 2.2 %slice.392 = f32[4,16,256]{2,1,0:T(8,128)S(1)} slice(f32[4,16,516]{2,1,0:T(8,128)S(1)} %multiply_add_fusion.1), slice={[0:4:1], [0:16:1], [4:516:2]} | slice | bytes 131072 | tf_op jit(solution)/shard_map/slice | solution.py:44
  60.3 2.2 %slice.391 = f32[4,16,256]{2,1,0:T(8,128)S(1)} slice(f32[4,16,516]{2,1,0:T(8,128)S(1)} %multiply_add_fusion.1), slice={[0:4:1], [0:16:1], [3:515:2]} | slice | bytes 131072 | tf_op jit(solution)/shard_map/slice | solution.py:44
  62.5 2.2 %slice.390 = f32[4,16,256]{2,1,0:T(8,128)S(1)} slice(f32[4,16,516]{2,1,0:T(8,128)S(1)} %multiply_add_fusion.1), slice={[0:4:1], [0:16:1], [2:514:2]} | slice | bytes 131072 | tf_op jit(solution)/shard_map/slice | solution.py:44
  64.7 2.2 %slice.389 = f32[4,16,256]{2,1,0:T(8,128)S(1)} slice(f32[4,16,516]{2,1,0:T(8,128)S(1)} %multiply_add_fusion.1), slice={[0:4:1], [0:16:1], [1:513:2]} | slice | bytes 131072 | tf_op jit(solution)/shard_map/slice | solution.py:44
  66.9 2.2 %slice.388 = f32[4,16,256]{2,1,0:T(8,128)S(1)} slice(f32[4,16,516]{2,1,0:T(8,128)S(1)} %multiply_add_fusion.1), slice={[0:4:1], [0:16:1], [0:512:2]} | slice | bytes 131072 | tf_op jit(solution)/shard_map/slice | solution.py:42
  69.2 1.9 %all_gather.3 = f32[4,16,512]{2,1,0:T(8,128)S(1)} all-gather(f32[4,16,256]{2,1,0:T(8,128)S(1)} %multiply_add_fusion.3), channel_id=1, replica_groups=mesh['groups'=2,'sec'=4,'tile'=2,'xt'=2] {'xt'}, dimensions={2}, use_global_device_ids=true | all-gather | bytes 196608 | tf_op jit(solution)/shard_map/all_gather | solution.py:93
  71.1 3.5 %collective-permute-start.12 = (f32[3,16,512]{2,1,0:T(8,128)S(1)}, f32[3,16,512]{2,1,0:T(8,128)S(1)}, u32[]{:S(2)}, u32[]{:S(2)}) collective-permute-start(f32[3,16,512]{2,1,0:T(8,128)S(1)} %get-tuple-element.43), channel_id=1, source_target_pairs={{0,4},{4,8},{8,12},{1,5},{5,9},{9,13},{2,6},{6,10},{10,14},{3,7},{... | collective-permute-start | bytes 294920 | tf_op jit(solution)/shard_map/ppermute | solution.py:21
  76.9 4.1 %collective-permute-done.13 = f32[3,16,512]{2,1,0:T(8,128)S(1)} collective-permute-done((f32[3,16,512]{2,1,0:T(8,128)S(1)}, f32[3,16,512]{2,1,0:T(8,128)S(1)}, u32[]{:S(2)}, u32[]{:S(2)}) %collective-permute-start.13) | collective-permute-done | bytes 98336 | tf_op jit(solution)/shard_map/ppermute | solution.py:23
  81.1 1.6 %collective-permute-start.14 = (f32[10,3,512]{2,1,0:T(4,128)S(1)}, f32[10,3,512]{2,1,0:T(4,128)S(1)}, u32[]{:S(2)}, u32[]{:S(2)}) collective-permute-start(f32[10,3,512]{2,1,0:T(4,128)S(1)} %get-tuple-element.34), channel_id=1, source_target_pairs={{0,2},{1,3},{4,6},{5,7},{8,10},{9,11},{12,14},{13,15},{16,18},{17,... | collective-permute-start | bytes 184328 | tf_op jit(solution)/shard_map/ppermute | solution.py:21
  85.1 4.0 %collective-permute-done.15 = f32[10,3,512]{2,1,0:T(4,128)S(1)} collective-permute-done((f32[10,3,512]{2,1,0:T(4,128)S(1)}, f32[10,3,512]{2,1,0:T(4,128)S(1)}, u32[]{:S(2)}, u32[]{:S(2)}) %collective-permute-start.15) | collective-permute-done | bytes 61472 | tf_op jit(solution)/shard_map/ppermute | solution.py:23
  90.6 2.2 %collective-permute-start.16 = (f32[2,16,512]{2,1,0:T(8,128)S(1)}, f32[2,16,512]{2,1,0:T(8,128)S(1)}, u32[]{:S(2)}, u32[]{:S(2)}) collective-permute-start(f32[2,16,512]{2,1,0:T(8,128)S(1)} %get-tuple-element.40), channel_id=1, source_target_pairs={{0,4},{4,8},{8,12},{1,5},{5,9},{9,13},{2,6},{6,10},{10,14},{3,7},{... | collective-permute-start | bytes 196616 | tf_op jit(solution)/shard_map/ppermute | solution.py:21
  94.7 4.3 %collective-permute-done.17 = f32[2,16,512]{2,1,0:T(8,128)S(1)} collective-permute-done((f32[2,16,512]{2,1,0:T(8,128)S(1)}, f32[2,16,512]{2,1,0:T(8,128)S(1)}, u32[]{:S(2)}, u32[]{:S(2)}) %collective-permute-start.17) | collective-permute-done | bytes 65568 | tf_op jit(solution)/shard_map/ppermute | solution.py:23
  99.2 1.6 %collective-permute-start.18 = (f32[8,2,512]{2,0,1:T(8,128)S(1)}, f32[8,2,512]{2,0,1:T(8,128)S(1)}, u32[]{:S(2)}, u32[]{:S(2)}) collective-permute-start(f32[8,2,512]{2,0,1:T(8,128)S(1)} %get-tuple-element.36), channel_id=1, source_target_pairs={{0,2},{1,3},{4,6},{5,7},{8,10},{9,11},{12,14},{13,15},{16,18},{17,... | collective-permute-start | bytes 98312 | tf_op jit(solution)/shard_map/ppermute | solution.py:21
  102.1 2.6 %copy.112 = f32[8,32,256,2]{1,0,3,2:T(8,128)} copy(f32[8,32,256,2]{2,0,1,3:T(8,128)S(1)} %pad_maximum_fusion.2) | data formatting | bytes 1048576 | tf_op jit(solution)/shard_map/stack | solution.py:57
  104.6 1.9 %collective-permute-done.19 = f32[8,2,512]{2,0,1:T(8,128)S(1)} collective-permute-done((f32[8,2,512]{2,0,1:T(8,128)S(1)}, f32[8,2,512]{2,0,1:T(8,128)S(1)}, u32[]{:S(2)}, u32[]{:S(2)}) %collective-permute-start.19) | collective-permute-done | bytes 32800 | tf_op jit(solution)/shard_map/ppermute | solution.py:23
  112.5 2.2 %collective-permute-start.20 = (f32[1,8,256]{2,0,1:T(1,128)S(1)}, f32[1,8,256]{2,0,1:T(1,128)S(1)}, u32[]{:S(2)}, u32[]{:S(2)}) collective-permute-start(f32[1,8,256]{2,0,1:T(1,128)S(1)} %get-tuple-element.52), channel_id=1, source_target_pairs={{0,4},{4,8},{8,12},{1,5},{5,9},{9,13},{2,6},{6,10},{10,14},{3,7},{... | collective-permute-start | bytes 24584 | tf_op jit(solution)/shard_map/ppermute | solution.py:21
  115.9 3.1 %bitcast_subtract_fusion = f32[8,32,512]{1,0,2:T(8,128)} fusion(f32[8,32,512]{1,0,2:T(8,128)S(1)} %copy.113, f32[8,32,256,2]{1,0,3,2:T(8,128)} %copy.112), kind=kLoop, calls=%fused_computation | loop fusion | flops 131072 | bytes 1572864 | tf_op jit(solution)/shard_map/sub | solution.py:105
  119.1 3.0 %copy.123 = f32[8,32,512]{2,1,0:T(8,128)} copy(f32[8,32,512]{1,0,2:T(8,128)} %bitcast_subtract_fusion) | data formatting | bytes 1048576
  122.1 2.7 %collective-permute-start.22 = (f32[4,1,256]{2,0,1:T(4,128)S(1)}, f32[4,1,256]{2,0,1:T(4,128)S(1)}, u32[]{:S(2)}, u32[]{:S(2)}) collective-permute-start(f32[4,1,256]{2,0,1:T(4,128)S(1)} %get-tuple-element.50), channel_id=1, source_target_pairs={{0,2},{1,3},{4,6},{5,7},{8,10},{9,11},{12,14},{13,15},{16,18},{17,... | collective-permute-start | bytes 12296 | tf_op jit(solution)/shard_map/ppermute | solution.py:21
  126.7 3.5 %collective-permute-done.23 = f32[4,1,256]{2,0,1:T(4,128)S(1)} collective-permute-done((f32[4,1,256]{2,0,1:T(4,128)S(1)}, f32[4,1,256]{2,0,1:T(4,128)S(1)}, u32[]{:S(2)}, u32[]{:S(2)}) %collective-permute-start.23) | collective-permute-done | bytes 4128 | tf_op jit(solution)/shard_map/ppermute | solution.py:23
  (109 shorter events, 37.9 us)
Async XLA Ops:
  0.6 10.2 %copy-start = (f32[8,32,512]{2,1,0:T(8,128)S(1)}, f32[8,32,512]{2,1,0:T(8,128)}, u32[]{:S(2)}) copy-start(f32[8,32,512]{2,1,0:T(8,128)} %param.1) | copy-start | bytes 1572868
  1.8 9.1 %collective-permute-start = (f32[3,32,512]{2,1,0:T(8,128)S(1)}, f32[3,32,512]{2,1,0:T(8,128)S(1)}, u32[]{:S(2)}, u32[]{:S(2)}) collective-permute-start(f32[3,32,512]{2,1,0:T(8,128)S(1)} %get-tuple-element.29), channel_id=1, source_target_pairs={{0,4},{4,8},{8,12},{1,5},{5,9},{9,13},{2,6},{6,10},{10,14},{3,7},{... | collective-permute-start | bytes 589832 | tf_op jit(solution)/shard_map/ppermute | solution.py:21
  6.7 8.3 %collective-permute-start.1 = (f32[3,32,512]{2,1,0:T(8,128)S(1)}, f32[3,32,512]{2,1,0:T(8,128)S(1)}, u32[]{:S(2)}, u32[]{:S(2)}) collective-permute-start(f32[3,32,512]{2,1,0:T(8,128)S(1)} %get-tuple-element.28), channel_id=1, source_target_pairs={{4,0},{8,4},{12,8},{5,1},{9,5},{13,9},{6,2},{10,6},{14,10},{7,3},{... | collective-permute-start | bytes 589832 | tf_op jit(solution)/shard_map/ppermute | solution.py:23
  15.1 6.5 %collective-permute-start.3 = (f32[14,3,512]{2,0,1:T(8,128)S(1)}, f32[14,3,512]{2,0,1:T(8,128)S(1)}, u32[]{:S(2)}, u32[]{:S(2)}) collective-permute-start(f32[14,3,512]{2,0,1:T(8,128)S(1)} %copy.128), channel_id=1, source_target_pairs={{2,0},{3,1},{6,4},{7,5},{10,8},{11,9},{14,12},{15,13},{18,16},{19,... | collective-permute-start | bytes 258056 | tf_op jit(solution)/shard_map/ppermute | solution.py:23
  16.4 6.8 %collective-permute-start.2 = (f32[14,3,512]{2,0,1:T(8,128)S(1)}, f32[14,3,512]{2,0,1:T(8,128)S(1)}, u32[]{:S(2)}, u32[]{:S(2)}) collective-permute-start(f32[14,3,512]{2,0,1:T(8,128)S(1)} %copy.127), channel_id=1, source_target_pairs={{0,2},{1,3},{4,6},{5,7},{8,10},{9,11},{12,14},{13,15},{16,18},{17,... | collective-permute-start | bytes 258056 | tf_op jit(solution)/shard_map/ppermute | solution.py:21
  23.4 2.6 %collective-permute-start.4 = (f32[14,38,3]{2,1,0:T(8,128)S(1)}, f32[14,38,3]{2,1,0:T(8,128)S(1)}, u32[]{:S(2)}, u32[]{:S(2)}) collective-permute-start(f32[14,38,3]{2,1,0:T(8,128)S(1)} %get-tuple-element.18), channel_id=1, source_target_pairs={{0,1},{2,3},{4,5},{6,7},{8,9},{10,11},{12,13},{14,15},{16,17},{18,... | collective-permute-start | bytes 19160 | tf_op jit(solution)/shard_map/ppermute | solution.py:21
  24.7 3.5 %collective-permute-start.5 = (f32[14,38,3]{2,1,0:T(8,128)S(1)}, f32[14,38,3]{2,1,0:T(8,128)S(1)}, u32[]{:S(2)}, u32[]{:S(2)}) collective-permute-start(f32[14,38,3]{2,1,0:T(8,128)S(1)} %get-tuple-element.19), channel_id=1, source_target_pairs={{1,0},{3,2},{5,4},{7,6},{9,8},{11,10},{13,12},{15,14},{17,16},{19,... | collective-permute-start | bytes 19160 | tf_op jit(solution)/shard_map/ppermute | solution.py:23
  30.7 6.5 %collective-permute-start.6 = (f32[2,32,512]{2,1,0:T(8,128)S(1)}, f32[2,32,512]{2,1,0:T(8,128)S(1)}, u32[]{:S(2)}, u32[]{:S(2)}) collective-permute-start(f32[2,32,512]{2,1,0:T(8,128)S(1)} %get-tuple-element.26), channel_id=1, source_target_pairs={{0,4},{4,8},{8,12},{1,5},{5,9},{9,13},{2,6},{6,10},{10,14},{3,7},{... | collective-permute-start | bytes 393224 | tf_op jit(solution)/shard_map/ppermute | solution.py:21
  34.2 7.2 %collective-permute-start.7 = (f32[2,32,512]{2,1,0:T(8,128)S(1)}, f32[2,32,512]{2,1,0:T(8,128)S(1)}, u32[]{:S(2)}, u32[]{:S(2)}) collective-permute-start(f32[2,32,512]{2,1,0:T(8,128)S(1)} %get-tuple-element.27), channel_id=1, source_target_pairs={{4,0},{8,4},{12,8},{5,1},{9,5},{13,9},{6,2},{10,6},{14,10},{7,3},{... | collective-permute-start | bytes 393224 | tf_op jit(solution)/shard_map/ppermute | solution.py:23
  41.4 6.0 %collective-permute-start.8 = (f32[12,2,512]{2,1,0:T(2,128)S(1)}, f32[12,2,512]{2,1,0:T(2,128)S(1)}, u32[]{:S(2)}, u32[]{:S(2)}) collective-permute-start(f32[12,2,512]{2,1,0:T(2,128)S(1)} %get-tuple-element.24), channel_id=1, source_target_pairs={{0,2},{1,3},{4,6},{5,7},{8,10},{9,11},{12,14},{13,15},{16,18},{17,... | collective-permute-start | bytes 147464 | tf_op jit(solution)/shard_map/ppermute | solution.py:21
  45.7 6.0 %collective-permute-start.9 = (f32[12,2,512]{2,1,0:T(2,128)S(1)}, f32[12,2,512]{2,1,0:T(2,128)S(1)}, u32[]{:S(2)}, u32[]{:S(2)}) collective-permute-start(f32[12,2,512]{2,1,0:T(2,128)S(1)} %get-tuple-element.25), channel_id=1, source_target_pairs={{2,0},{3,1},{6,4},{7,5},{10,8},{11,9},{14,12},{15,13},{18,16},{19,... | collective-permute-start | bytes 147464 | tf_op jit(solution)/shard_map/ppermute | solution.py:23
  51.8 2.8 %collective-permute-start.10 = (f32[12,36,2]{2,1,0:T(8,128)S(1)}, f32[12,36,2]{2,1,0:T(8,128)S(1)}, u32[]{:S(2)}, u32[]{:S(2)}) collective-permute-start(f32[12,36,2]{2,1,0:T(8,128)S(1)} %get-tuple-element.22), channel_id=1, source_target_pairs={{0,1},{2,3},{4,5},{6,7},{8,9},{10,11},{12,13},{14,15},{16,17},{18,... | collective-permute-start | bytes 10376 | tf_op jit(solution)/shard_map/ppermute | solution.py:21
  53.1 3.4 %collective-permute-start.11 = (f32[12,36,2]{2,1,0:T(8,128)S(1)}, f32[12,36,2]{2,1,0:T(8,128)S(1)}, u32[]{:S(2)}, u32[]{:S(2)}) collective-permute-start(f32[12,36,2]{2,1,0:T(8,128)S(1)} %get-tuple-element.23), channel_id=1, source_target_pairs={{1,0},{3,2},{5,4},{7,6},{9,8},{11,10},{13,12},{15,14},{17,16},{19,... | collective-permute-start | bytes 10376 | tf_op jit(solution)/shard_map/ppermute | solution.py:23
  71.1 5.8 %collective-permute-start.12 = (f32[3,16,512]{2,1,0:T(8,128)S(1)}, f32[3,16,512]{2,1,0:T(8,128)S(1)}, u32[]{:S(2)}, u32[]{:S(2)}) collective-permute-start(f32[3,16,512]{2,1,0:T(8,128)S(1)} %get-tuple-element.43), channel_id=1, source_target_pairs={{0,4},{4,8},{8,12},{1,5},{5,9},{9,13},{2,6},{6,10},{10,14},{3,7},{... | collective-permute-start | bytes 294920 | tf_op jit(solution)/shard_map/ppermute | solution.py:21
  74.6 6.5 %collective-permute-start.13 = (f32[3,16,512]{2,1,0:T(8,128)S(1)}, f32[3,16,512]{2,1,0:T(8,128)S(1)}, u32[]{:S(2)}, u32[]{:S(2)}) collective-permute-start(f32[3,16,512]{2,1,0:T(8,128)S(1)} %get-tuple-element.42), channel_id=1, source_target_pairs={{4,0},{8,4},{12,8},{5,1},{9,5},{13,9},{6,2},{10,6},{14,10},{7,3},{... | collective-permute-start | bytes 294920 | tf_op jit(solution)/shard_map/ppermute | solution.py:23
  81.1 3.9 %collective-permute-start.14 = (f32[10,3,512]{2,1,0:T(4,128)S(1)}, f32[10,3,512]{2,1,0:T(4,128)S(1)}, u32[]{:S(2)}, u32[]{:S(2)}) collective-permute-start(f32[10,3,512]{2,1,0:T(4,128)S(1)} %get-tuple-element.34), channel_id=1, source_target_pairs={{0,2},{1,3},{4,6},{5,7},{8,10},{9,11},{12,14},{13,15},{16,18},{17,... | collective-permute-start | bytes 184328 | tf_op jit(solution)/shard_map/ppermute | solution.py:21
  82.7 6.3 %collective-permute-start.15 = (f32[10,3,512]{2,1,0:T(4,128)S(1)}, f32[10,3,512]{2,1,0:T(4,128)S(1)}, u32[]{:S(2)}, u32[]{:S(2)}) collective-permute-start(f32[10,3,512]{2,1,0:T(4,128)S(1)} %get-tuple-element.35), channel_id=1, source_target_pairs={{2,0},{3,1},{6,4},{7,5},{10,8},{11,9},{14,12},{15,13},{18,16},{19,... | collective-permute-start | bytes 184328 | tf_op jit(solution)/shard_map/ppermute | solution.py:23
  90.6 4.1 %collective-permute-start.16 = (f32[2,16,512]{2,1,0:T(8,128)S(1)}, f32[2,16,512]{2,1,0:T(8,128)S(1)}, u32[]{:S(2)}, u32[]{:S(2)}) collective-permute-start(f32[2,16,512]{2,1,0:T(8,128)S(1)} %get-tuple-element.40), channel_id=1, source_target_pairs={{0,4},{4,8},{8,12},{1,5},{5,9},{9,13},{2,6},{6,10},{10,14},{3,7},{... | collective-permute-start | bytes 196616 | tf_op jit(solution)/shard_map/ppermute | solution.py:21
  92.8 6.2 %collective-permute-start.17 = (f32[2,16,512]{2,1,0:T(8,128)S(1)}, f32[2,16,512]{2,1,0:T(8,128)S(1)}, u32[]{:S(2)}, u32[]{:S(2)}) collective-permute-start(f32[2,16,512]{2,1,0:T(8,128)S(1)} %get-tuple-element.41), channel_id=1, source_target_pairs={{4,0},{8,4},{12,8},{5,1},{9,5},{13,9},{6,2},{10,6},{14,10},{7,3},{... | collective-permute-start | bytes 196616 | tf_op jit(solution)/shard_map/ppermute | solution.py:23
  99.2 5.5 %collective-permute-start.18 = (f32[8,2,512]{2,0,1:T(8,128)S(1)}, f32[8,2,512]{2,0,1:T(8,128)S(1)}, u32[]{:S(2)}, u32[]{:S(2)}) collective-permute-start(f32[8,2,512]{2,0,1:T(8,128)S(1)} %get-tuple-element.36), channel_id=1, source_target_pairs={{0,2},{1,3},{4,6},{5,7},{8,10},{9,11},{12,14},{13,15},{16,18},{17,... | collective-permute-start | bytes 98312 | tf_op jit(solution)/shard_map/ppermute | solution.py:21
  100.7 5.8 %collective-permute-start.19 = (f32[8,2,512]{2,0,1:T(8,128)S(1)}, f32[8,2,512]{2,0,1:T(8,128)S(1)}, u32[]{:S(2)}, u32[]{:S(2)}) collective-permute-start(f32[8,2,512]{2,0,1:T(8,128)S(1)} %get-tuple-element.37), channel_id=1, source_target_pairs={{2,0},{3,1},{6,4},{7,5},{10,8},{11,9},{14,12},{15,13},{18,16},{19,... | collective-permute-start | bytes 98312 | tf_op jit(solution)/shard_map/ppermute | solution.py:23
  112.5 9.6 %collective-permute-start.20 = (f32[1,8,256]{2,0,1:T(1,128)S(1)}, f32[1,8,256]{2,0,1:T(1,128)S(1)}, u32[]{:S(2)}, u32[]{:S(2)}) collective-permute-start(f32[1,8,256]{2,0,1:T(1,128)S(1)} %get-tuple-element.52), channel_id=1, source_target_pairs={{0,4},{4,8},{8,12},{1,5},{5,9},{9,13},{2,6},{6,10},{10,14},{3,7},{... | collective-permute-start | bytes 24584 | tf_op jit(solution)/shard_map/ppermute | solution.py:21
  114.6 7.4 %collective-permute-start.21 = (f32[1,8,256]{2,0,1:T(1,128)S(1)}, f32[1,8,256]{2,0,1:T(1,128)S(1)}, u32[]{:S(2)}, u32[]{:S(2)}) collective-permute-start(f32[1,8,256]{2,0,1:T(1,128)S(1)} %get-tuple-element.53), channel_id=1, source_target_pairs={{4,0},{8,4},{12,8},{5,1},{9,5},{13,9},{6,2},{10,6},{14,10},{7,3},{... | collective-permute-start | bytes 24584 | tf_op jit(solution)/shard_map/ppermute | solution.py:23
  122.1 4.7 %collective-permute-start.22 = (f32[4,1,256]{2,0,1:T(4,128)S(1)}, f32[4,1,256]{2,0,1:T(4,128)S(1)}, u32[]{:S(2)}, u32[]{:S(2)}) collective-permute-start(f32[4,1,256]{2,0,1:T(4,128)S(1)} %get-tuple-element.50), channel_id=1, source_target_pairs={{0,2},{1,3},{4,6},{5,7},{8,10},{9,11},{12,14},{13,15},{16,18},{17,... | collective-permute-start | bytes 12296 | tf_op jit(solution)/shard_map/ppermute | solution.py:21
  124.7 5.5 %collective-permute-start.23 = (f32[4,1,256]{2,0,1:T(4,128)S(1)}, f32[4,1,256]{2,0,1:T(4,128)S(1)}, u32[]{:S(2)}, u32[]{:S(2)}) collective-permute-start(f32[4,1,256]{2,0,1:T(4,128)S(1)} %get-tuple-element.51), channel_id=1, source_target_pairs={{2,0},{3,1},{6,4},{7,5},{10,8},{11,9},{14,12},{15,13},{18,16},{19,... | collective-permute-start | bytes 12296 | tf_op jit(solution)/shard_map/ppermute | solution.py:23
where the time goes:
time: 133 us; the launch traced here: 132 us
  starting transfers between devices  49.5 us (37%)
  waiting for transfers between devices  42.7 us (32%)
  local copies, waits for them, and re-layouts  27.1 us (20%)
  other arithmetic  9.69 us (7%)
  blocking collectives  1.9 us (1%)
  between operations  1.43 us (1%)
    ppermute x12, waiting for transfers between devices, padded(): lax.ppermute(head, axis, [((i + 1) % count, i) for i in range(ends)])  34.9 us
    ppermute x12, starting transfers between devices, padded(): lax.ppermute(tail, axis, [(i, (i + 1) % count) for i in range(ends)])  33.5 us
    ppermute x12, starting transfers between devices, padded(): lax.ppermute(head, axis, [((i + 1) % count, i) for i in range(ends)])  15.9 us
    slice x16, local copies, waits for them, and re-layouts, reduce_valid(): lax.slice_in_dim(padded_in, offset, offset + length, 2, along)  13.7 us
    ppermute x12, waiting for transfers between devices, padded(): lax.ppermute(tail, axis, [(i, (i + 1) % count) for i in range(ends)])  7.83 us
    unnamed x12, local copies, waits for them, and re-layouts  4.63 us
    slice x4, local copies, waits for them, and re-layouts, reduce_valid(): summed = BINOMIAL_TAPS[0] * lax.slice_in_dim(padded_in, 0, length, 2, along)  3.42 us
    another operation x6, local copies, waits for them, and re-layouts, expand_valid(): paired = jnp.stack([even_part, odd_part], axis=along + 1)  3.41 us
  transfers between devices with their start and end apart: 24, of which 17 were waited for; matrix products, arithmetic and copies ran while one was open for 8% of the time, Pallas kernels for 0%

commit v1 on v0

v1 whole, which is shorter than its diff:
```python
import functools
import math

import jax
import jax.numpy as jnp
import ml_dtypes
import numpy as np
from jax import lax
from jax.experimental import pallas as pl
from jax.experimental.pallas import tpu as pltpu
from jax.sharding import PartitionSpec as P

LANES = 128
f32 = jnp.float32
bf16 = jnp.bfloat16


def round_up(value, to):
    return -(-value // to) * to


def banded(rows, cols, stride, taps):
    half = len(taps) // 2
    out = np.zeros((rows, cols))
    for i in range(rows):
        for k in range(-half, half + 1):
            if 0 <= stride * i + k < cols:
                out[i, stride * i + k] = taps[k + half]
    return out


def down(size):
    pole = math.sqrt(3.0) - 2.0
    prefilter = banded(size, size, 1, [math.sqrt(3.0) * pole ** abs(k) for k in range(-3, 4)])
    return banded(size // 2, size, 2, [0.0625, 0.25, 0.375, 0.25, 0.0625]) @ prefilter


def expand(cells):
    out = np.zeros((2 * cells, cells + 2))
    for m in range(cells):
        out[2 * m, m : m + 3] = [0.125, 0.75, 0.125]
        out[2 * m + 1, m + 1 : m + 3] = [0.5, 0.5]
    return out


def windows(operator, parts):
    rows, cols = operator.shape
    own, block = rows // parts, cols // parts
    padded = np.zeros((rows + 2, cols))
    padded[1:-1] = operator
    return np.stack(
        [
            np.stack([padded[t * own : t * own + own + 2, s * block : (s + 1) * block] for s in range(parts)])
            for t in range(parts)
        ]
    )


class Axis:
    def __init__(self, size, parts):
        first = down(size)
        self.parts, self.block = parts, size // parts
        self.fine = windows(first, parts)
        self.coarse = windows(down(size // 2) @ first, parts)
        self.shifts = [
            k
            for k in range(1, parts)
            if any(self.fine[(s + k) % parts, s].any() or self.coarse[(s + k) % parts, s].any() for s in range(parts))
        ]


def split(matrix):
    high = matrix.astype(np.float32).astype(ml_dtypes.bfloat16)
    low = (matrix - high.astype(np.float64)).astype(np.float32).astype(ml_dtypes.bfloat16)
    return np.stack([high, low])


def pad_to(matrix, rows, cols):
    return np.pad(matrix, ((0, rows - matrix.shape[0]), (0, cols - matrix.shape[1])))


def columns(axis):
    n, block = axis.parts, axis.block
    sides = [] if n == 1 else [0] if n == 2 else [-1, 1]
    tables = []
    for t in range(n):
        fine = np.concatenate(list(axis.fine[t]), 1)
        coarse = np.concatenate(list(axis.coarse[t]), 1)
        halo = np.stack([fine[0], fine[-1], coarse[0], coarse[-1]])
        halo = pad_to(halo, LANES, n * block)
        whole = np.concatenate([fine[1:-1], halo, coarse[1:-1]]).T
        at = [range(t * block, (t + 1) * block)]
        for side in sides:
            if side == 0:
                side = 1 - 2 * t
            start = (t + 1) * block if side > 0 else t * block - LANES
            at.append(range(start, start + LANES))
        picked = np.zeros((sum(len(a) for a in at), whole.shape[1]))
        row = 0
        for a in at:
            for i in a:
                if 0 <= i < n * block:
                    picked[row] = whole[i]
                row += 1
        outside = np.delete(whole, [i for a in at for i in a if 0 <= i < n * block], 0)
        assert not outside.any()
        tables.append(split(picked))
    return np.stack(tables)


def touched(blocks):
    filled = np.nonzero(np.any(blocks != 0, axis=tuple(i for i in range(blocks.ndim) if i != blocks.ndim - 2)))[0]
    return (int(filled[0]), int(filled[-1]) + 1) if len(filled) else (0, 0)


class RowPlan:
    def __init__(self, axis, depth):
        n = axis.parts
        self.parts = []
        for shift in axis.shifts:
            for level, table in enumerate((axis.fine, axis.coarse)):
                spans = [touched(table[(s + shift) % n, s]) for s in range(n)]
                count = max(b - a for a, b in spans)
                own = table.shape[2]
                starts = [min(a, own - count) for a, b in spans]
                self.parts.append((shift, level, starts, count))
        self.depth = depth

    def send(self, axis, s, shift, level):
        table = (axis.fine, axis.coarse)[level]
        _, _, starts, count = next(p for p in self.parts if p[0] == shift and p[1] == level)
        block = table[(s + shift) % axis.parts, s][starts[s] : starts[s] + count]
        return np.kron(np.eye(self.depth), block)

    def place(self, axis, t, shift, level):
        table = (axis.fine, axis.coarse)[level]
        s = (t - shift) % axis.parts
        _, _, starts, count = next(p for p in self.parts if p[0] == shift and p[1] == level)
        out = np.zeros((table.shape[2], count))
        if table[t, s].any():
            out[starts[s] : starts[s] + count] = np.eye(count)
        return out


def fine_slots(zaxis, yaxis):
    n, depth, height = zaxis.parts, zaxis.fine.shape[2], yaxis.fine.shape[2]
    front = np.zeros(depth, bool)
    back = np.zeros(depth, bool)
    for t in range(n):
        for s in range(n):
            filled = (zaxis.fine[t, s] != 0).any(1)
            if s < t:
                front |= filled
            if s > t:
                back |= filled
    low = [(0, y, 0) for y in range(height)]
    high = [(depth - 1, y, 0) for y in range(height)]
    for z in range(1, depth - 1):
        for y in (0, height - 1):
            if front[z]:
                low.append((z, y, 1 if back[z] else 0))
            if back[z] or not front[z]:
                high.append((z, y, -1 if front[z] else 0))
    own = [(z, y, 0) for z in range(1, depth - 1) for y in range(1, height - 1)]
    low += [None] * (-len(low) % 8)
    slots = low + own + high
    return slots + [None] * (-len(slots) % 16), len(low), len(own)


def coarse_slots(zaxis, yaxis):
    depth, height = zaxis.coarse.shape[2], yaxis.coarse.shape[2]
    own = [(z, y, 0) for z in range(1, depth - 1) for y in range(1, height - 1)]
    rest = [(z, y, 0) for z in range(depth) for y in range(height) if (z, y, 0) not in own]
    cut = round_up(len(rest) // 2, 8)
    slots = rest[:cut] + own + rest[cut:]
    return slots + [None] * (-len(slots) % 8), cut, len(own)


def slot_matrix(slots, zblock, yblock, side):
    out = np.zeros((len(slots), zblock.shape[1] * yblock.shape[1]))
    for row, slot in enumerate(slots):
        if slot and (slot[2] == 0 or (slot[2] > 0) == (side >= 0)):
            out[row] = np.kron(zblock[slot[0]], yblock[slot[1]])
    return out


def slot_expand(slots, depth, height):
    zs, ys = expand(depth), expand(height)
    out = np.zeros((4 * depth * height, len(slots)))
    for row, slot in enumerate(slots):
        if slot:
            out[:, row] = np.kron(zs[:, slot[0]], ys[:, slot[1]])
    return out


def mm(a, b):
    return jnp.dot(a, b, preferred_element_type=f32)


def halves(x):
    high = x.astype(bf16)
    return high, (x - high.astype(f32)).astype(bf16)


def mm3(a, b):
    return mm(a[0], b[0]) + (mm(a[0], b[1]) + mm(a[1], b[0]))


def mm2(a, b):
    return mm(a, b[0]) + mm(a, b[1])


def pack(tiles):
    total = tiles[0]
    for j in range(1, len(tiles)):
        total = total + pltpu.roll(tiles[j], 4 * j, 1)
    return total


def unpack(packed, j, only=False):
    tile = packed if j == 0 else pltpu.roll(packed, LANES - 4 * j, 1)
    if only:
        tile = jnp.where(lax.broadcasted_iota(jnp.int32, tile.shape, 1) < 4, tile, 0.0)
    return tile


def row_tiles(x):
    return [x[i : i + 8] for i in range(0, x.shape[0], 8)]


class Packing:
    def __init__(self, fine_rows, coarse_rows, tiles):
        self.fine, self.coarse, self.tiles = fine_rows, coarse_rows, tiles
        assert (fine_rows + coarse_rows) // 8 * 4 <= LANES
        self.rows = fine_rows * tiles + coarse_rows + 8

    def store(self, ref, fine, coarse):
        at = 0
        halo = []
        if self.fine:
            for j in range(self.tiles):
                ref[at : at + self.fine] = fine[:, j * LANES : (j + 1) * LANES]
                at += self.fine
            halo += row_tiles(fine[:, self.tiles * LANES :])
        ref[at : at + self.coarse] = coarse[:, LANES:]
        at += self.coarse
        halo += row_tiles(coarse[:, :LANES])
        ref[at : at + 8] = pack(halo)

    def load(self, ref, only=False):
        at = 0
        halo = ref[self.rows - 8 : self.rows]
        fine = None
        if self.fine:
            parts = []
            for j in range(self.tiles):
                parts.append(ref[at : at + self.fine])
                at += self.fine
            parts.append(jnp.concatenate([unpack(halo, j, only) for j in range(self.fine // 8)], 0))
            fine = jnp.concatenate(parts, 1)
        count = self.fine // 8
        side = jnp.concatenate([unpack(halo, count + j, only) for j in range(self.coarse // 8)], 0)
        return fine, jnp.concatenate([side, ref[at : at + self.coarse]], 1)


def over_columns(tiles, plans, n_slabs, volume, *refs):
    slabs, (wx, wy), (high, low, *sent) = refs[:n_slabs], refs[n_slabs : n_slabs + 2], refs[n_slabs + 2 :]
    depth, height, width = volume.shape
    cells = halves(volume[...].reshape(depth * height, width))
    total = mm3(cells, (wx[0, :width], wx[1, :width]))
    at = width
    for slab in slabs:
        edge = halves(slab[...].reshape(depth * height, LANES))
        total = total + mm3(edge, (wx[0, at : at + LANES], wx[1, at : at + LANES]))
        at += LANES
    x = halves(total)
    high[...], low[...] = x
    level_end = (tiles + 1) * LANES
    at = 0
    for packing, out in zip(plans, sent):
        rows, more = round_up(packing.fine, 16), round_up(packing.coarse, 16)
        fine = mm3((wy[0, at : at + rows], wy[1, at : at + rows]), tuple(p[:, :level_end] for p in x))
        at += rows
        coarse = mm3((wy[0, at : at + more], wy[1, at : at + more]), tuple(p[:, level_end - LANES :] for p in x))
        at += more
        packing.store(out, fine[: packing.fine], coarse[: packing.coarse])


def over_rows(tiles, plans_in, plans_out, fine_own, coarse_own, high, low, *refs):
    n_in = len(plans_in)
    got, (gf, gc), (fine_out, coarse_out, *sent) = refs[:n_in], refs[n_in : n_in + 2], refs[n_in + 2 :]
    level_end = (tiles + 1) * LANES
    cells = high.shape[0]
    fine = mm3((gf[0, :, :cells], gf[1, :, :cells]), (high[:, :level_end], low[:, :level_end]))
    coarse = mm3((gc[0, :, :cells], gc[1, :, :cells]), (high[:, level_end - LANES :], low[:, level_end - LANES :]))
    at = cells
    for packing, ref in zip(plans_in, got):
        more, less = packing.load(ref, True)
        fine = fine + mm3(tuple(gf[i, :, at : at + packing.fine] for i in range(2)), halves(more))
        coarse = coarse + mm3(tuple(gc[i, :, at : at + packing.coarse] for i in range(2)), halves(less))
        at += LANES
    fine_out[...] = fine[:fine_own]
    coarse_out[...] = coarse[:coarse_own]
    at, also = fine_own, round_up(coarse_own, 16)
    for packing, out in zip(plans_out, sent):
        packing.store(out, fine[at : at + packing.fine], coarse[also : also + packing.coarse])
        at += round_up(packing.fine, 16)
        also += round_up(packing.coarse, 16)


def over_sections(tiles, plans, starts, fine_at, coarse_at, volume, fine_ref, coarse_ref, *refs):
    n_in = len(plans)
    got, (ex, ezy, fx, fzy), (zero_out, one_out, coarse_out, level) = refs[:n_in], refs[n_in : n_in + 4], refs[n_in + 4 :]
    depth, height, width = volume.shape
    level[...] = fine_ref[...]
    coarse = coarse_ref[...]
    for packing, start, ref in zip(plans, starts, got):
        more, less = packing.load(ref)
        if more is not None:
            level[start : start + packing.fine] += more
        coarse = coarse + less
    wide = halves(mm2_right(halves(level[...]), ex[...]))
    zero_out[...] = volume[...] - mm2(ezy[...], wide).reshape(volume.shape)
    narrow = halves(mm2_right(halves(coarse), fx[...]))
    first, count = fine_at
    own = level[first : first + count, : tiles * LANES]
    one_out[...] = (own - mm2(fzy[...], narrow)).reshape(one_out.shape)
    first, count = coarse_at
    coarse_out[...] = coarse[first : first + count, LANES:].reshape(coarse_out.shape)


def mm2_right(a, b):
    return mm(a[0], b) + mm(a[1], b)


def cost(flops, moved):
    return pl.CostEstimate(flops=flops, bytes_accessed=moved, transcendentals=0)


def shifted(x, axis, shift):
    n = lax.axis_size(axis)
    return lax.ppermute(x, axis, [(i, (i + shift) % n) for i in range(n)])


def call(body, outs, args, scratch=()):
    vmem = pl.BlockSpec(memory_space=pltpu.VMEM)
    moved = sum(math.prod(a.shape) * a.dtype.itemsize for a in (*args, *outs))
    return pl.pallas_call(
        body,
        out_shape=outs,
        in_specs=[vmem] * len(args),
        out_specs=[vmem] * len(outs),
        scratch_shapes=list(scratch),
        cost_estimate=cost(2 * 10**8, moved),
        compiler_params=pltpu.CompilerParams(vmem_limit_bytes=48 * 2**20),
    )(*args)


def unique(tables):
    kept, places, seen = [], [], {}
    for table in tables:
        key = tuple(t.tobytes() for t in table)
        if key not in seen:
            seen[key] = len(kept)
            kept.append(table)
        places.append(seen[key])
    return [np.stack(column) for column in zip(*kept)], np.array(places, np.int32)


def shards(sections, volume):
    sizes = (sections, volume.shape[1] * lax.axis_size("tile"), volume.shape[2] * lax.axis_size("xt"))
    zaxis, yaxis, xaxis = (Axis(s, lax.axis_size(a)) for s, a in zip(sizes, ("sec", "tile", "xt")))
    depth, height, width = volume.shape
    cells = depth * height
    tiles = width // 2 // LANES
    coarse_tiles = width // 4 // LANES
    assert coarse_tiles == 1 and width % (4 * LANES) == 0
    z, y, x = (lax.axis_index(a) for a in ("sec", "tile", "xt"))

    if xaxis.parts == 1:
        slabs = []
    elif xaxis.parts == 2:
        edge = jnp.where(x == 0, volume[:, :, width - LANES :], volume[:, :, :LANES])
        slabs = [shifted(edge, "xt", 1)]
    else:
        slabs = [shifted(volume[:, :, width - LANES :], "xt", 1), shifted(volume[:, :, :LANES], "xt", -1)]
    wx = lax.dynamic_index_in_dim(jnp.asarray(columns(xaxis)), x, 0, False)

    rowplan = RowPlan(yaxis, depth)
    row_packs = []
    for shift in yaxis.shifts:
        fine_count, coarse_count = (p[3] for p in rowplan.parts if p[0] == shift)
        row_packs.append(Packing(depth * fine_count, depth * coarse_count, tiles))
    wys = []
    for s in range(yaxis.parts):
        blocks = []
        for shift in yaxis.shifts:
            for level in range(2):
                m = rowplan.send(yaxis, s, shift, level)
                blocks.append(pad_to(m, round_up(m.shape[0], 16), cells))
        wys.append((split(np.concatenate(blocks)),))
    (wy,), place = unique(wys)
    wy = lax.dynamic_index_in_dim(jnp.asarray(wy), jnp.asarray(place)[y], 0, False)

    fslots, ffirst, fcount = fine_slots(zaxis, yaxis)
    cslots, cfirst, ccount = coarse_slots(zaxis, yaxis)

    def matrices(s, t, ty):
        out = []
        for level, slots in enumerate((fslots, cslots)):
            zb = (zaxis.fine, zaxis.coarse)[level][t, s]
            blocks = [slot_matrix(slots, zb, (yaxis.fine, yaxis.coarse)[level][ty, ty], t - s)]
            for shift in yaxis.shifts:
                m = slot_matrix(slots, zb, rowplan.place(yaxis, ty, shift, level), t - s)
                blocks.append(pad_to(m, len(slots), LANES))
            out.append(np.concatenate(blocks, 1))
        return out

    starts, z_packs = [], []
    for shift in zaxis.shifts:
        filled = np.zeros(len(fslots), bool)
        for s in range(zaxis.parts):
            filled |= (matrices(s, (s + shift) % zaxis.parts, 0)[0] != 0).any(1)
            filled |= (matrices(s, (s + shift) % zaxis.parts, yaxis.parts - 1)[0] != 0).any(1)
        at = np.nonzero(filled)[0]
        start, end = (int(at[0]) // 8 * 8, round_up(int(at[-1]) + 1, 8)) if len(at) else (0, 0)
        starts.append(start)
        z_packs.append(Packing(end - start, len(cslots), tiles))

    gs = []
    for s in range(zaxis.parts):
        for ty in range(yaxis.parts):
            fine, coarse = matrices(s, s, ty)
            fines, coarses = [fine], [pad_to(coarse, round_up(len(cslots), 16), coarse.shape[1])]
            for shift, start, packing in zip(zaxis.shifts, starts, z_packs):
                fine, coarse = matrices(s, (s + shift) % zaxis.parts, ty)
                fine = fine[start : start + packing.fine]
                fines.append(pad_to(fine, round_up(packing.fine, 16), fine.shape[1]))
                coarses.append(pad_to(coarse, round_up(packing.coarse, 16), coarse.shape[1]))
            gs.append((split(np.concatenate(fines)), split(np.concatenate(coarses))))
    (gf, gc), place = unique(gs)
    at = jnp.asarray(place)[z * yaxis.parts + y]
    gf = lax.dynamic_index_in_dim(jnp.asarray(gf), at, 0, False)
    gc = lax.dynamic_index_in_dim(jnp.asarray(gc), at, 0, False)

    own = width // 2
    table = expand(own)
    ex = np.zeros((own + LANES, width))
    ex[:own], ex[own], ex[own + 1] = table[:, 1:-1].T, table[:, 0], table[:, -1]
    own = width // 4
    table = expand(own)
    fx = np.zeros((LANES + own, width // 2))
    fx[2], fx[3], fx[LANES:] = table[:, 0], table[:, -1], table[:, 1:-1].T
    ezy = slot_expand(fslots, depth // 2, height // 2)
    fzy = slot_expand(cslots, depth // 4, height // 4)
    constants = [jnp.asarray(m.astype(ml_dtypes.bfloat16)) for m in (ex, ezy, fx, fzy)]

    n = (tiles + 1 + 1) * LANES
    shape = jax.ShapeDtypeStruct
    high, low, *sent = call(
        functools.partial(over_columns, tiles, row_packs, len(slabs)),
        [shape((cells, n), bf16)] * 2 + [shape((p.rows, LANES), f32) for p in row_packs],
        [volume, *slabs, wx, wy],
    )
    got = [shifted(a, "tile", k) for a, k in zip(sent, yaxis.shifts)]
    fine, coarse, *sent = call(
        functools.partial(over_rows, tiles, row_packs, z_packs, len(fslots), len(cslots)),
        [shape((len(fslots), (tiles + 1) * LANES), f32), shape((len(cslots), 2 * LANES), f32)]
        + [shape((p.rows, LANES), f32) for p in z_packs],
        [high, low, *got, gf, gc],
    )
    got = [shifted(a, "sec", k) for a, k in zip(sent, zaxis.shifts)]
    return tuple(
        call(
            functools.partial(over_sections, tiles, z_packs, starts, (ffirst, fcount), (cfirst, ccount)),
            [
                shape(volume.shape, f32),
                shape((depth // 2, height // 2, width // 2), f32),
                shape((depth // 4, height // 4, width // 4), f32),
            ],
            [volume, fine, coarse, *got, *constants],
            [pltpu.VMEM((len(fslots), (tiles + 1) * LANES), f32)],
        )
    )


def solution(mesh):
    spec = P(("groups", "sec"), "tile", "xt")
    groups = mesh.shape["groups"]

    def whole(volume):
        body = functools.partial(shards, volume.shape[0] // groups)
        run = jax.shard_map(body, mesh=mesh, in_specs=(spec,), out_specs=(spec,) * 3, check_vma=False)
        return run(volume)

    return whole
```

time: 133 us -> 22.8 us (0.17)
  starting transfers between devices: 49.5 us -> 7.98 us
  waiting for transfers between devices: 42.7 us -> 6.02 us
  local copies, waits for them, and re-layouts: 27.1 us -> 3.54 us
  other arithmetic: 9.69 us -> 1.06 us
  Pallas kernels: 0 us -> 3.23 us
  blocking collectives: 1.9 us -> 0 us
    ppermute x24 -> x5, starting transfers between devices: 49.5 us -> 7.98 us  [shifted(): return lax.ppermute(x, axis, [(i, (i + shift) % n) for i in range(n)])]
    ppermute x24 -> x5, waiting for transfers between devices: 42.7 us -> 6.02 us  [shifted(): return lax.ppermute(x, axis, [(i, (i + shift) % n) for i in range(n)])]
    slice x29 -> x0, local copies, waits for them, and re-layouts: 18.4 us -> none  [the longest x16 13.7 us: reduce_valid(): lax.slice_in_dim(padded_in, offset, offset + length, 2, along)]
    unnamed x12, local copies, waits for them, and re-layouts: 4.63 us -> 0.04 us
    sub x2 -> x0, other arithmetic: 3.78 us -> none  [the longest x1 3.13 us: shards(): detail_zero = volume - expand_all(level_rim)]
    squeeze x0 -> x4, local copies, waits for them, and re-layouts: none -> 3.5 us  [the longest x1 1.4 us: shards(): wx = lax.dynamic_index_in_dim(jnp.asarray(columns(xaxis)), x, 0, False)]
    another operation x6 -> x0, local copies, waits for them, and re-layouts: 3.41 us -> none  [expand_valid(): paired = jnp.stack([even_part, odd_part], axis=along + 1)]
    pallas_call x0 -> x3, Pallas kernels: none -> 3.23 us  [call(): pl.pallas_call(body, out_shape=outs, in_specs=[vmem] * len(args), out_spe...]
  transfers between devices with their start and end apart: 24 -> 5, of which waited for: 17 -> 2; matrix products, arithmetic and copies ran while one was open for 8% -> 15% of each run, Pallas kernels for 0% -> 0%
where the time goes in v1:
time: 22.8 us; the launch traced here: 22.6 us
  starting transfers between devices  7.98 us (35%)
  waiting for transfers between devices  6.02 us (26%)
  local copies, waits for them, and re-layouts  3.54 us (16%)
  Pallas kernels  3.23 us (14%)
  other arithmetic  1.06 us (5%)
  between operations  0.78 us (3%)
    ppermute x5, starting transfers between devices, shifted(): return lax.ppermute(x, axis, [(i, (i + shift) % n) for i in range(n)])  7.98 us
    ppermute x5, waiting for transfers between devices, shifted(): return lax.ppermute(x, axis, [(i, (i + shift) % n) for i in range(n)])  6.02 us
    pallas_call x3, Pallas kernels, call(): pl.pallas_call(body, out_shape=outs, in_specs=[vmem] * len(args), out_spe...  3.23 us
    squeeze x1, local copies, waits for them, and re-layouts, shards(): wx = lax.dynamic_index_in_dim(jnp.asarray(columns(xaxis)), x, 0, False)  1.4 us
    squeeze x1, local copies, waits for them, and re-layouts, shards(): gf = lax.dynamic_index_in_dim(jnp.asarray(gf), at, 0, False)  1.09 us
    select_n x1, other arithmetic, shards(): edge = jnp.where(x == 0, volume[:, :, width - LANES:], volume[:, :, :LANES])  1.06 us
    squeeze x1, local copies, waits for them, and re-layouts, shards(): gc = lax.dynamic_index_in_dim(jnp.asarray(gc), at, 0, False)  0.99 us
  transfers between devices with their start and end apart: 5, of which 2 were waited for; matrix products, arithmetic and copies ran while one was open for 15% of the time, Pallas kernels for 0%

profile of v1, /device:TPU:0, one launch (start us, length us, event | category | flops | bytes accessed | tf_op | source)
XLA Modules:
  0.0 22.6 jit_solution(17109211834551896139)
XLA Ops:
  0.6 0.0 copy-start.5
  0.6 0.0 copy-start
  0.7 1.1 %slice_select_fusion = f32[8,32,128]{2,1,0:T(8,128)S(1)} fusion(f32[8,32,512]{2,1,0:T(8,128)} %volume.3, pred[]{:T(512)S(6)} %eq.3), kind=kLoop, calls=%fused_computation.3 | loop fusion | flops 32768 | bytes 393217 | tf_op jit(solution)/shard_map/jit(_where)/select_n | solution.py:383
  1.7 0.5 %collective-permute-start = (f32[8,32,128]{2,1,0:T(8,128)S(1)}, f32[8,32,128]{2,1,0:T(8,128)S(1)}, u32[]{:S(2)}, u32[]{:S(2)}) collective-permute-start(f32[8,32,128]{2,1,0:T(8,128)S(1)} %slice_select_fusion), channel_id=1, source_target_pairs={{0,1},{1,0},{2,3},{3,2},{4,5},{5,4},{6,7},{7,6},{8,9},{9,8},{10,11... | collective-permute-start | bytes 393224 | tf_op jit(solution)/shard_map/ppermute | solution.py:342
  2.2 1.4 %dynamic-slice_bitcast_fusion.refs_1_ = bf16[2,640,512]{2,1,0:T(8,128)(2,1)S(1)} fusion(bf16[2,2,640,512]{3,2,1,0:T(8,128)(2,1)} %constant.53.clone, s32[]{:T(128)S(6)} %select_n.30), kind=kLoop, calls=%fused_computation | loop fusion | bytes 2621444 | tf_op jit(solution)/shard_map/jit(dynamic_index_in_dim)/squeeze | solution.py:387
  3.6 0.0 copy-done.5
  3.6 0.0 copy-start.1
  3.7 0.0 copy-start.2
  3.7 0.0 copy-start.3
  3.7 0.0 copy-start.4
  3.7 1.1 %dynamic-slice_bitcast_fusion.1.refs_1_ = bf16[2,256,384]{2,1,0:T(8,128)(2,1)S(1)} fusion(bf16[8,2,256,384]{3,2,1,0:T(8,128)(2,1)} %constant.55.clone, s32[]{:T(128)S(6)} %select_n.34), kind=kLoop, calls=%fused_computation.1 | loop fusion | bytes 786436 | tf_op jit(solution)/shard_map/jit(dynamic_index_in_dim)/squeeze | solution.py:443
  4.8 0.0 collective-permute-done.refs_0_
  4.8 0.0 copy-done
  4.9 1.1 %shard_map.130 = (bf16[256,512]{1,0:T(8,128)(2,1)S(1)}, bf16[256,512]{1,0:T(8,128)(2,1)S(1)}, f32[112,128]{1,0:T(8,128)S(1)}) custom-call(f32[8,32,512]{2,1,0:T(8,128)S(1)} %copy-done, f32[8,32,128]{2,1,0:T(8,128)S(1)} %collective-permute-done.refs_0_, bf16[2,640,512]{2,1,0:T(8,128)(2,1)S(1)} %dynamic-slice_bitcast_fusion.refs_1_, ...), custom_call_target="tpu_custom_call" | custom-call | flops 200000000 | bytes 2629632 | tf_op jit(solution)/shard_map/pallas_call | solution.py:348
  5.9 2.5 %collective-permute-start.1 = (f32[112,128]{1,0:T(8,128)S(1)}, f32[112,128]{1,0:T(8,128)S(1)}, u32[]{:S(2)}, u32[]{:S(2)}) collective-permute-start(f32[112,128]{1,0:T(8,128)S(1)} %get-tuple-element.13), channel_id=1, source_target_pairs={{0,2},{2,0},{1,3},{3,1},{4,6},{6,4},{5,7},{7,5},{8,10},{10,8},{9,1... | collective-permute-start | bytes 172040 | tf_op jit(solution)/shard_map/ppermute | solution.py:342
  8.5 1.0 %dynamic-slice_bitcast_fusion.2.refs_2_ = bf16[2,192,384]{2,1,0:T(8,128)(2,1)S(1)} fusion(bf16[8,2,192,384]{3,2,1,0:T(8,128)(2,1)} %constant.56.clone, s32[]{:T(128)S(6)} %select_n.34), kind=kLoop, calls=%fused_computation.2 | loop fusion | bytes 589828 | tf_op jit(solution)/shard_map/jit(dynamic_index_in_dim)/squeeze | solution.py:444
  9.5 1.6 %collective-permute-done.1.refs_0_ = f32[112,128]{1,0:T(8,128)S(1)} collective-permute-done((f32[112,128]{1,0:T(8,128)S(1)}, f32[112,128]{1,0:T(8,128)S(1)}, u32[]{:S(2)}, u32[]{:S(2)}) %collective-permute-start.1) | collective-permute-done | bytes 57376 | tf_op jit(solution)/shard_map/ppermute | solution.py:342
  11.0 0.7 %shard_map.131 = (f32[112,384]{1,0:T(8,128)S(1)}, f32[40,256]{1,0:T(8,128)S(1)}, f32[192,128]{1,0:T(8,128)S(1)}, f32[48,128]{1,0:T(8,128)S(1)}, f32[160,128]{1,0:T(8,128)S(1)}) custom-call(bf16[256,512]{1,0:T(8,128)(2,1)S(1)} %get-tuple-element.11.high, bf16[256,512]{1,0:T(8,128)(2,1)S(1)} %get-tuple-element.12.low, ...), custom_call_target="tpu_custom_call" | custom-call | flops 200000000 | bytes 1687552 | tf_op jit(solution)/shard_map/pallas_call | solution.py:348
  11.8 1.9 %collective-permute-start.2 = (f32[192,128]{1,0:T(8,128)S(1)}, f32[192,128]{1,0:T(8,128)S(1)}, u32[]{:S(2)}, u32[]{:S(2)}) collective-permute-start(f32[192,128]{1,0:T(8,128)S(1)} %get-tuple-element.16), channel_id=1, source_target_pairs={{0,4},{4,8},{8,12},{12,0},{1,5},{5,9},{9,13},{13,1},{2,6},{6,10},{... | collective-permute-start | bytes 294920 | tf_op jit(solution)/shard_map/ppermute | solution.py:342
  13.7 2.1 %collective-permute-start.4 = (f32[160,128]{1,0:T(8,128)S(1)}, f32[160,128]{1,0:T(8,128)S(1)}, u32[]{:S(2)}, u32[]{:S(2)}) collective-permute-start(f32[160,128]{1,0:T(8,128)S(1)} %get-tuple-element.18), channel_id=1, source_target_pairs={{0,12},{4,0},{8,4},{12,8},{1,13},{5,1},{9,5},{13,9},{2,14},{6,2},{... | collective-permute-start | bytes 245768 | tf_op jit(solution)/shard_map/ppermute | solution.py:342
  15.8 0.9 %collective-permute-start.3 = (f32[48,128]{1,0:T(8,128)S(1)}, f32[48,128]{1,0:T(8,128)S(1)}, u32[]{:S(2)}, u32[]{:S(2)}) collective-permute-start(f32[48,128]{1,0:T(8,128)S(1)} %get-tuple-element.17), channel_id=1, source_target_pairs={{0,8},{4,12},{8,0},{12,4},{1,9},{5,13},{9,1},{13,5},{2,10},{6,14},... | collective-permute-start | bytes 73736 | tf_op jit(solution)/shard_map/ppermute | solution.py:342
  16.7 4.4 %collective-permute-done.3.refs_1_ = f32[48,128]{1,0:T(8,128)S(1)} collective-permute-done((f32[48,128]{1,0:T(8,128)S(1)}, f32[48,128]{1,0:T(8,128)S(1)}, u32[]{:S(2)}, u32[]{:S(2)}) %collective-permute-start.3) | collective-permute-done | bytes 24608 | tf_op jit(solution)/shard_map/ppermute | solution.py:342
  21.2 0.0 collective-permute-done.4.refs_2_
  21.2 0.0 collective-permute-done.2.refs_0_
  21.2 0.0 copy-done.1
  21.2 0.0 copy-done.2
  21.2 0.0 copy-done.3
  21.2 0.0 copy-done.4
  21.2 1.4 %shard_map.132 = (f32[8,32,512]{2,1,0:T(8,128)}, f32[4,16,256]{2,1,0:T(8,128)}, f32[2,8,128]{2,1,0:T(8,128)}) custom-call(f32[8,32,512]{2,1,0:T(8,128)S(1)} %copy-done, f32[112,384]{1,0:T(8,128)S(1)} %get-tuple-element.14.fine_ref, f32[40,256]{1,0:T(8,128)S(1)} %get-tuple-element.15.coarse_ref, f32[192,128]{1,0:T(8,128)S(1)} %collective-permute-done.2.refs_0_, ...), custom_call_target="tpu_custom_call" | custom-call | flops 200000000 | bytes 2126848 | tf_op jit(solution)/shard_map/pallas_call | solution.py:348
  (1 shorter events, 0.0 us)
Async XLA Ops:
  0.6 3.0 %copy-start.5 = (bf16[2,2,80,256]{3,2,1,0:T(8,128)(2,1)S(1)}, bf16[2,2,80,256]{3,2,1,0:T(8,128)(2,1)}, u32[]{:S(2)}) copy-start(bf16[2,2,80,256]{3,2,1,0:T(8,128)(2,1)} %constant.54.clone) | copy-start | bytes 491524
  0.6 4.2 %copy-start = (f32[8,32,512]{2,1,0:T(8,128)S(1)}, f32[8,32,512]{2,1,0:T(8,128)}, u32[]{:S(2)}) copy-start(f32[8,32,512]{2,1,0:T(8,128)} %volume.3) | copy-start | bytes 1572868
  1.7 3.1 %collective-permute-start = (f32[8,32,128]{2,1,0:T(8,128)S(1)}, f32[8,32,128]{2,1,0:T(8,128)S(1)}, u32[]{:S(2)}, u32[]{:S(2)}) collective-permute-start(f32[8,32,128]{2,1,0:T(8,128)S(1)} %slice_select_fusion), channel_id=1, source_target_pairs={{0,1},{1,0},{2,3},{3,2},{4,5},{5,4},{6,7},{7,6},{8,9},{9,8},{10,11... | collective-permute-start | bytes 393224 | tf_op jit(solution)/shard_map/ppermute | solution.py:342
  3.6 17.5 %copy-start.1 = (bf16[384,512]{1,0:T(8,128)(2,1)S(1)}, bf16[384,512]{1,0:T(8,128)(2,1)}, u32[]{:S(2)}) copy-start(bf16[384,512]{1,0:T(8,128)(2,1)} %constant.57.clone.refs_3_) | copy-start | bytes 1179652
  3.7 17.5 %copy-start.2 = (bf16[256,256]{1,0:T(8,128)(2,1)S(1)}, bf16[256,256]{1,0:T(8,128)(2,1)}, u32[]{:S(2)}) copy-start(bf16[256,256]{1,0:T(8,128)(2,1)} %constant.59.clone.refs_5_) | copy-start | bytes 393220
  3.7 17.5 %copy-start.3 = (bf16[256,112]{1,0:T(8,128)(2,1)S(1)}, bf16[256,112]{1,0:T(8,128)(2,1)}, u32[]{:S(2)}) copy-start(bf16[256,112]{1,0:T(8,128)(2,1)} %constant.58.clone.refs_4_) | copy-start | bytes 172036
  3.7 17.5 %copy-start.4 = (bf16[64,40]{1,0:T(8,128)(2,1)S(1)}, bf16[64,40]{1,0:T(8,128)(2,1)}, u32[]{:S(2)}) copy-start(bf16[64,40]{1,0:T(8,128)(2,1)} %constant.60.clone.refs_6_) | copy-start | bytes 15364
  5.9 5.1 %collective-permute-start.1 = (f32[112,128]{1,0:T(8,128)S(1)}, f32[112,128]{1,0:T(8,128)S(1)}, u32[]{:S(2)}, u32[]{:S(2)}) collective-permute-start(f32[112,128]{1,0:T(8,128)S(1)} %get-tuple-element.13), channel_id=1, source_target_pairs={{0,2},{2,0},{1,3},{3,1},{4,6},{6,4},{5,7},{7,5},{8,10},{10,8},{9,1... | collective-permute-start | bytes 172040 | tf_op jit(solution)/shard_map/ppermute | solution.py:342
  11.8 9.4 %collective-permute-start.2 = (f32[192,128]{1,0:T(8,128)S(1)}, f32[192,128]{1,0:T(8,128)S(1)}, u32[]{:S(2)}, u32[]{:S(2)}) collective-permute-start(f32[192,128]{1,0:T(8,128)S(1)} %get-tuple-element.16), channel_id=1, source_target_pairs={{0,4},{4,8},{8,12},{12,0},{1,5},{5,9},{9,13},{13,1},{2,6},{6,10},{... | collective-permute-start | bytes 294920 | tf_op jit(solution)/shard_map/ppermute | solution.py:342
  13.7 7.5 %collective-permute-start.4 = (f32[160,128]{1,0:T(8,128)S(1)}, f32[160,128]{1,0:T(8,128)S(1)}, u32[]{:S(2)}, u32[]{:S(2)}) collective-permute-start(f32[160,128]{1,0:T(8,128)S(1)} %get-tuple-element.18), channel_id=1, source_target_pairs={{0,12},{4,0},{8,4},{12,8},{1,13},{5,1},{9,5},{13,9},{2,14},{6,2},{... | collective-permute-start | bytes 245768 | tf_op jit(solution)/shard_map/ppermute | solution.py:342
  15.8 5.4 %collective-permute-start.3 = (f32[48,128]{1,0:T(8,128)S(1)}, f32[48,128]{1,0:T(8,128)S(1)}, u32[]{:S(2)}, u32[]{:S(2)}) collective-permute-start(f32[48,128]{1,0:T(8,128)S(1)} %get-tuple-element.17), channel_id=1, source_target_pairs={{0,8},{4,12},{8,0},{12,4},{1,9},{5,13},{9,1},{13,5},{2,10},{6,14},... | collective-permute-start | bytes 73736 | tf_op jit(solution)/shard_map/ppermute | solution.py:342

commit v2 on v1

--- a/solution.py
+++ b/solution.py
@@ -79,33 +79,70 @@
     return np.pad(matrix, ((0, rows - matrix.shape[0]), (0, cols - matrix.shape[1])))
 
 
-def columns(axis):
+HALO = ((1, 3), (2, 0))
+
+
+def taps(level):
+    inner = down(256) if level == 0 else down(128) @ down(256)
+    row, stride = 32, 2 << level
+    values = inner[row, stride * row :]
+    return [float(v) for v in values[: np.nonzero(values)[0][-1] + 1]]
+
+
+def lane_matrix(pair, cells, lanes):
+    left = [table.copy() for table in pair]
+    out = np.zeros((len(cells), LANES))
+    inside = [i for i in cells if 0 <= i < left[0].shape[1]]
+    rows = [k for k, i in enumerate(cells) if 0 <= i < left[0].shape[1]]
+    for lane, (level, column) in lanes.items():
+        out[rows, lane] = left[level][column + 1, inside]
+        left[level][column + 1, inside] = 0
+    assert not any(table[:, inside].any() for table in left)
+    return out
+
+
+def side_lanes(own):
+    left = {j: (1, j) for j in range(4)}
+    left.update({64 + j: (0, j) for j in range(3)})
+    left.update({32 + HALO[0][0]: (0, -1), 32 + HALO[1][0]: (1, -1)})
+    right = {j: (1, j) for j in range(LANES - 3, LANES)}
+    right.update({62 + j: (0, own - 2 + j) for j in range(2)})
+    right.update({32 + HALO[0][1]: (0, own), 32 + HALO[1][1]: (1, own // 2)})
+    return left, right
+
+
+def side_tables(axis):
     n, block = axis.parts, axis.block
-    sides = [] if n == 1 else [0] if n == 2 else [-1, 1]
-    tables = []
+    sides = [0] if n == 2 else [-1, 1]
+    own = block // 2
+    lanes = side_lanes(own)
+    out = []
     for t in range(n):
-        fine = np.concatenate(list(axis.fine[t]), 1)
-        coarse = np.concatenate(list(axis.coarse[t]), 1)
-        halo = np.stack([fine[0], fine[-1], coarse[0], coarse[-1]])
-        halo = pad_to(halo, LANES, n * block)
-        whole = np.concatenate([fine[1:-1], halo, coarse[1:-1]]).T
-        at = [range(t * block, (t + 1) * block)]
+        pair = [np.concatenate(list(table[t]), 1) for table in (axis.fine, axis.coarse)]
+        tables = []
         for side in sides:
-            if side == 0:
-                side = 1 - 2 * t
+            side = side or 1 - 2 * t
             start = (t + 1) * block if side > 0 else t * block - LANES
-            at.append(range(start, start + LANES))
-        picked = np.zeros((sum(len(a) for a in at), whole.shape[1]))
-        row = 0
-        for a in at:
-            for i in a:
-                if 0 <= i < n * block:
-                    picked[row] = whole[i]
-                row += 1
-        outside = np.delete(whole, [i for a in at for i in a if 0 <= i < n * block], 0)
-        assert not outside.any()
-        tables.append(split(picked))
-    return np.stack(tables)
+            tables.append(lane_matrix(pair, range(start, start + LANES), lanes[side > 0]))
+        difference = []
+        for level, table in enumerate(pair):
+            values, stride = taps(level), 2 << level
+            wide = own >> level
+            same = table.copy()
+            for r in range(wide + 2):
+                for i in range(t * block, (t + 1) * block):
+                    k = abs(stride * (t * wide + r - 1) - i)
+                    same[r, i] -= values[k] if k < len(values) else 0.0
+            difference.append(np.where(abs(same) > 1e-12, same, 0.0))
+        if t == 0:
+            ends = range(0, LANES)
+        else:
+            ends = range((t + 1) * block - LANES, (t + 1) * block)
+        rest = np.setdiff1d(range(t * block, (t + 1) * block), ends)
+        assert not any(d[:, rest].any() for d in difference)
+        tables.append(lane_matrix(difference, ends, lanes[t > 0]))
+        out.append(split(np.concatenate(tables)))
+    return np.stack(out)
 
 
 def touched(blocks):
@@ -263,41 +300,154 @@
         return fine, jnp.concatenate([side, ref[at : at + self.coarse]], 1)
 
 
-def over_columns(tiles, plans, n_slabs, volume, *refs):
-    slabs, (wx, wy), (high, low, *sent) = refs[:n_slabs], refs[n_slabs : n_slabs + 2], refs[n_slabs + 2 :]
-    depth, height, width = volume.shape
-    cells = halves(volume[...].reshape(depth * height, width))
-    total = mm3(cells, (wx[0, :width], wx[1, :width]))
-    at = width
-    for slab in slabs:
-        edge = halves(slab[...].reshape(depth * height, LANES))
-        total = total + mm3(edge, (wx[0, at : at + LANES], wx[1, at : at + LANES]))
-        at += LANES
+def sections(parts):
+    return jnp.concatenate([p[...].reshape(-1, p.shape[2]) for p in parts], 0)
+
+
+class Tables:
+    def __init__(self, lanes):
+        self.lanes, self.blocks, self.count = lanes, [], 0
+
+    def add(self, tables):
+        places, two, rows, cols = tables.shape
+        assert rows % 16 == 0 and cols <= self.lanes
+        flat = tables.reshape(places * two * rows, cols)
+        self.blocks.append(np.pad(flat, ((0, 0), (0, self.lanes - cols))))
+        start = self.count
+        self.count += len(flat)
+        return start, two * rows, cols
+
+    def whole(self):
+        return jnp.asarray(np.concatenate(self.blocks))
+
+
+def fetch(table, spot, place, out, sem, col=0):
+    start, rows, _ = spot
+    here = pl.ds(pl.multiple_of(start + place * rows, 16), rows)
+    copy = pltpu.make_async_copy(table.at[here, pl.ds(col, out.shape[1])], out, sem)
+    copy.start()
+    return copy
+
+
+def ladder(distance, values):
+    out = jnp.zeros(distance.shape, f32)
+    for k, value in enumerate(values):
+        out = jnp.where(distance == k, value, out)
+    return out
+
+
+def chunk_matrices(rows):
+    row = lax.broadcasted_iota(jnp.int32, (8, LANES), 0)
+    lane = lax.broadcasted_iota(jnp.int32, (8, LANES), 1)
+    near = jnp.where(lane < LANES // 2, lane, lane - LANES)
+    fine = ladder(jnp.abs(row - 2 * near), taps(0))
+    coarse = ladder(jnp.abs(row - 4 * near), taps(1))
+    level, first, last = [], [], []
+    count = rows // 8
+    for r in range(count):
+        f = pltpu.roll(fine, 4 * r % LANES, 1) if r else fine
+        a = pltpu.roll(coarse, 2 * r % LANES, 1) if r else coarse
+        b = pltpu.roll(coarse, (2 * r + LANES // 2) % LANES, 1)
+        if r < 2:
+            a = jnp.where((lane < 96) | (lane == LANES - 1), a, 0.0)
+            a = a + pltpu.roll(jnp.where(lane == LANES - 1, f, 0.0), LANES - 1, 1)
+            b = b + pltpu.roll(jnp.where(lane >= LANES - 2, f, 0.0), 58, 1)
+            f = jnp.where(lane < LANES // 2, f, 0.0)
+        if r >= count - 2:
+            a = a + pltpu.roll(jnp.where(lane < 3, f, 0.0), 68, 1)
+            b = jnp.where((lane == 0) | (lane >= LANES // 2 - 8), b, 0.0)
+            b = b + pltpu.roll(jnp.where(lane == 0, f, 0.0), 3, 1)
+            f = jnp.where(lane >= LANES // 2, f, 0.0)
+        level.append(f)
+        first.append(a)
+        last.append(b)
+    level, first, last = (halves(jnp.concatenate(tiles, 0)) for tiles in (level, first, last))
+    return [tuple(jnp.concatenate(p, 1) for p in zip(level, rest)) for rest in (first, last)]
+
+
+def own_columns(places, spots, first, last, table, total, wy, wside, sems):
+    send_spot, side_spot = spots
+    copies = [
+        fetch(table, send_spot, choose(places, lax.axis_index("tile")), wy, sems.at[0]),
+        fetch(table, side_spot, lax.axis_index("xt"), wside, sems.at[1]),
+    ]
+    cells = halves(sections((first, last)))
+    width = cells[0].shape[1] // 2
+    out = [
+        mm3(tuple(p[:, c * width : (c + 1) * width] for p in cells), w) for c, w in enumerate(chunk_matrices(width))
+    ]
+    a, b = (part[:, LANES:] for part in out)
+    lane = lax.broadcasted_iota(jnp.int32, a.shape, 1)
+    total[:, :LANES] = out[0][:, :LANES] + jnp.where(lane >= LANES - 2, pltpu.roll(b, LANES - 58, 1), 0.0)
+    total[:, LANES : 2 * LANES] = out[1][:, :LANES] + jnp.where(lane < 3, pltpu.roll(a, LANES - 68, 1), 0.0)
+    halo = jnp.where((lane == 1) | (lane == 2), pltpu.roll(a, 3, 1), b)
+    total[:, 2 * LANES : 3 * LANES] = jnp.where(lane < 4, halo, 0.0)
+    total[:, 3 * LANES :] = jnp.where(lane < 68, a, 0.0) + jnp.where(lane >= 61, b, 0.0)
+    for copy in copies:
+        copy.wait()
+
+
+def over_columns(tiles, plans, total, wy, wside, first, last, *refs):
+    n_slabs = wside.shape[0] // 2 // LANES - 1
+    slabs, (high, low, *sent) = refs[:n_slabs], refs[n_slabs:]
+    at = pl.multiple_of(jnp.where(lax.axis_index("xt") == 0, 0, first.shape[2] - LANES), LANES)
+    ends = [p[:, :, pl.ds(at, LANES)].reshape(-1, LANES) for p in (first, last)]
+    edge = jnp.concatenate([p[...].reshape(-1, LANES) for p in slabs] + [jnp.concatenate(ends, 0)], 1)
+    half = wside.shape[0] // 2
+    side = mm3(halves(edge), (wside[:half], wside[half:]))
+    lane = lax.broadcasted_iota(jnp.int32, side.shape, 1)
+    level, halo = pltpu.roll(side, LANES // 2, 1), pltpu.roll(side, LANES - 32, 1)
+    total = total[...] + jnp.concatenate(
+        [
+            jnp.where(lane < 3, level, 0.0),
+            jnp.where(lane >= LANES - 2, level, 0.0),
+            jnp.where(lane < 4, halo, 0.0),
+            jnp.where((lane < 4) | (lane >= LANES - 3), side, 0.0),
+        ],
+        1,
+    )
     x = halves(total)
     high[...], low[...] = x
     level_end = (tiles + 1) * LANES
-    at = 0
+    at, half = 0, wy.shape[0] // 2
     for packing, out in zip(plans, sent):
         rows, more = round_up(packing.fine, 16), round_up(packing.coarse, 16)
-        fine = mm3((wy[0, at : at + rows], wy[1, at : at + rows]), tuple(p[:, :level_end] for p in x))
+        fine = mm3((wy[at : at + rows], wy[half + at : half + at + rows]), tuple(p[:, :level_end] for p in x))
         at += rows
-        coarse = mm3((wy[0, at : at + more], wy[1, at : at + more]), tuple(p[:, level_end - LANES :] for p in x))
+        coarse = mm3((wy[at : at + more], wy[half + at : half + at + more]), tuple(p[:, level_end - LANES :] for p in x))
         at += more
         packing.store(out, fine[: packing.fine], coarse[: packing.coarse])
 
 
-def over_rows(tiles, plans_in, plans_out, fine_own, coarse_own, high, low, *refs):
+def own_rows(tiles, places, spots, high, low, table, fine, coarse, gf_got, gc_got, gf, gc, sems):
+    z_places, y_places = places
+    place = choose(z_places, lax.axis_index("sec")) * (max(y_places) + 1) + choose(y_places, lax.axis_index("tile"))
+    cells = high.shape[0]
+    copies = []
+    for i, (spot, own, got) in enumerate(zip(spots, (gf, gc), (gf_got, gc_got))):
+        copies.append(fetch(table, spot, place, own, sems.at[2 * i]))
+        copies.append(fetch(table, spot, place, got, sems.at[2 * i + 1], cells))
+    level_end = (tiles + 1) * LANES
+    copies[0].wait()
+    half = gf.shape[0] // 2
+    fine[...] = mm3((gf[:half], gf[half:]), (high[:, :level_end], low[:, :level_end]))
+    copies[2].wait()
+    half = gc.shape[0] // 2
+    coarse[...] = mm3((gc[:half], gc[half:]), (high[:, level_end - LANES :], low[:, level_end - LANES :]))
+    copies[1].wait()
+    copies[3].wait()
+
+
+def over_rows(plans_in, plans_out, fine_own, coarse_own, fine_ref, coarse_ref, gf, gc, *refs):
     n_in = len(plans_in)
-    got, (gf, gc), (fine_out, coarse_out, *sent) = refs[:n_in], refs[n_in : n_in + 2], refs[n_in + 2 :]
-    level_end = (tiles + 1) * LANES
-    cells = high.shape[0]
-    fine = mm3((gf[0, :, :cells], gf[1, :, :cells]), (high[:, :level_end], low[:, :level_end]))
-    coarse = mm3((gc[0, :, :cells], gc[1, :, :cells]), (high[:, level_end - LANES :], low[:, level_end - LANES :]))
-    at = cells
+    got, (fine_out, coarse_out, *sent) = refs[:n_in], refs[n_in:]
+    fine, coarse = fine_ref[...], coarse_ref[...]
+    gf, gc = ((g.at[: g.shape[0] // 2], g.at[g.shape[0] // 2 :]) for g in (gf, gc))
+    at = 0
     for packing, ref in zip(plans_in, got):
         more, less = packing.load(ref, True)
-        fine = fine + mm3(tuple(gf[i, :, at : at + packing.fine] for i in range(2)), halves(more))
-        coarse = coarse + mm3(tuple(gc[i, :, at : at + packing.coarse] for i in range(2)), halves(less))
+        fine = fine + mm3(tuple(g[:, at : at + packing.fine] for g in gf), halves(more))
+        coarse = coarse + mm3(tuple(g[:, at : at + packing.coarse] for g in gc), halves(less))
         at += LANES
     fine_out[...] = fine[:fine_own]
     coarse_out[...] = coarse[:coarse_own]
@@ -308,10 +458,9 @@
         also += round_up(packing.coarse, 16)
 
 
-def over_sections(tiles, plans, starts, fine_at, coarse_at, volume, fine_ref, coarse_ref, *refs):
+def over_sections(tiles, plans, starts, fine_at, coarse_at, first, last, fine_ref, coarse_ref, *refs):
     n_in = len(plans)
     got, (ex, ezy, fx, fzy), (zero_out, one_out, coarse_out, level) = refs[:n_in], refs[n_in : n_in + 4], refs[n_in + 4 :]
-    depth, height, width = volume.shape
     level[...] = fine_ref[...]
     coarse = coarse_ref[...]
     for packing, start, ref in zip(plans, starts, got):
@@ -320,13 +469,13 @@
             level[start : start + packing.fine] += more
         coarse = coarse + less
     wide = halves(mm2_right(halves(level[...]), ex[...]))
-    zero_out[...] = volume[...] - mm2(ezy[...], wide).reshape(volume.shape)
+    zero_out[...] = (sections((first, last)) - mm2(ezy[...], wide)).reshape(zero_out.shape)
     narrow = halves(mm2_right(halves(coarse), fx[...]))
-    first, count = fine_at
-    own = level[first : first + count, : tiles * LANES]
+    start, count = fine_at
+    own = level[start : start + count, : tiles * LANES]
     one_out[...] = (own - mm2(fzy[...], narrow)).reshape(one_out.shape)
-    first, count = coarse_at
-    coarse_out[...] = coarse[first : first + count, LANES:].reshape(coarse_out.shape)
+    start, count = coarse_at
+    coarse_out[...] = coarse[start : start + count, LANES:].reshape(coarse_out.shape)
 
 
 def mm2_right(a, b):
@@ -342,49 +491,61 @@
     return lax.ppermute(x, axis, [(i, (i + shift) % n) for i in range(n)])
 
 
-def call(body, outs, args, scratch=()):
-    vmem = pl.BlockSpec(memory_space=pltpu.VMEM)
+def call(body, outs, args, scratch=(), fetched=0, limit=48):
+    vmem, stays = pl.BlockSpec(memory_space=pltpu.VMEM), pl.BlockSpec(memory_space=pl.ANY)
     moved = sum(math.prod(a.shape) * a.dtype.itemsize for a in (*args, *outs))
     return pl.pallas_call(
         body,
         out_shape=outs,
-        in_specs=[vmem] * len(args),
+        in_specs=[vmem] * (len(args) - fetched) + [stays] * fetched,
         out_specs=[vmem] * len(outs),
         scratch_shapes=list(scratch),
         cost_estimate=cost(2 * 10**8, moved),
-        compiler_params=pltpu.CompilerParams(vmem_limit_bytes=48 * 2**20),
+        compiler_params=pltpu.CompilerParams(vmem_limit_bytes=int(limit * 2**20)),
     )(*args)
 
 
-def unique(tables):
-    kept, places, seen = [], [], {}
-    for table in tables:
-        key = tuple(t.tobytes() for t in table)
-        if key not in seen:
-            seen[key] = len(kept)
-            kept.append(table)
-        places.append(seen[key])
-    return [np.stack(column) for column in zip(*kept)], np.array(places, np.int32)
-
-
-def shards(sections, volume):
-    sizes = (sections, volume.shape[1] * lax.axis_size("tile"), volume.shape[2] * lax.axis_size("xt"))
+def choose(places, index):
+    if list(places) == list(range(len(places))):
+        return index
+    out = jnp.int32(places[0])
+    for i, place in enumerate(places):
+        out = jnp.where(index == i, jnp.int32(place), out)
+    return out
+
+
+def unique(keys):
+    seen = {}
+    for i, key in enumerate(keys):
+        seen.setdefault(key, i)
+    kept = list(seen.values())
+    return kept, [kept.index(seen[key]) for key in keys]
+
+
+def key_of(*arrays):
+    return tuple(a.tobytes() for a in arrays)
+
+
+def shards(depth_of_all, volume):
+    sizes = (depth_of_all, volume.shape[1] * lax.axis_size("tile"), volume.shape[2] * lax.axis_size("xt"))
     zaxis, yaxis, xaxis = (Axis(s, lax.axis_size(a)) for s, a in zip(sizes, ("sec", "tile", "xt")))
     depth, height, width = volume.shape
     cells = depth * height
     tiles = width // 2 // LANES
-    coarse_tiles = width // 4 // LANES
-    assert coarse_tiles == 1 and width % (4 * LANES) == 0
-    z, y, x = (lax.axis_index(a) for a in ("sec", "tile", "xt"))
-
-    if xaxis.parts == 1:
-        slabs = []
-    elif xaxis.parts == 2:
-        edge = jnp.where(x == 0, volume[:, :, width - LANES :], volume[:, :, :LANES])
+    assert width == 4 * LANES
+    x = lax.axis_index("xt")
+
+    cut = depth // 2 + 1
+    first = lax.dynamic_slice_in_dim(volume, -x, cut, 0, allow_negative_indices=False)
+    last = lax.dynamic_slice_in_dim(volume, cut + x, depth - cut, 0, allow_negative_indices=False)
+
+    assert xaxis.parts > 1
+    if xaxis.parts == 2:
+        edge = lax.dynamic_slice_in_dim(volume, (width - LANES) * (1 - x), LANES, 2, allow_negative_indices=False)
         slabs = [shifted(edge, "xt", 1)]
     else:
         slabs = [shifted(volume[:, :, width - LANES :], "xt", 1), shifted(volume[:, :, :LANES], "xt", -1)]
-    wx = lax.dynamic_index_in_dim(jnp.asarray(columns(xaxis)), x, 0, False)
+    wside = side_tables(xaxis)
 
     rowplan = RowPlan(yaxis, depth)
     row_packs = []
@@ -398,9 +559,9 @@
             for level in range(2):
                 m = rowplan.send(yaxis, s, shift, level)
                 blocks.append(pad_to(m, round_up(m.shape[0], 16), cells))
-        wys.append((split(np.concatenate(blocks)),))
-    (wy,), place = unique(wys)
-    wy = lax.dynamic_index_in_dim(jnp.asarray(wy), jnp.asarray(place)[y], 0, False)
+        wys.append(split(np.concatenate(blocks)))
+    kept, send_places = unique([key_of(m) for m in wys])
+    wy = np.stack([wys[s] for s in kept])
 
     fslots, ffirst, fcount = fine_slots(zaxis, yaxis)
     cslots, cfirst, ccount = coarse_slots(zaxis, yaxis)
@@ -427,9 +588,19 @@
         starts.append(start)
         z_packs.append(Packing(end - start, len(cslots), tiles))
 
-    gs = []
-    for s in range(zaxis.parts):
-        for ty in range(yaxis.parts):
+    def z_key(s):
+        to = [(s + k) % zaxis.parts for k in [0] + zaxis.shifts]
+        return key_of(*(table[t, s] * (1 if t >= s else -1) for t in to for table in (zaxis.fine, zaxis.coarse)))
+
+    def y_key(t):
+        placed = [rowplan.place(yaxis, t, k, level) for k in yaxis.shifts for level in range(2)]
+        return key_of(yaxis.fine[t, t], yaxis.coarse[t, t], *placed)
+
+    z_kept, z_places = unique([z_key(s) for s in range(zaxis.parts)])
+    y_kept, y_places = unique([y_key(t) for t in range(yaxis.parts)])
+    gf, gc = [], []
+    for s in z_kept:
+        for ty in y_kept:
             fine, coarse = matrices(s, s, ty)
             fines, coarses = [fine], [pad_to(coarse, round_up(len(cslots), 16), coarse.shape[1])]
             for shift, start, packing in zip(zaxis.shifts, starts, z_packs):
@@ -437,37 +608,58 @@
                 fine = fine[start : start + packing.fine]
                 fines.append(pad_to(fine, round_up(packing.fine, 16), fine.shape[1]))
                 coarses.append(pad_to(coarse, round_up(packing.coarse, 16), coarse.shape[1]))
-            gs.append((split(np.concatenate(fines)), split(np.concatenate(coarses))))
-    (gf, gc), place = unique(gs)
-    at = jnp.asarray(place)[z * yaxis.parts + y]
-    gf = lax.dynamic_index_in_dim(jnp.asarray(gf), at, 0, False)
-    gc = lax.dynamic_index_in_dim(jnp.asarray(gc), at, 0, False)
+            gf.append(split(np.concatenate(fines)))
+            gc.append(split(np.concatenate(coarses)))
+    gf, gc = np.stack(gf), np.stack(gc)
 
     own = width // 2
-    table = expand(own)
+    one = expand(own)
     ex = np.zeros((own + LANES, width))
-    ex[:own], ex[own], ex[own + 1] = table[:, 1:-1].T, table[:, 0], table[:, -1]
+    ex[:own], ex[own + HALO[0][0]], ex[own + HALO[0][1]] = one[:, 1:-1].T, one[:, 0], one[:, -1]
     own = width // 4
-    table = expand(own)
+    one = expand(own)
     fx = np.zeros((LANES + own, width // 2))
-    fx[2], fx[3], fx[LANES:] = table[:, 0], table[:, -1], table[:, 1:-1].T
+    fx[HALO[1][0]], fx[HALO[1][1]], fx[LANES:] = one[:, 0], one[:, -1], one[:, 1:-1].T
     ezy = slot_expand(fslots, depth // 2, height // 2)
     fzy = slot_expand(cslots, depth // 4, height // 4)
     constants = [jnp.asarray(m.astype(ml_dtypes.bfloat16)) for m in (ex, ezy, fx, fzy)]
 
     n = (tiles + 1 + 1) * LANES
     shape = jax.ShapeDtypeStruct
+    tables = Tables(max(t.shape[-1] for t in (gf, gc, wy)))
+    f_spot, c_spot, send_spot, side_spot = (tables.add(t) for t in (gf, gc, wy, wside))
+    table = tables.whole()
+    total, wy, wside = call(
+        functools.partial(own_columns, send_places, (send_spot, side_spot)),
+        [shape((cells, n), f32), shape(send_spot[1:], bf16), shape(side_spot[1:], bf16)],
+        [first, last, table],
+        [pltpu.SemaphoreType.DMA((2,))],
+        fetched=1,
+    )
     high, low, *sent = call(
-        functools.partial(over_columns, tiles, row_packs, len(slabs)),
+        functools.partial(over_columns, tiles, row_packs),
         [shape((cells, n), bf16)] * 2 + [shape((p.rows, LANES), f32) for p in row_packs],
-        [volume, *slabs, wx, wy],
+        [total, wy, wside, first, last, *slabs],
     )
     got = [shifted(a, "tile", k) for a, k in zip(sent, yaxis.shifts)]
+    (_, f_rows, f_cols), (_, c_rows, c_cols) = f_spot, c_spot
+    fine, coarse, gf, gc = call(
+        functools.partial(own_rows, tiles, (z_places, y_places), (f_spot, c_spot)),
+        [
+            shape((f_rows // 2, (tiles + 1) * LANES), f32),
+            shape((c_rows // 2, 2 * LANES), f32),
+            shape((f_rows, f_cols - cells), bf16),
+            shape((c_rows, c_cols - cells), bf16),
+        ],
+        [high, low, table],
+        [pltpu.VMEM((f_rows, cells), bf16), pltpu.VMEM((c_rows, cells), bf16), pltpu.SemaphoreType.DMA((4,))],
+        fetched=1,
+    )
     fine, coarse, *sent = call(
-        functools.partial(over_rows, tiles, row_packs, z_packs, len(fslots), len(cslots)),
+        functools.partial(over_rows, row_packs, z_packs, len(fslots), len(cslots)),
         [shape((len(fslots), (tiles + 1) * LANES), f32), shape((len(cslots), 2 * LANES), f32)]
         + [shape((p.rows, LANES), f32) for p in z_packs],
-        [high, low, *got, gf, gc],
+        [fine, coarse, gf, gc, *got],
     )
     got = [shifted(a, "sec", k) for a, k in zip(sent, zaxis.shifts)]
     return tuple(
@@ -478,7 +670,7 @@
                 shape((depth // 2, height // 2, width // 2), f32),
                 shape((depth // 4, height // 4, width // 4), f32),
             ],
-            [volume, fine, coarse, *got, *constants],
+            [first, last, fine, coarse, *got, *constants],
             [pltpu.VMEM((len(fslots), (tiles + 1) * LANES), f32)],
         )
     )

time: 22.8 us -> 21.1 us (0.925)
  Pallas kernels: 3.23 us -> 5.8 us
  local copies, waits for them, and re-layouts: 3.54 us -> 1.13 us
  other arithmetic: 1.06 us -> 0 us
  waiting for transfers between devices: 6.02 us -> 5.3 us
    squeeze x4 -> x0, local copies, waits for them, and re-layouts: 3.5 us -> none  [the longest x1 1.4 us: shards(): wx = lax.dynamic_index_in_dim(jnp.asarray(columns(xaxis)), x, 0, False)]
    pallas_call x3 -> x5, Pallas kernels: 3.23 us -> 5.8 us  [call(): pl.pallas_call(body, out_shape=outs, in_specs=[vmem] * (len(args) - fetch...]
    select_n x1 -> x0, other arithmetic: 1.06 us -> none  [shards(): edge = jnp.where(x == 0, volume[:, :, width - LANES:], volume[:, :, :LANES])]
    unnamed x12 -> x10, local copies, waits for them, and re-layouts: 0.04 us -> 1.06 us
    ppermute x5, waiting for transfers between devices: 6.02 us -> 5.3 us  [shifted(): return lax.ppermute(x, axis, [(i, (i + shift) % n) for i in range(n)])]
  transfers between devices with their start and end apart: 5 -> 5, of which waited for: 2 -> 2; matrix products, arithmetic and copies ran while one was open for 15% -> 0% of each run, Pallas kernels for 0% -> 16%
where the time goes in v2:
time: 21.1 us; the launch traced here: 20.9 us
  starting transfers between devices  7.96 us (38%)
  Pallas kernels  5.8 us (27%)
  waiting for transfers between devices  5.3 us (25%)
  local copies, waits for them, and re-layouts  1.13 us (5%)
  between operations  0.75 us (4%)
    ppermute x5, starting transfers between devices, shifted(): return lax.ppermute(x, axis, [(i, (i + shift) % n) for i in range(n)])  7.96 us
    pallas_call x5, Pallas kernels, call(): pl.pallas_call(body, out_shape=outs, in_specs=[vmem] * (len(args) - fetch...  5.8 us
    ppermute x5, waiting for transfers between devices, shifted(): return lax.ppermute(x, axis, [(i, (i + shift) % n) for i in range(n)])  5.3 us
    unnamed x10, local copies, waits for them, and re-layouts  1.06 us
  transfers between devices with their start and end apart: 5, of which 2 were waited for; matrix products, arithmetic and copies ran while one was open for 0% of the time, Pallas kernels for 16%

profile of v2, /device:TPU:0, one launch (start us, length us, event | category | flops | bytes accessed | tf_op | source)
XLA Modules:
  0.0 20.9 jit_solution(13124944722674000489)
XLA Ops:
  0.6 0.0 copy-start
  0.6 1.0 %copy-done = f32[8,32,512]{2,1,0:T(8,128)S(1)} copy-done((f32[8,32,512]{2,1,0:T(8,128)S(1)}, f32[8,32,512]{2,1,0:T(8,128)}, u32[]{:S(2)}) %copy-start) | copy-done | bytes 524312
  1.7 0.5 %collective-permute-start = (f32[8,32,128]{2,1,0:T(8,128)S(1)}, f32[8,32,128]{2,1,0:T(8,128)S(1)}, u32[]{:S(2)}, u32[]{:S(2)}) collective-permute-start(f32[8,32,128]{2,1,0:T(8,128)S(1)} %constant_dynamic-slice_fusion), channel_id=1, source_target_pairs={{0,1},{1,0},{2,3},{3,2},{4,5},{5,4},{6,7},{7,6},{8,9},{9,8},{10,11... | collective-permute-start | bytes 393224 | tf_op jit(solution)/shard_map/ppermute | solution.py:491
  2.3 0.0 copy-start.1
  2.3 0.0 copy-start.2
  2.3 0.0 copy-start.3
  2.3 0.0 copy-start.4
  2.3 1.5 %shard_map.85 = (f32[256,512]{1,0:T(8,128)S(1)}, bf16[160,256]{1,0:T(8,128)(2,1)S(1)}, bf16[512,128]{1,0:T(8,128)(2,1)S(1)}) custom-call(f32[5,32,512]{2,1,0:T(8,128)S(1)} %constant_dynamic-slice_fusion.2.first, f32[3,32,512]{2,1,0:T(8,128)S(1)} %constant_dynamic-slice_fusion.1.last, bf16[8512,384]{1,0:T(8,128)(2,1)} %constant.26.clone.table), custom_call_target="tpu_custom_call" | custom-call | flops 200000000 | bytes 7798784 | tf_op jit(solution)/shard_map/pallas_call | solution.py:497
  3.9 0.0 collective-permute-done.refs_0_
  3.9 0.7 %shard_map.86 = (bf16[256,512]{1,0:T(8,128)(2,1)S(1)}, bf16[256,512]{1,0:T(8,128)(2,1)S(1)}, f32[112,128]{1,0:T(8,128)S(1)}) custom-call(f32[256,512]{1,0:T(8,128)S(1)} %get-tuple-element.18.total, bf16[160,256]{1,0:T(8,128)(2,1)S(1)} %get-tuple-element.19.wy, bf16[512,128]{1,0:T(8,128)(2,1)S(1)} %get-tuple-element.20.wside, ...), custom_call_target="tpu_custom_call" | custom-call | flops 200000000 | bytes 1974272 | tf_op jit(solution)/shard_map/pallas_call | solution.py:497
  4.5 2.5 %collective-permute-start.1 = (f32[112,128]{1,0:T(8,128)S(1)}, f32[112,128]{1,0:T(8,128)S(1)}, u32[]{:S(2)}, u32[]{:S(2)}) collective-permute-start(f32[112,128]{1,0:T(8,128)S(1)} %get-tuple-element.27), channel_id=1, source_target_pairs={{0,2},{2,0},{1,3},{3,1},{4,6},{6,4},{5,7},{7,5},{8,10},{10,8},{9,1... | collective-permute-start | bytes 172040 | tf_op jit(solution)/shard_map/ppermute | solution.py:491
  7.1 1.7 %shard_map.87 = (f32[256,384]{1,0:T(8,128)S(1)}, f32[192,256]{1,0:T(8,128)S(1)}, bf16[512,128]{1,0:T(8,128)(2,1)S(1)}, bf16[384,128]{1,0:T(8,128)(2,1)S(1)}) custom-call(bf16[256,512]{1,0:T(8,128)(2,1)S(1)} %get-tuple-element.21.high, bf16[256,512]{1,0:T(8,128)(2,1)S(1)} %get-tuple-element.22.low, bf16[8512,384]{1,0:T(8,128)(2,1)} %constant.26.clone.table), custom_call_target="tpu_custom_call" | custom-call | flops 200000000 | bytes 7880704 | tf_op jit(solution)/shard_map/pallas_call | solution.py:497
  8.8 0.8 %collective-permute-done.1.refs_0_ = f32[112,128]{1,0:T(8,128)S(1)} collective-permute-done((f32[112,128]{1,0:T(8,128)S(1)}, f32[112,128]{1,0:T(8,128)S(1)}, u32[]{:S(2)}, u32[]{:S(2)}) %collective-permute-start.1) | collective-permute-done | bytes 57376 | tf_op jit(solution)/shard_map/ppermute | solution.py:491
  9.6 0.5 %shard_map.88 = (f32[112,384]{1,0:T(8,128)S(1)}, f32[40,256]{1,0:T(8,128)S(1)}, f32[192,128]{1,0:T(8,128)S(1)}, f32[48,128]{1,0:T(8,128)S(1)}, f32[160,128]{1,0:T(8,128)S(1)}) custom-call(f32[256,384]{1,0:T(8,128)S(1)} %get-tuple-element.23.fine_ref, f32[192,256]{1,0:T(8,128)S(1)} %get-tuple-element.24.coarse_ref, ...), custom_call_target="tpu_custom_call" | custom-call | flops 200000000 | bytes 1294336 | tf_op jit(solution)/shard_map/pallas_call | solution.py:497
  10.1 1.9 %collective-permute-start.2 = (f32[192,128]{1,0:T(8,128)S(1)}, f32[192,128]{1,0:T(8,128)S(1)}, u32[]{:S(2)}, u32[]{:S(2)}) collective-permute-start(f32[192,128]{1,0:T(8,128)S(1)} %get-tuple-element.30), channel_id=1, source_target_pairs={{0,4},{4,8},{8,12},{12,0},{1,5},{5,9},{9,13},{13,1},{2,6},{6,10},{... | collective-permute-start | bytes 294920 | tf_op jit(solution)/shard_map/ppermute | solution.py:491
  12.0 2.1 %collective-permute-start.4 = (f32[160,128]{1,0:T(8,128)S(1)}, f32[160,128]{1,0:T(8,128)S(1)}, u32[]{:S(2)}, u32[]{:S(2)}) collective-permute-start(f32[160,128]{1,0:T(8,128)S(1)} %get-tuple-element.32), channel_id=1, source_target_pairs={{0,12},{4,0},{8,4},{12,8},{1,13},{5,1},{9,5},{13,9},{2,14},{6,2},{... | collective-permute-start | bytes 245768 | tf_op jit(solution)/shard_map/ppermute | solution.py:491
  14.1 1.0 %collective-permute-start.3 = (f32[48,128]{1,0:T(8,128)S(1)}, f32[48,128]{1,0:T(8,128)S(1)}, u32[]{:S(2)}, u32[]{:S(2)}) collective-permute-start(f32[48,128]{1,0:T(8,128)S(1)} %get-tuple-element.31), channel_id=1, source_target_pairs={{0,8},{4,12},{8,0},{12,4},{1,9},{5,13},{9,1},{13,5},{2,10},{6,14},... | collective-permute-start | bytes 73736 | tf_op jit(solution)/shard_map/ppermute | solution.py:491
  15.0 4.5 %collective-permute-done.3.refs_1_ = f32[48,128]{1,0:T(8,128)S(1)} collective-permute-done((f32[48,128]{1,0:T(8,128)S(1)}, f32[48,128]{1,0:T(8,128)S(1)}, u32[]{:S(2)}, u32[]{:S(2)}) %collective-permute-start.3) | collective-permute-done | bytes 24608 | tf_op jit(solution)/shard_map/ppermute | solution.py:491
  19.5 0.0 collective-permute-done.4.refs_2_
  19.5 0.0 collective-permute-done.2.refs_0_
  19.5 0.0 copy-done.1
  19.5 0.0 copy-done.2
  19.5 0.0 copy-done.3
  19.5 0.0 copy-done.4
  19.5 1.4 %shard_map.89 = (f32[8,32,512]{2,1,0:T(8,128)}, f32[4,16,256]{2,1,0:T(8,128)}, f32[2,8,128]{2,1,0:T(8,128)}) custom-call(f32[5,32,512]{2,1,0:T(8,128)S(1)} %constant_dynamic-slice_fusion.2.first, f32[3,32,512]{2,1,0:T(8,128)S(1)} %constant_dynamic-slice_fusion.1.last, f32[112,384]{1,0:T(8,128)S(1)} %get-tuple-element.28.fine_ref, ...), custom_call_target="tpu_custom_call" | custom-call | flops 200000000 | bytes 2126848 | tf_op jit(solution)/shard_map/pallas_call | solution.py:497
  (3 shorter events, 0.1 us)
Async XLA Ops:
  0.6 1.0 %copy-start = (f32[8,32,512]{2,1,0:T(8,128)S(1)}, f32[8,32,512]{2,1,0:T(8,128)}, u32[]{:S(2)}) copy-start(f32[8,32,512]{2,1,0:T(8,128)} %param.6) | copy-start | bytes 1572868
  1.7 2.2 %collective-permute-start = (f32[8,32,128]{2,1,0:T(8,128)S(1)}, f32[8,32,128]{2,1,0:T(8,128)S(1)}, u32[]{:S(2)}, u32[]{:S(2)}) collective-permute-start(f32[8,32,128]{2,1,0:T(8,128)S(1)} %constant_dynamic-slice_fusion), channel_id=1, source_target_pairs={{0,1},{1,0},{2,3},{3,2},{4,5},{5,4},{6,7},{7,6},{8,9},{9,8},{10,11... | collective-permute-start | bytes 393224 | tf_op jit(solution)/shard_map/ppermute | solution.py:491
  2.3 17.2 %copy-start.1 = (bf16[384,512]{1,0:T(8,128)(2,1)S(1)}, bf16[384,512]{1,0:T(8,128)(2,1)}, u32[]{:S(2)}) copy-start(bf16[384,512]{1,0:T(8,128)(2,1)} %constant.22.clone.refs_3_) | copy-start | bytes 1179652
  2.3 17.2 %copy-start.2 = (bf16[256,256]{1,0:T(8,128)(2,1)S(1)}, bf16[256,256]{1,0:T(8,128)(2,1)}, u32[]{:S(2)}) copy-start(bf16[256,256]{1,0:T(8,128)(2,1)} %constant.24.clone.refs_5_) | copy-start | bytes 393220
  2.3 17.2 %copy-start.3 = (bf16[256,112]{1,0:T(8,128)(2,1)S(1)}, bf16[256,112]{1,0:T(8,128)(2,1)}, u32[]{:S(2)}) copy-start(bf16[256,112]{1,0:T(8,128)(2,1)} %constant.23.clone.refs_4_) | copy-start | bytes 172036
  2.3 17.2 %copy-start.4 = (bf16[64,40]{1,0:T(8,128)(2,1)S(1)}, bf16[64,40]{1,0:T(8,128)(2,1)}, u32[]{:S(2)}) copy-start(bf16[64,40]{1,0:T(8,128)(2,1)} %constant.25.clone.refs_6_) | copy-start | bytes 15364
  4.5 5.1 %collective-permute-start.1 = (f32[112,128]{1,0:T(8,128)S(1)}, f32[112,128]{1,0:T(8,128)S(1)}, u32[]{:S(2)}, u32[]{:S(2)}) collective-permute-start(f32[112,128]{1,0:T(8,128)S(1)} %get-tuple-element.27), channel_id=1, source_target_pairs={{0,2},{2,0},{1,3},{3,1},{4,6},{6,4},{5,7},{7,5},{8,10},{10,8},{9,1... | collective-permute-start | bytes 172040 | tf_op jit(solution)/shard_map/ppermute | solution.py:491
  10.1 9.4 %collective-permute-start.2 = (f32[192,128]{1,0:T(8,128)S(1)}, f32[192,128]{1,0:T(8,128)S(1)}, u32[]{:S(2)}, u32[]{:S(2)}) collective-permute-start(f32[192,128]{1,0:T(8,128)S(1)} %get-tuple-element.30), channel_id=1, source_target_pairs={{0,4},{4,8},{8,12},{12,0},{1,5},{5,9},{9,13},{13,1},{2,6},{6,10},{... | collective-permute-start | bytes 294920 | tf_op jit(solution)/shard_map/ppermute | solution.py:491
  12.0 7.5 %collective-permute-start.4 = (f32[160,128]{1,0:T(8,128)S(1)}, f32[160,128]{1,0:T(8,128)S(1)}, u32[]{:S(2)}, u32[]{:S(2)}) collective-permute-start(f32[160,128]{1,0:T(8,128)S(1)} %get-tuple-element.32), channel_id=1, source_target_pairs={{0,12},{4,0},{8,4},{12,8},{1,13},{5,1},{9,5},{13,9},{2,14},{6,2},{... | collective-permute-start | bytes 245768 | tf_op jit(solution)/shard_map/ppermute | solution.py:491
  14.1 5.4 %collective-permute-start.3 = (f32[48,128]{1,0:T(8,128)S(1)}, f32[48,128]{1,0:T(8,128)S(1)}, u32[]{:S(2)}, u32[]{:S(2)}) collective-permute-start(f32[48,128]{1,0:T(8,128)S(1)} %get-tuple-element.31), channel_id=1, source_target_pairs={{0,8},{4,12},{8,0},{12,4},{1,9},{5,13},{9,1},{13,5},{2,10},{6,14},... | collective-permute-start | bytes 73736 | tf_op jit(solution)/shard_map/ppermute | solution.py:491

commit v3 on v2

--- a/solution.py
+++ b/solution.py
@@ -111,38 +111,30 @@
     return left, right
 
 
-def side_tables(axis):
+def end_entries(axis):
     n, block = axis.parts, axis.block
-    sides = [0] if n == 2 else [-1, 1]
-    own = block // 2
-    lanes = side_lanes(own)
+    lanes = side_lanes(block // 2)
     out = []
     for t in range(n):
-        pair = [np.concatenate(list(table[t]), 1) for table in (axis.fine, axis.coarse)]
-        tables = []
-        for side in sides:
-            side = side or 1 - 2 * t
-            start = (t + 1) * block if side > 0 else t * block - LANES
-            tables.append(lane_matrix(pair, range(start, start + LANES), lanes[side > 0]))
         difference = []
-        for level, table in enumerate(pair):
+        for level, table in enumerate((axis.fine, axis.coarse)):
             values, stride = taps(level), 2 << level
-            wide = own >> level
-            same = table.copy()
+            wide = block // stride
+            same = np.concatenate(list(table[t]), 1)
             for r in range(wide + 2):
                 for i in range(t * block, (t + 1) * block):
                     k = abs(stride * (t * wide + r - 1) - i)
                     same[r, i] -= values[k] if k < len(values) else 0.0
             difference.append(np.where(abs(same) > 1e-12, same, 0.0))
-        if t == 0:
-            ends = range(0, LANES)
-        else:
-            ends = range((t + 1) * block - LANES, (t + 1) * block)
+        ends = range(0, LANES) if t == 0 else range((t + 1) * block - LANES, (t + 1) * block)
         rest = np.setdiff1d(range(t * block, (t + 1) * block), ends)
         assert not any(d[:, rest].any() for d in difference)
-        tables.append(lane_matrix(difference, ends, lanes[t > 0]))
-        out.append(split(np.concatenate(tables)))
-    return np.stack(out)
+        table = lane_matrix(difference, ends, lanes[t > 0])
+        if t in (0, n - 1):
+            out.append([(int(r), int(c), float(table[r, c])) for r, c in zip(*np.nonzero(table))])
+        else:
+            assert not table.any()
+    return out
 
 
 def touched(blocks):
@@ -168,6 +160,21 @@
         _, _, starts, count = next(p for p in self.parts if p[0] == shift and p[1] == level)
         block = table[(s + shift) % axis.parts, s][starts[s] : starts[s] + count]
         return np.kron(np.eye(self.depth), block)
+
+    def centres(self, axis, shift, level):
+        n, stride, values = axis.parts, 2 << level, taps(level)
+        _, _, starts, count = next(p for p in self.parts if p[0] == shift and p[1] == level)
+        out = []
+        for s in range(n):
+            first = ((s + shift) % n - s) * axis.block + stride * (starts[s] - 1)
+            out.append(first)
+            made = np.zeros((count, axis.block))
+            for r in range(count):
+                for i in range(axis.block):
+                    k = abs(i - first - stride * r)
+                    made[r, i] = values[k] if k < len(values) else 0.0
+            assert abs(np.kron(np.eye(self.depth), made) - self.send(axis, s, shift, level)).max() < 1e-12
+        return out
 
     def place(self, axis, t, shift, level):
         table = (axis.fine, axis.coarse)[level]
@@ -211,6 +218,66 @@
     cut = round_up(len(rest) // 2, 8)
     slots = rest[:cut] + own + rest[cut:]
     return slots + [None] * (-len(slots) % 8), cut, len(own)
+
+
+class Move:
+    def __init__(self, to, pairs):
+        self.to, self.pairs = to, pairs
+
+    def plan(self, matrices, n, kinds, tiles):
+        spans = []
+        for level in range(2):
+            found = {}
+            for s, t in self.to.items():
+                filled = np.zeros(0)
+                for ty in kinds:
+                    rows = (matrices(s, t, ty)[level] != 0).any(1)
+                    filled = rows if not len(filled) else filled | rows
+                at = np.nonzero(filled)[0]
+                if len(at):
+                    found[t] = (int(at[0]) // 8 * 8, round_up(int(at[-1]) + 1, 8), len(filled))
+            count = max((b - a for a, b, _ in found.values()), default=0)
+            starts = [min(found[t][0], found[t][2] - count) if t in found else 0 for t in range(n)]
+            spans.append((count, starts))
+        (self.fine, self.fine_at), (self.coarse, self.coarse_at) = spans
+        self.packing = Packing(self.fine, self.coarse, tiles)
+
+    def rows(self, s, level, of_target):
+        count, starts = ((self.fine, self.fine_at), (self.coarse, self.coarse_at))[level]
+        t = self.to.get(s)
+        whole = of_target(s if t is None else t)
+        part = np.zeros((round_up(count, 16), whole.shape[1]))
+        if t is not None:
+            part[:count] = whole[starts[t] : starts[t] + count]
+        return part
+
+
+def z_moves(zaxis, lanes):
+    n = zaxis.parts
+    need = {
+        (s, t) for s in range(n) for t in range(n) if s != t and (zaxis.fine[t, s].any() or zaxis.coarse[t, s].any())
+    }
+    near = n % 2 == 0 and n >= 4 and lanes > 1
+
+    def pairs(to):
+        out = []
+        for s in range(n):
+            for c in range(lanes):
+                t, d = (to[s], c) if s in to else (s, (c + 1) % lanes)
+                out.append((s * lanes + c, t * lanes + d))
+        return out
+
+    moves = []
+    for shift in reversed(range(1, n)):
+        to = {s: (s + shift) % n for s in range(n)}
+        used = {s: t for s, t in to.items() if (s, t) in need and not (near and abs(s - t) == 1)}
+        if used:
+            moves.append(Move(used, pairs(to)))
+    if near:
+        even = {s: s ^ 1 for s in range(n)}
+        odd = {s: ((s - 1) ^ 1) + 1 for s in range(1, n - 1)}
+        moves += [Move(to, pairs(to)) for to in (even, odd)]
+    return moves[::-1]
 
 
 def slot_matrix(slots, zblock, yblock, side):
@@ -365,12 +432,60 @@
     return [tuple(jnp.concatenate(p, 1) for p in zip(level, rest)) for rest in (first, last)]
 
 
-def own_columns(places, spots, first, last, table, total, wy, wside, sems):
-    send_spot, side_spot = spots
-    copies = [
-        fetch(table, send_spot, choose(places, lax.axis_index("tile")), wy, sems.at[0]),
-        fetch(table, side_spot, lax.axis_index("xt"), wside, sems.at[1]),
-    ]
+def row_matrix(sends, depth, height):
+    blocks = []
+    tile = lax.axis_index("tile")
+    for level, centres, count in sends:
+        shape = (round_up(depth * count, 16), depth * height)
+        row = lax.broadcasted_iota(jnp.int32, shape, 0)
+        z = sum((row >= count * k).astype(jnp.int32) for k in range(1, depth + 1))
+        at = lax.broadcasted_iota(jnp.int32, shape, 1) - height * z
+        distance = jnp.abs(at - choose(centres, tile) - (2 << level) * (row - count * z))
+        inside = (at >= 0) & (at < height) & (z < depth)
+        blocks.append(jnp.where(inside, ladder(distance, taps(level)), 0.0))
+    return jnp.concatenate(blocks, 0)
+
+
+def side_matrix(n_slabs, entries, own):
+    x, n = lax.axis_index("xt"), lax.axis_size("xt")
+    row = lax.broadcasted_iota(jnp.int32, (8, LANES), 0)
+    lane = lax.broadcasted_iota(jnp.int32, (8, LANES), 1)
+    none = jnp.full((8, LANES), -(10**6), jnp.int32)
+    centres = []
+    for side, lanes in enumerate(side_lanes(own)):
+        shift = LANES if side == 0 else -2 * own
+        pair = [none, none]
+        for at, (level, column) in lanes.items():
+            pair[level] = jnp.where(lane == at, (2 << level) * column + shift, pair[level])
+        centres.append(pair)
+    blocks = []
+    for slab in range(n_slabs):
+        right = x == 0 if n_slabs == 1 else slab == 1
+        pair = [jnp.where(right, b, a) for a, b in zip(*centres)]
+        for r in range(LANES // 8):
+            tile = jnp.zeros((8, LANES), f32)
+            if r < 2 or r >= LANES // 8 - 2:
+                for level in range(2):
+                    tile = tile + ladder(jnp.abs(row + 8 * r - pair[level]), taps(level))
+            blocks.append(tile)
+    for r in range(LANES // 8):
+        total = jnp.zeros((8, LANES), f32)
+        for end, part in zip(entries, (0, n - 1)):
+            here = [(i - 8 * r, at, value) for i, at, value in end if i // 8 == r]
+            if here:
+                tile = jnp.zeros((8, LANES), f32)
+                for i, at, value in here:
+                    tile = jnp.where(row * LANES + lane == i * LANES + at, value, tile)
+                total = jnp.where(x == part, tile, total)
+        blocks.append(total)
+    return jnp.concatenate(blocks, 0)
+
+
+def own_columns(sends, n_slabs, entries, first, last, total, wy, wside):
+    depth, height, own = first.shape[0] + last.shape[0], first.shape[1], first.shape[2] // 2
+    for out, matrix in ((wy, row_matrix(sends, depth, height)), (wside, side_matrix(n_slabs, entries, own))):
+        half = matrix.shape[0]
+        out[:half], out[half:] = halves(matrix)
     cells = halves(sections((first, last)))
     width = cells[0].shape[1] // 2
     out = [
@@ -383,8 +498,6 @@
     halo = jnp.where((lane == 1) | (lane == 2), pltpu.roll(a, 3, 1), b)
     total[:, 2 * LANES : 3 * LANES] = jnp.where(lane < 4, halo, 0.0)
     total[:, 3 * LANES :] = jnp.where(lane < 68, a, 0.0) + jnp.where(lane >= 61, b, 0.0)
-    for copy in copies:
-        copy.wait()
 
 
 def over_columns(tiles, plans, total, wy, wside, first, last, *refs):
@@ -438,39 +551,44 @@
     copies[3].wait()
 
 
-def over_rows(plans_in, plans_out, fine_own, coarse_own, fine_ref, coarse_ref, gf, gc, *refs):
+def over_rows(plans_in, moves, fine_own, coarse_own, fine_made, coarse_made, gf, gc, *refs):
     n_in = len(plans_in)
     got, (fine_out, coarse_out, *sent) = refs[:n_in], refs[n_in:]
-    fine, coarse = fine_ref[...], coarse_ref[...]
-    gf, gc = ((g.at[: g.shape[0] // 2], g.at[g.shape[0] // 2 :]) for g in (gf, gc))
+    sums = [fine_made[...], coarse_made[...]]
     at = 0
     for packing, ref in zip(plans_in, got):
-        more, less = packing.load(ref, True)
-        fine = fine + mm3(tuple(g[:, at : at + packing.fine] for g in gf), halves(more))
-        coarse = coarse + mm3(tuple(g[:, at : at + packing.coarse] for g in gc), halves(less))
+        for level, (g, part) in enumerate(zip((gf, gc), packing.load(ref, True))):
+            half, rows = g.shape[0] // 2, part.shape[0]
+            w = g[:half, at : at + rows], g[half:, at : at + rows]
+            sums[level] = sums[level] + mm3(w, halves(part))
         at += LANES
+    fine, coarse = sums
     fine_out[...] = fine[:fine_own]
     coarse_out[...] = coarse[:coarse_own]
     at, also = fine_own, round_up(coarse_own, 16)
-    for packing, out in zip(plans_out, sent):
-        packing.store(out, fine[at : at + packing.fine], coarse[also : also + packing.coarse])
-        at += round_up(packing.fine, 16)
-        also += round_up(packing.coarse, 16)
-
-
-def over_sections(tiles, plans, starts, fine_at, coarse_at, first, last, fine_ref, coarse_ref, *refs):
-    n_in = len(plans)
-    got, (ex, ezy, fx, fzy), (zero_out, one_out, coarse_out, level) = refs[:n_in], refs[n_in : n_in + 4], refs[n_in + 4 :]
+    for move, out in zip(moves, sent):
+        move.packing.store(out, fine[at : at + move.fine], coarse[also : also + move.coarse])
+        at += round_up(move.fine, 16)
+        also += round_up(move.coarse, 16)
+
+
+def over_sections(tiles, moves, fine_at, coarse_at, first, last, fine_ref, coarse_ref, *refs):
+    n_in = len(moves)
+    got, (ex, ezy, fx, fzy), outs = refs[:n_in], refs[n_in : n_in + 4], refs[n_in + 4 :]
+    zero_out, one_out, coarse_out, level, coarse = outs
     level[...] = fine_ref[...]
-    coarse = coarse_ref[...]
-    for packing, start, ref in zip(plans, starts, got):
-        more, less = packing.load(ref)
+    coarse[...] = coarse_ref[...]
+    z = lax.axis_index("sec")
+    for move, ref in zip(moves, got):
+        more, less = move.packing.load(ref)
         if more is not None:
-            level[start : start + packing.fine] += more
-        coarse = coarse + less
+            at = pl.multiple_of(choose(move.fine_at, z), 8)
+            level[pl.ds(at, move.fine)] += more
+        at = pl.multiple_of(choose(move.coarse_at, z), 8)
+        coarse[pl.ds(at, move.coarse)] += less
     wide = halves(mm2_right(halves(level[...]), ex[...]))
     zero_out[...] = (sections((first, last)) - mm2(ezy[...], wide)).reshape(zero_out.shape)
-    narrow = halves(mm2_right(halves(coarse), fx[...]))
+    narrow = halves(mm2_right(halves(coarse[...]), fx[...]))
     start, count = fine_at
     own = level[start : start + count, : tiles * LANES]
     one_out[...] = (own - mm2(fzy[...], narrow)).reshape(one_out.shape)
@@ -508,6 +626,8 @@
 def choose(places, index):
     if list(places) == list(range(len(places))):
         return index
+    if len(set(places)) == 1:
+        return places[0]
     out = jnp.int32(places[0])
     for i, place in enumerate(places):
         out = jnp.where(index == i, jnp.int32(place), out)
@@ -545,23 +665,13 @@
         slabs = [shifted(edge, "xt", 1)]
     else:
         slabs = [shifted(volume[:, :, width - LANES :], "xt", 1), shifted(volume[:, :, :LANES], "xt", -1)]
-    wside = side_tables(xaxis)
 
     rowplan = RowPlan(yaxis, depth)
     row_packs = []
     for shift in yaxis.shifts:
         fine_count, coarse_count = (p[3] for p in rowplan.parts if p[0] == shift)
         row_packs.append(Packing(depth * fine_count, depth * coarse_count, tiles))
-    wys = []
-    for s in range(yaxis.parts):
-        blocks = []
-        for shift in yaxis.shifts:
-            for level in range(2):
-                m = rowplan.send(yaxis, s, shift, level)
-                blocks.append(pad_to(m, round_up(m.shape[0], 16), cells))
-        wys.append(split(np.concatenate(blocks)))
-    kept, send_places = unique([key_of(m) for m in wys])
-    wy = np.stack([wys[s] for s in kept])
+    sends = [(level, rowplan.centres(yaxis, shift, level), count) for shift, level, _, count in rowplan.parts]
 
     fslots, ffirst, fcount = fine_slots(zaxis, yaxis)
     cslots, cfirst, ccount = coarse_slots(zaxis, yaxis)
@@ -577,39 +687,34 @@
             out.append(np.concatenate(blocks, 1))
         return out
 
-    starts, z_packs = [], []
-    for shift in zaxis.shifts:
-        filled = np.zeros(len(fslots), bool)
-        for s in range(zaxis.parts):
-            filled |= (matrices(s, (s + shift) % zaxis.parts, 0)[0] != 0).any(1)
-            filled |= (matrices(s, (s + shift) % zaxis.parts, yaxis.parts - 1)[0] != 0).any(1)
-        at = np.nonzero(filled)[0]
-        start, end = (int(at[0]) // 8 * 8, round_up(int(at[-1]) + 1, 8)) if len(at) else (0, 0)
-        starts.append(start)
-        z_packs.append(Packing(end - start, len(cslots), tiles))
-
-    def z_key(s):
-        to = [(s + k) % zaxis.parts for k in [0] + zaxis.shifts]
-        return key_of(*(table[t, s] * (1 if t >= s else -1) for t in to for table in (zaxis.fine, zaxis.coarse)))
-
     def y_key(t):
         placed = [rowplan.place(yaxis, t, k, level) for k in yaxis.shifts for level in range(2)]
         return key_of(yaxis.fine[t, t], yaxis.coarse[t, t], *placed)
 
+    y_kept, y_places = unique([y_key(t) for t in range(yaxis.parts)])
+    moves = z_moves(zaxis, xaxis.parts)
+    for move in moves:
+        move.plan(matrices, zaxis.parts, y_kept, tiles)
+
+    def z_key(s):
+        out = [key_of(zaxis.fine[s, s], zaxis.coarse[s, s])]
+        for move in moves:
+            t = move.to.get(s)
+            if t is not None:
+                out.append((t > s, move.fine_at[t], move.coarse_at[t], *key_of(zaxis.fine[t, s], zaxis.coarse[t, s])))
+            else:
+                out.append(None)
+        return tuple(out)
+
     z_kept, z_places = unique([z_key(s) for s in range(zaxis.parts)])
-    y_kept, y_places = unique([y_key(t) for t in range(yaxis.parts)])
     gf, gc = [], []
     for s in z_kept:
         for ty in y_kept:
-            fine, coarse = matrices(s, s, ty)
-            fines, coarses = [fine], [pad_to(coarse, round_up(len(cslots), 16), coarse.shape[1])]
-            for shift, start, packing in zip(zaxis.shifts, starts, z_packs):
-                fine, coarse = matrices(s, (s + shift) % zaxis.parts, ty)
-                fine = fine[start : start + packing.fine]
-                fines.append(pad_to(fine, round_up(packing.fine, 16), fine.shape[1]))
-                coarses.append(pad_to(coarse, round_up(packing.coarse, 16), coarse.shape[1]))
-            gf.append(split(np.concatenate(fines)))
-            gc.append(split(np.concatenate(coarses)))
+            for level, out in enumerate((gf, gc)):
+                rows = matrices(s, s, ty)[level]
+                blocks = [pad_to(rows, round_up(rows.shape[0], 16), rows.shape[1])]
+                blocks += [m.rows(s, level, lambda t: matrices(s, t, ty)[level]) for m in moves]
+                out.append(split(np.concatenate(blocks)))
     gf, gc = np.stack(gf), np.stack(gc)
 
     own = width // 2
@@ -626,15 +731,14 @@
 
     n = (tiles + 1 + 1) * LANES
     shape = jax.ShapeDtypeStruct
-    tables = Tables(max(t.shape[-1] for t in (gf, gc, wy)))
-    f_spot, c_spot, send_spot, side_spot = (tables.add(t) for t in (gf, gc, wy, wside))
+    tables = Tables(max(t.shape[-1] for t in (gf, gc)))
+    f_spot, c_spot = (tables.add(t) for t in (gf, gc))
     table = tables.whole()
+    sent_rows = sum(round_up(depth * count, 16) for _, _, count in sends)
     total, wy, wside = call(
-        functools.partial(own_columns, send_places, (send_spot, side_spot)),
-        [shape((cells, n), f32), shape(send_spot[1:], bf16), shape(side_spot[1:], bf16)],
-        [first, last, table],
-        [pltpu.SemaphoreType.DMA((2,))],
-        fetched=1,
+        functools.partial(own_columns, sends, len(slabs), end_entries(xaxis)),
+        [shape((cells, n), f32), shape((2 * sent_rows, cells), bf16), shape((2 * LANES * (len(slabs) + 1), LANES), bf16)],
+        [first, last],
     )
     high, low, *sent = call(
         functools.partial(over_columns, tiles, row_packs),
@@ -656,22 +760,22 @@
         fetched=1,
     )
     fine, coarse, *sent = call(
-        functools.partial(over_rows, row_packs, z_packs, len(fslots), len(cslots)),
+        functools.partial(over_rows, row_packs, moves, len(fslots), len(cslots)),
         [shape((len(fslots), (tiles + 1) * LANES), f32), shape((len(cslots), 2 * LANES), f32)]
-        + [shape((p.rows, LANES), f32) for p in z_packs],
+        + [shape((m.packing.rows, LANES), f32) for m in moves],
         [fine, coarse, gf, gc, *got],
     )
-    got = [shifted(a, "sec", k) for a, k in zip(sent, zaxis.shifts)]
+    got = [lax.ppermute(a, ("sec", "xt"), m.pairs) for a, m in zip(sent, moves)]
     return tuple(
         call(
-            functools.partial(over_sections, tiles, z_packs, starts, (ffirst, fcount), (cfirst, ccount)),
+            functools.partial(over_sections, tiles, moves, (ffirst, fcount), (cfirst, ccount)),
             [
                 shape(volume.shape, f32),
                 shape((depth // 2, height // 2, width // 2), f32),
                 shape((depth // 4, height // 4, width // 4), f32),
             ],
             [first, last, fine, coarse, *got, *constants],
-            [pltpu.VMEM((len(fslots), (tiles + 1) * LANES), f32)],
+            [pltpu.VMEM((len(fslots), (tiles + 1) * LANES), f32), pltpu.VMEM((len(cslots), 2 * LANES), f32)],
         )
     )
 

time: 21.1 us -> 19.6 us (0.929)
  waiting for transfers between devices: 5.3 us -> 3.13 us
  starting transfers between devices: 7.96 us -> 9.41 us
  Pallas kernels: 5.8 us -> 5.1 us
    ppermute x0 -> x4, starting transfers between devices: none -> 6.03 us  [shards(): got = [lax.ppermute(a, ('sec', 'xt'), m.pairs) for a, m in zip(sent, moves)]]
    ppermute x5 -> x2, waiting for transfers between devices: 5.3 us -> 0.64 us  [shifted(): return lax.ppermute(x, axis, [(i, (i + shift) % n) for i in range(n)])]
    ppermute x5 -> x2, starting transfers between devices: 7.96 us -> 3.38 us  [shifted(): return lax.ppermute(x, axis, [(i, (i + shift) % n) for i in range(n)])]
    ppermute x0 -> x4, waiting for transfers between devices: none -> 2.49 us  [shards(): got = [lax.ppermute(a, ('sec', 'xt'), m.pairs) for a, m in zip(sent, moves)]]
    pallas_call x5, Pallas kernels: 5.8 us -> 5.1 us  [call(): pl.pallas_call(body, out_shape=outs, in_specs=[vmem] * (len(args) - fetch...]
  transfers between devices with their start and end apart: 5 -> 6, of which waited for: 2 -> 3; matrix products, arithmetic and copies ran while one was open for 0% -> 0% of each run, Pallas kernels for 16% -> 13%
where the time goes in v3:
time: 19.6 us; the launch traced here: 19.5 us
  starting transfers between devices  9.41 us (48%)
  Pallas kernels  5.1 us (26%)
  waiting for transfers between devices  3.13 us (16%)
  local copies, waits for them, and re-layouts  1.07 us (5%)
  between operations  0.76 us (4%)
    ppermute x4, starting transfers between devices, shards(): got = [lax.ppermute(a, ('sec', 'xt'), m.pairs) for a, m in zip(sent, moves)]  6.03 us
    pallas_call x5, Pallas kernels, call(): pl.pallas_call(body, out_shape=outs, in_specs=[vmem] * (len(args) - fetch...  5.1 us
    ppermute x2, starting transfers between devices, shifted(): return lax.ppermute(x, axis, [(i, (i + shift) % n) for i in range(n)])  3.38 us
    ppermute x4, waiting for transfers between devices, shards(): got = [lax.ppermute(a, ('sec', 'xt'), m.pairs) for a, m in zip(sent, moves)]  2.49 us
    unnamed x10, local copies, waits for them, and re-layouts  1.01 us
    ppermute x2, waiting for transfers between devices, shifted(): return lax.ppermute(x, axis, [(i, (i + shift) % n) for i in range(n)])  0.64 us
  transfers between devices with their start and end apart: 6, of which 3 were waited for; matrix products, arithmetic and copies ran while one was open for 0% of the time, Pallas kernels for 13%

profile of v3, /device:TPU:0, one launch (start us, length us, event | category | flops | bytes accessed | tf_op | source)
XLA Modules:
  0.0 19.5 jit_solution(10387281890666962153)
XLA Ops:
  0.6 0.0 copy-start
  0.6 0.0 copy-start.4
  0.7 0.0 copy-start.2
  0.7 0.0 copy-start.3
  0.7 0.0 copy-start.1
  0.7 1.0 %copy-done = f32[8,32,512]{2,1,0:T(8,128)S(1)} copy-done((f32[8,32,512]{2,1,0:T(8,128)S(1)}, f32[8,32,512]{2,1,0:T(8,128)}, u32[]{:S(2)}) %copy-start) | copy-done | bytes 524312
  1.7 0.5 %collective-permute-start = (f32[8,32,128]{2,1,0:T(8,128)S(1)}, f32[8,32,128]{2,1,0:T(8,128)S(1)}, u32[]{:S(2)}, u32[]{:S(2)}) collective-permute-start(f32[8,32,128]{2,1,0:T(8,128)S(1)} %constant_dynamic-slice_fusion), channel_id=1, source_target_pairs={{0,1},{1,0},{2,3},{3,2},{4,5},{5,4},{6,7},{7,6},{8,9},{9,8},{10,11... | collective-permute-start | bytes 393224 | tf_op jit(solution)/shard_map/ppermute | solution.py:609
  2.3 0.8 %shard_map.85 = (f32[256,512]{1,0:T(8,128)S(1)}, bf16[160,256]{1,0:T(8,128)(2,1)S(1)}, bf16[512,128]{1,0:T(8,128)(2,1)S(1)}) custom-call(f32[5,32,512]{2,1,0:T(8,128)S(1)} %constant_dynamic-slice_fusion.2.first, f32[3,32,512]{2,1,0:T(8,128)S(1)} %constant_dynamic-slice_fusion.1.last), custom_call_target="tpu_custom_call" | custom-call | flops 200000000 | bytes 1261568 | tf_op jit(solution)/shard_map/pallas_call | solution.py:615
  3.0 0.2 collective-permute-done.refs_0_
  3.2 0.7 %shard_map.86 = (bf16[256,512]{1,0:T(8,128)(2,1)S(1)}, bf16[256,512]{1,0:T(8,128)(2,1)S(1)}, f32[112,128]{1,0:T(8,128)S(1)}) custom-call(f32[256,512]{1,0:T(8,128)S(1)} %get-tuple-element.19.total, bf16[160,256]{1,0:T(8,128)(2,1)S(1)} %get-tuple-element.20.wy, bf16[512,128]{1,0:T(8,128)(2,1)S(1)} %get-tuple-element.21.wside, ...), custom_call_target="tpu_custom_call" | custom-call | flops 200000000 | bytes 1974272 | tf_op jit(solution)/shard_map/pallas_call | solution.py:615
  3.9 2.9 %collective-permute-start.1 = (f32[112,128]{1,0:T(8,128)S(1)}, f32[112,128]{1,0:T(8,128)S(1)}, u32[]{:S(2)}, u32[]{:S(2)}) collective-permute-start(f32[112,128]{1,0:T(8,128)S(1)} %get-tuple-element.28), channel_id=1, source_target_pairs={{0,2},{2,0},{1,3},{3,1},{4,6},{6,4},{5,7},{7,5},{8,10},{10,8},{9,1... | collective-permute-start | bytes 172040 | tf_op jit(solution)/shard_map/ppermute | solution.py:609
  6.7 1.7 %shard_map.87 = (f32[272,384]{1,0:T(8,128)S(1)}, f32[192,256]{1,0:T(8,128)S(1)}, bf16[544,128]{1,0:T(8,128)(2,1)S(1)}, bf16[384,128]{1,0:T(8,128)(2,1)S(1)}) custom-call(bf16[256,512]{1,0:T(8,128)(2,1)S(1)} %get-tuple-element.22.high, bf16[256,512]{1,0:T(8,128)(2,1)S(1)} %get-tuple-element.23.low, bf16[7424,384]{1,0:T(8,128)(2,1)} %constant.26.clone.table), custom_call_target="tpu_custom_call" | custom-call | flops 200000000 | bytes 7077888 | tf_op jit(solution)/shard_map/pallas_call | solution.py:615
  8.5 0.5 %collective-permute-done.1.refs_0_ = f32[112,128]{1,0:T(8,128)S(1)} collective-permute-done((f32[112,128]{1,0:T(8,128)S(1)}, f32[112,128]{1,0:T(8,128)S(1)}, u32[]{:S(2)}, u32[]{:S(2)}) %collective-permute-start.1) | collective-permute-done | bytes 57376 | tf_op jit(solution)/shard_map/ppermute | solution.py:609
  9.0 0.5 %shard_map.88 = (f32[112,384]{1,0:T(8,128)S(1)}, f32[40,256]{1,0:T(8,128)S(1)}, f32[192,128]{1,0:T(8,128)S(1)}, f32[192,128]{1,0:T(8,128)S(1)}, f32[40,128]{1,0:T(8,128)S(1)}, /*index=5*/f32[24,128]{1,0:T(8,128)S(1)}) custom-call(f32[272,384]{1,0:T(8,128)S(1)} %get-tuple-element.24.fine_made, f32[192,256]{1,0:T(8,128)S(1)} %get-tuple-element.25.coarse_made, ...), custom_call_target="tpu_custom_call" | custom-call | flops 200000000 | bytes 1351680 | tf_op jit(solution)/shard_map/pallas_call | solution.py:615
  9.5 0.1 collective-permute-start.2
  9.5 3.6 %collective-permute-start.3 = (f32[192,128]{1,0:T(8,128)S(1)}, f32[192,128]{1,0:T(8,128)S(1)}, u32[]{:S(2)}, u32[]{:S(2)}) collective-permute-start(f32[192,128]{1,0:T(8,128)S(1)} %get-tuple-element.32), channel_id=1, source_target_pairs={{0,4},{1,5},{4,0},{5,1},{8,12},{9,13},{12,8},{13,9},{2,6},{3,7},{6... | collective-permute-start | bytes 294920 | tf_op jit(solution)/shard_map/ppermute | solution.py:768
  13.1 1.1 %collective-permute-start.4 = (f32[40,128]{1,0:T(8,128)S(1)}, f32[40,128]{1,0:T(8,128)S(1)}, u32[]{:S(2)}, u32[]{:S(2)}) collective-permute-start(f32[40,128]{1,0:T(8,128)S(1)} %get-tuple-element.33), channel_id=1, source_target_pairs={{0,8},{1,9},{4,12},{5,13},{8,0},{9,1},{12,4},{13,5},{2,10},{3,11},... | collective-permute-start | bytes 61448 | tf_op jit(solution)/shard_map/ppermute | solution.py:768
  14.2 1.3 %collective-permute-start.5 = (f32[24,128]{1,0:T(8,128)S(1)}, f32[24,128]{1,0:T(8,128)S(1)}, u32[]{:S(2)}, u32[]{:S(2)}) collective-permute-start(f32[24,128]{1,0:T(8,128)S(1)} %get-tuple-element.34), channel_id=1, source_target_pairs={{0,12},{1,13},{4,0},{5,1},{8,4},{9,5},{12,8},{13,9},{2,14},{3,15},... | collective-permute-start | bytes 36872 | tf_op jit(solution)/shard_map/ppermute | solution.py:768
  15.5 2.5 %collective-permute-done.5.refs_3_ = f32[24,128]{1,0:T(8,128)S(1)} collective-permute-done((f32[24,128]{1,0:T(8,128)S(1)}, f32[24,128]{1,0:T(8,128)S(1)}, u32[]{:S(2)}, u32[]{:S(2)}) %collective-permute-start.5) | collective-permute-done | bytes 12320 | tf_op jit(solution)/shard_map/ppermute | solution.py:768
  18.0 0.0 collective-permute-done.4.refs_2_
  18.0 0.0 collective-permute-done.2.refs_0_
  18.0 0.0 collective-permute-done.3.refs_1_
  18.0 0.0 copy-done.4
  18.0 0.0 copy-done.2
  18.0 0.0 copy-done.3
  18.0 0.0 copy-done.1
  18.0 1.4 %shard_map.89 = (f32[8,32,512]{2,1,0:T(8,128)}, f32[4,16,256]{2,1,0:T(8,128)}, f32[2,8,128]{2,1,0:T(8,128)}) custom-call(f32[5,32,512]{2,1,0:T(8,128)S(1)} %constant_dynamic-slice_fusion.2.first, f32[3,32,512]{2,1,0:T(8,128)S(1)} %constant_dynamic-slice_fusion.1.last, f32[112,384]{1,0:T(8,128)S(1)} %get-tuple-element.29.fine_ref, ...), custom_call_target="tpu_custom_call" | custom-call | flops 200000000 | bytes 2151424 | tf_op jit(solution)/shard_map/pallas_call | solution.py:615
  (3 shorter events, 0.1 us)
Async XLA Ops:
  0.6 1.0 %copy-start = (f32[8,32,512]{2,1,0:T(8,128)S(1)}, f32[8,32,512]{2,1,0:T(8,128)}, u32[]{:S(2)}) copy-start(f32[8,32,512]{2,1,0:T(8,128)} %param.6) | copy-start | bytes 1572868
  0.6 17.4 %copy-start.4 = (bf16[64,40]{1,0:T(8,128)(2,1)S(1)}, bf16[64,40]{1,0:T(8,128)(2,1)}, u32[]{:S(2)}) copy-start(bf16[64,40]{1,0:T(8,128)(2,1)} %constant.25.clone.refs_7_) | copy-start | bytes 15364
  0.7 17.3 %copy-start.2 = (bf16[256,256]{1,0:T(8,128)(2,1)S(1)}, bf16[256,256]{1,0:T(8,128)(2,1)}, u32[]{:S(2)}) copy-start(bf16[256,256]{1,0:T(8,128)(2,1)} %constant.24.clone.refs_6_) | copy-start | bytes 393220
  0.7 17.3 %copy-start.3 = (bf16[256,112]{1,0:T(8,128)(2,1)S(1)}, bf16[256,112]{1,0:T(8,128)(2,1)}, u32[]{:S(2)}) copy-start(bf16[256,112]{1,0:T(8,128)(2,1)} %constant.23.clone.refs_5_) | copy-start | bytes 172036
  0.7 17.3 %copy-start.1 = (bf16[384,512]{1,0:T(8,128)(2,1)S(1)}, bf16[384,512]{1,0:T(8,128)(2,1)}, u32[]{:S(2)}) copy-start(bf16[384,512]{1,0:T(8,128)(2,1)} %constant.22.clone.refs_4_) | copy-start | bytes 1179652
  1.7 1.5 %collective-permute-start = (f32[8,32,128]{2,1,0:T(8,128)S(1)}, f32[8,32,128]{2,1,0:T(8,128)S(1)}, u32[]{:S(2)}, u32[]{:S(2)}) collective-permute-start(f32[8,32,128]{2,1,0:T(8,128)S(1)} %constant_dynamic-slice_fusion), channel_id=1, source_target_pairs={{0,1},{1,0},{2,3},{3,2},{4,5},{5,4},{6,7},{7,6},{8,9},{9,8},{10,11... | collective-permute-start | bytes 393224 | tf_op jit(solution)/shard_map/ppermute | solution.py:609
  3.9 5.1 %collective-permute-start.1 = (f32[112,128]{1,0:T(8,128)S(1)}, f32[112,128]{1,0:T(8,128)S(1)}, u32[]{:S(2)}, u32[]{:S(2)}) collective-permute-start(f32[112,128]{1,0:T(8,128)S(1)} %get-tuple-element.28), channel_id=1, source_target_pairs={{0,2},{2,0},{1,3},{3,1},{4,6},{6,4},{5,7},{7,5},{8,10},{10,8},{9,1... | collective-permute-start | bytes 172040 | tf_op jit(solution)/shard_map/ppermute | solution.py:609
  9.5 8.5 %collective-permute-start.2 = (f32[192,128]{1,0:T(8,128)S(1)}, f32[192,128]{1,0:T(8,128)S(1)}, u32[]{:S(2)}, u32[]{:S(2)}) collective-permute-start(f32[192,128]{1,0:T(8,128)S(1)} %get-tuple-element.31), channel_id=1, source_target_pairs={{0,1},{1,0},{4,8},{5,9},{8,4},{9,5},{12,13},{13,12},{2,3},{3,2},{6... | collective-permute-start | bytes 294920 | tf_op jit(solution)/shard_map/ppermute | solution.py:768
  9.5 8.5 %collective-permute-start.3 = (f32[192,128]{1,0:T(8,128)S(1)}, f32[192,128]{1,0:T(8,128)S(1)}, u32[]{:S(2)}, u32[]{:S(2)}) collective-permute-start(f32[192,128]{1,0:T(8,128)S(1)} %get-tuple-element.32), channel_id=1, source_target_pairs={{0,4},{1,5},{4,0},{5,1},{8,12},{9,13},{12,8},{13,9},{2,6},{3,7},{6... | collective-permute-start | bytes 294920 | tf_op jit(solution)/shard_map/ppermute | solution.py:768
  13.1 4.8 %collective-permute-start.4 = (f32[40,128]{1,0:T(8,128)S(1)}, f32[40,128]{1,0:T(8,128)S(1)}, u32[]{:S(2)}, u32[]{:S(2)}) collective-permute-start(f32[40,128]{1,0:T(8,128)S(1)} %get-tuple-element.33), channel_id=1, source_target_pairs={{0,8},{1,9},{4,12},{5,13},{8,0},{9,1},{12,4},{13,5},{2,10},{3,11},... | collective-permute-start | bytes 61448 | tf_op jit(solution)/shard_map/ppermute | solution.py:768
  14.2 3.7 %collective-permute-start.5 = (f32[24,128]{1,0:T(8,128)S(1)}, f32[24,128]{1,0:T(8,128)S(1)}, u32[]{:S(2)}, u32[]{:S(2)}) collective-permute-start(f32[24,128]{1,0:T(8,128)S(1)} %get-tuple-element.34), channel_id=1, source_target_pairs={{0,12},{1,13},{4,0},{5,1},{8,4},{9,5},{12,8},{13,9},{2,14},{3,15},... | collective-permute-start | bytes 36872 | tf_op jit(solution)/shard_map/ppermute | solution.py:768

commit v4 on v3

--- a/solution.py
+++ b/solution.py
@@ -481,36 +481,47 @@
     return jnp.concatenate(blocks, 0)
 
 
-def own_columns(sends, n_slabs, entries, first, last, total, wy, wside):
-    depth, height, own = first.shape[0] + last.shape[0], first.shape[1], first.shape[2] // 2
+def inner_matrices(sends, n_slabs, entries, depth, height, own, wx, wy, wside):
+    for c, pair in enumerate(chunk_matrices(own)):
+        wx[2 * c], wx[2 * c + 1] = pair
     for out, matrix in ((wy, row_matrix(sends, depth, height)), (wside, side_matrix(n_slabs, entries, own))):
         half = matrix.shape[0]
         out[:half], out[half:] = halves(matrix)
+
+
+def halved(ref):
+    half = ref.shape[0] // 2
+    return ref[:half], ref[half:]
+
+
+def own_columns(tiles, first, last, wx, wy, total, fine, coarse):
     cells = halves(sections((first, last)))
     width = cells[0].shape[1] // 2
-    out = [
-        mm3(tuple(p[:, c * width : (c + 1) * width] for p in cells), w) for c, w in enumerate(chunk_matrices(width))
-    ]
+    out = []
+    for c in range(2):
+        out.append(mm3(tuple(p[:, c * width : (c + 1) * width] for p in cells), (wx[2 * c], wx[2 * c + 1])))
     a, b = (part[:, LANES:] for part in out)
     lane = lax.broadcasted_iota(jnp.int32, a.shape, 1)
-    total[:, :LANES] = out[0][:, :LANES] + jnp.where(lane >= LANES - 2, pltpu.roll(b, LANES - 58, 1), 0.0)
-    total[:, LANES : 2 * LANES] = out[1][:, :LANES] + jnp.where(lane < 3, pltpu.roll(a, LANES - 68, 1), 0.0)
     halo = jnp.where((lane == 1) | (lane == 2), pltpu.roll(a, 3, 1), b)
-    total[:, 2 * LANES : 3 * LANES] = jnp.where(lane < 4, halo, 0.0)
-    total[:, 3 * LANES :] = jnp.where(lane < 68, a, 0.0) + jnp.where(lane >= 61, b, 0.0)
-
-
-def over_columns(tiles, plans, total, wy, wside, first, last, *refs):
-    n_slabs = wside.shape[0] // 2 // LANES - 1
-    slabs, (high, low, *sent) = refs[:n_slabs], refs[n_slabs:]
-    at = pl.multiple_of(jnp.where(lax.axis_index("xt") == 0, 0, first.shape[2] - LANES), LANES)
-    ends = [p[:, :, pl.ds(at, LANES)].reshape(-1, LANES) for p in (first, last)]
-    edge = jnp.concatenate([p[...].reshape(-1, LANES) for p in slabs] + [jnp.concatenate(ends, 0)], 1)
-    half = wside.shape[0] // 2
-    side = mm3(halves(edge), (wside[:half], wside[half:]))
+    sums = jnp.concatenate(
+        [
+            out[0][:, :LANES] + jnp.where(lane >= LANES - 2, pltpu.roll(b, LANES - 58, 1), 0.0),
+            out[1][:, :LANES] + jnp.where(lane < 3, pltpu.roll(a, LANES - 68, 1), 0.0),
+            jnp.where(lane < 4, halo, 0.0),
+            jnp.where(lane < 68, a, 0.0) + jnp.where(lane >= 61, b, 0.0),
+        ],
+        1,
+    )
+    total[...] = sums
+    rows = mm3(halved(wy), halves(sums))
+    fine[...] = rows[:, : (tiles + 1) * LANES]
+    coarse[...] = rows[:, tiles * LANES :]
+
+
+def scatter(side):
     lane = lax.broadcasted_iota(jnp.int32, side.shape, 1)
     level, halo = pltpu.roll(side, LANES // 2, 1), pltpu.roll(side, LANES - 32, 1)
-    total = total[...] + jnp.concatenate(
+    return jnp.concatenate(
         [
             jnp.where(lane < 3, level, 0.0),
             jnp.where(lane >= LANES - 2, level, 0.0),
@@ -519,34 +530,44 @@
         ],
         1,
     )
-    x = halves(total)
-    high[...], low[...] = x
-    level_end = (tiles + 1) * LANES
-    at, half = 0, wy.shape[0] // 2
+
+
+def side_columns(first, last, slabs):
+    at = pl.multiple_of(jnp.where(lax.axis_index("xt") == 0, 0, first.shape[2] - LANES), LANES)
+    ends = [p[:, :, pl.ds(at, LANES)].reshape(-1, LANES) for p in (first, last)]
+    return halves(jnp.concatenate([p[...].reshape(-1, LANES) for p in slabs] + [jnp.concatenate(ends, 0)], 1))
+
+
+def over_columns(tiles, plans, fine_ref, coarse_ref, wy, wside, first, last, *refs):
+    n_slabs = wside.shape[0] // 2 // LANES - 1
+    slabs, sent = refs[:n_slabs], refs[n_slabs:]
+    rows = mm3(halved(wy), side_columns(first, last, slabs))
+    rows = scatter(mm3(halves(rows), halved(wside)))
+    fine = fine_ref[...] + rows[:, : (tiles + 1) * LANES]
+    coarse = coarse_ref[...] + rows[:, tiles * LANES :]
+    at = 0
     for packing, out in zip(plans, sent):
-        rows, more = round_up(packing.fine, 16), round_up(packing.coarse, 16)
-        fine = mm3((wy[at : at + rows], wy[half + at : half + at + rows]), tuple(p[:, :level_end] for p in x))
-        at += rows
-        coarse = mm3((wy[at : at + more], wy[half + at : half + at + more]), tuple(p[:, level_end - LANES :] for p in x))
-        at += more
-        packing.store(out, fine[: packing.fine], coarse[: packing.coarse])
-
-
-def own_rows(tiles, places, spots, high, low, table, fine, coarse, gf_got, gc_got, gf, gc, sems):
+        also = at + round_up(packing.fine, 16)
+        packing.store(out, fine[at : at + packing.fine], coarse[also : also + packing.coarse])
+        at = also + round_up(packing.coarse, 16)
+
+
+def own_rows(tiles, places, spots, total, wside, first, last, *refs):
+    n_slabs = wside.shape[0] // 2 // LANES - 1
+    slabs, (table, fine, coarse, gf_got, gc_got, gf, gc, sems) = refs[:n_slabs], refs[n_slabs:]
     z_places, y_places = places
     place = choose(z_places, lax.axis_index("sec")) * (max(y_places) + 1) + choose(y_places, lax.axis_index("tile"))
-    cells = high.shape[0]
+    cells = total.shape[0]
     copies = []
     for i, (spot, own, got) in enumerate(zip(spots, (gf, gc), (gf_got, gc_got))):
         copies.append(fetch(table, spot, place, own, sems.at[2 * i]))
         copies.append(fetch(table, spot, place, got, sems.at[2 * i + 1], cells))
-    level_end = (tiles + 1) * LANES
+    side = mm3(side_columns(first, last, slabs), halved(wside))
+    x = halves(total[...] + scatter(side))
     copies[0].wait()
-    half = gf.shape[0] // 2
-    fine[...] = mm3((gf[:half], gf[half:]), (high[:, :level_end], low[:, :level_end]))
+    fine[...] = mm3(halved(gf), tuple(p[:, : (tiles + 1) * LANES] for p in x))
     copies[2].wait()
-    half = gc.shape[0] // 2
-    coarse[...] = mm3((gc[:half], gc[half:]), (high[:, level_end - LANES :], low[:, level_end - LANES :]))
+    coarse[...] = mm3(halved(gc), tuple(p[:, tiles * LANES :] for p in x))
     copies[1].wait()
     copies[3].wait()
 
@@ -735,15 +756,22 @@
     f_spot, c_spot = (tables.add(t) for t in (gf, gc))
     table = tables.whole()
     sent_rows = sum(round_up(depth * count, 16) for _, _, count in sends)
-    total, wy, wside = call(
-        functools.partial(own_columns, sends, len(slabs), end_entries(xaxis)),
-        [shape((cells, n), f32), shape((2 * sent_rows, cells), bf16), shape((2 * LANES * (len(slabs) + 1), LANES), bf16)],
-        [first, last],
+    own = width // 2
+    wx, wy, wside = call(
+        functools.partial(inner_matrices, sends, len(slabs), end_entries(xaxis), depth, height, own),
+        [shape((4, own, 2 * LANES), bf16), shape((2 * sent_rows, cells), bf16)]
+        + [shape((2 * LANES * (len(slabs) + 1), LANES), bf16)],
+        [],
     )
-    high, low, *sent = call(
+    total, fine, coarse = call(
+        functools.partial(own_columns, tiles),
+        [shape((cells, n), f32), shape((sent_rows, (tiles + 1) * LANES), f32), shape((sent_rows, 2 * LANES), f32)],
+        [first, last, wx, wy],
+    )
+    sent = call(
         functools.partial(over_columns, tiles, row_packs),
-        [shape((cells, n), bf16)] * 2 + [shape((p.rows, LANES), f32) for p in row_packs],
-        [total, wy, wside, first, last, *slabs],
+        [shape((p.rows, LANES), f32) for p in row_packs],
+        [fine, coarse, wy, wside, first, last, *slabs],
     )
     got = [shifted(a, "tile", k) for a, k in zip(sent, yaxis.shifts)]
     (_, f_rows, f_cols), (_, c_rows, c_cols) = f_spot, c_spot
@@ -755,7 +783,7 @@
             shape((f_rows, f_cols - cells), bf16),
             shape((c_rows, c_cols - cells), bf16),
         ],
-        [high, low, table],
+        [total, wside, first, last, *slabs, table],
         [pltpu.VMEM((f_rows, cells), bf16), pltpu.VMEM((c_rows, cells), bf16), pltpu.SemaphoreType.DMA((4,))],
         fetched=1,
     )

time: 19.6 us -> 19.6 us (level)
  starting transfers between devices: 9.41 us -> 9.1 us
    pallas_call x5 -> x6, Pallas kernels: 5.1 us -> 5.25 us  [call(): pl.pallas_call(body, out_shape=outs, in_specs=[vmem] * (len(args) - fetch...]
  transfers between devices with their start and end apart: 6 -> 6, of which waited for: 3 -> 2; matrix products, arithmetic and copies ran while one was open for 0% -> 0% of each run, Pallas kernels for 13% -> 14%
where the time goes in v4:
time: 19.6 us; the launch traced here: 19.4 us
  starting transfers between devices  9.1 us (46%)
  Pallas kernels  5.25 us (27%)
  waiting for transfers between devices  3.16 us (16%)
  local copies, waits for them, and re-layouts  1.13 us (6%)
  between operations  0.77 us (4%)
    ppermute x4, starting transfers between devices, shards(): got = [lax.ppermute(a, ('sec', 'xt'), m.pairs) for a, m in zip(sent, moves)]  5.85 us
    pallas_call x6, Pallas kernels, call(): pl.pallas_call(body, out_shape=outs, in_specs=[vmem] * (len(args) - fetch...  5.25 us
    ppermute x2, starting transfers between devices, shifted(): return lax.ppermute(x, axis, [(i, (i + shift) % n) for i in range(n)])  3.25 us
    ppermute x4, waiting for transfers between devices, shards(): got = [lax.ppermute(a, ('sec', 'xt'), m.pairs) for a, m in zip(sent, moves)]  2.48 us
    unnamed x10, local copies, waits for them, and re-layouts  1.06 us
    ppermute x2, waiting for transfers between devices, shifted(): return lax.ppermute(x, axis, [(i, (i + shift) % n) for i in range(n)])  0.68 us
  transfers between devices with their start and end apart: 6, of which 2 were waited for; matrix products, arithmetic and copies ran while one was open for 0% of the time, Pallas kernels for 14%

profile of v4, /device:TPU:0, one launch (start us, length us, event | category | flops | bytes accessed | tf_op | source)
XLA Modules:
  0.0 19.4 jit_solution(11061312446192135165)
XLA Ops:
  0.6 0.0 copy-start
  0.6 1.0 %copy-done = f32[8,32,512]{2,1,0:T(8,128)S(1)} copy-done((f32[8,32,512]{2,1,0:T(8,128)S(1)}, f32[8,32,512]{2,1,0:T(8,128)}, u32[]{:S(2)}) %copy-start) | copy-done | bytes 524312
  1.7 0.5 %collective-permute-start = (f32[8,32,128]{2,1,0:T(8,128)S(1)}, f32[8,32,128]{2,1,0:T(8,128)S(1)}, u32[]{:S(2)}, u32[]{:S(2)}) collective-permute-start(f32[8,32,128]{2,1,0:T(8,128)S(1)} %constant_dynamic-slice_fusion), channel_id=1, source_target_pairs={{0,1},{1,0},{2,3},{3,2},{4,5},{5,4},{6,7},{7,6},{8,9},{9,8},{10,11... | collective-permute-start | bytes 393224 | tf_op jit(solution)/shard_map/ppermute | solution.py:630
  2.2 0.3 %shard_map.85 = (bf16[4,256,256]{2,1,0:T(8,128)(2,1)S(1)}, bf16[160,256]{1,0:T(8,128)(2,1)S(1)}, bf16[512,128]{1,0:T(8,128)(2,1)S(1)}) custom-call(), custom_call_target="tpu_custom_call" | custom-call | flops 200000000 | bytes 737280 | tf_op jit(solution)/shard_map/pallas_call | solution.py:636
  2.5 0.0 copy-start.1
  2.6 0.0 copy-start.2
  2.6 0.0 copy-start.3
  2.6 0.0 copy-start.4
  2.7 0.7 %shard_map.86 = (f32[256,512]{1,0:T(8,128)S(1)}, f32[80,384]{1,0:T(8,128)S(1)}, f32[80,256]{1,0:T(8,128)S(1)}) custom-call(f32[5,32,512]{2,1,0:T(8,128)S(1)} %constant_dynamic-slice_fusion.2.first, f32[3,32,512]{2,1,0:T(8,128)S(1)} %constant_dynamic-slice_fusion.1.last, bf16[4,256,256]{2,1,0:T(8,128)(2,1)S(1)} %get-tuple-element.19.wx, ...), custom_call_target="tpu_custom_call" | custom-call | flops 200000000 | bytes 1859584 | tf_op jit(solution)/shard_map/pallas_call | solution.py:636
  3.4 0.0 collective-permute-done.refs_0_
  3.4 0.6 %shard_map.88 = f32[112,128]{1,0:T(8,128)S(1)} custom-call(f32[80,384]{1,0:T(8,128)S(1)} %get-tuple-element.27.fine_ref, f32[80,256]{1,0:T(8,128)S(1)} %get-tuple-element.28.coarse_ref, bf16[160,256]{1,0:T(8,128)(2,1)S(1)} %get-tuple-element.20.wy, bf16[512,128]{1,0:T(8,128)(2,1)S(1)} %get-tuple-element.22.wside, ...), custom_call_target="tpu_custom_call" | custom-call | flops 200000000 | bytes 1130496 | tf_op jit(solution)/shard_map/pallas_call | solution.py:636
  3.9 2.7 %collective-permute-start.1 = (f32[112,128]{1,0:T(8,128)S(1)}, f32[112,128]{1,0:T(8,128)S(1)}, u32[]{:S(2)}, u32[]{:S(2)}) collective-permute-start(f32[112,128]{1,0:T(8,128)S(1)} %shard_map.88), channel_id=1, source_target_pairs={{0,2},{2,0},{1,3},{3,1},{4,6},{6,4},{5,7},{7,5},{8,10},{10,8},{9,1... | collective-permute-start | bytes 172040 | tf_op jit(solution)/shard_map/ppermute | solution.py:630
  6.7 1.7 %shard_map.87 = (f32[272,384]{1,0:T(8,128)S(1)}, f32[192,256]{1,0:T(8,128)S(1)}, bf16[544,128]{1,0:T(8,128)(2,1)S(1)}, bf16[384,128]{1,0:T(8,128)(2,1)S(1)}) custom-call(f32[256,512]{1,0:T(8,128)S(1)} %get-tuple-element.21.total, bf16[512,128]{1,0:T(8,128)(2,1)S(1)} %get-tuple-element.22.wside, f32[5,32,512]{2,1,0:T(8,128)S(1)} %constant_dynamic-slice_fusion.2.first, ...), custom_call_target="tpu_custom_call" | custom-call | flops 200000000 | bytes 7864320 | tf_op jit(solution)/shard_map/pallas_call | solution.py:636
  8.4 0.7 %collective-permute-done.1.refs_0_ = f32[112,128]{1,0:T(8,128)S(1)} collective-permute-done((f32[112,128]{1,0:T(8,128)S(1)}, f32[112,128]{1,0:T(8,128)S(1)}, u32[]{:S(2)}, u32[]{:S(2)}) %collective-permute-start.1) | collective-permute-done | bytes 57376 | tf_op jit(solution)/shard_map/ppermute | solution.py:630
  9.1 0.5 %shard_map.89 = (f32[112,384]{1,0:T(8,128)S(1)}, f32[40,256]{1,0:T(8,128)S(1)}, f32[192,128]{1,0:T(8,128)S(1)}, f32[192,128]{1,0:T(8,128)S(1)}, f32[40,128]{1,0:T(8,128)S(1)}, /*index=5*/f32[24,128]{1,0:T(8,128)S(1)}) custom-call(f32[272,384]{1,0:T(8,128)S(1)} %get-tuple-element.23.fine_made, f32[192,256]{1,0:T(8,128)S(1)} %get-tuple-element.24.coarse_made, ...), custom_call_target="tpu_custom_call" | custom-call | flops 200000000 | bytes 1351680 | tf_op jit(solution)/shard_map/pallas_call | solution.py:636
  9.6 0.1 collective-permute-start.2
  9.7 3.4 %collective-permute-start.3 = (f32[192,128]{1,0:T(8,128)S(1)}, f32[192,128]{1,0:T(8,128)S(1)}, u32[]{:S(2)}, u32[]{:S(2)}) collective-permute-start(f32[192,128]{1,0:T(8,128)S(1)} %get-tuple-element.32), channel_id=1, source_target_pairs={{0,4},{1,5},{4,0},{5,1},{8,12},{9,13},{12,8},{13,9},{2,6},{3,7},{6... | collective-permute-start | bytes 294920 | tf_op jit(solution)/shard_map/ppermute | solution.py:796
  13.1 1.1 %collective-permute-start.4 = (f32[40,128]{1,0:T(8,128)S(1)}, f32[40,128]{1,0:T(8,128)S(1)}, u32[]{:S(2)}, u32[]{:S(2)}) collective-permute-start(f32[40,128]{1,0:T(8,128)S(1)} %get-tuple-element.33), channel_id=1, source_target_pairs={{0,8},{1,9},{4,12},{5,13},{8,0},{9,1},{12,4},{13,5},{2,10},{3,11},... | collective-permute-start | bytes 61448 | tf_op jit(solution)/shard_map/ppermute | solution.py:796
  14.2 1.3 %collective-permute-start.5 = (f32[24,128]{1,0:T(8,128)S(1)}, f32[24,128]{1,0:T(8,128)S(1)}, u32[]{:S(2)}, u32[]{:S(2)}) collective-permute-start(f32[24,128]{1,0:T(8,128)S(1)} %get-tuple-element.34), channel_id=1, source_target_pairs={{0,12},{1,13},{4,0},{5,1},{8,4},{9,5},{12,8},{13,9},{2,14},{3,15},... | collective-permute-start | bytes 36872 | tf_op jit(solution)/shard_map/ppermute | solution.py:796
  15.4 2.5 %collective-permute-done.5.refs_3_ = f32[24,128]{1,0:T(8,128)S(1)} collective-permute-done((f32[24,128]{1,0:T(8,128)S(1)}, f32[24,128]{1,0:T(8,128)S(1)}, u32[]{:S(2)}, u32[]{:S(2)}) %collective-permute-start.5) | collective-permute-done | bytes 12320 | tf_op jit(solution)/shard_map/ppermute | solution.py:796
  17.9 0.0 collective-permute-done.4.refs_2_
  17.9 0.0 collective-permute-done.2.refs_0_
  17.9 0.0 collective-permute-done.3.refs_1_
  17.9 0.0 copy-done.1
  17.9 0.0 copy-done.2
  18.0 0.0 copy-done.3
  18.0 0.0 copy-done.4
  18.0 1.4 %shard_map.90 = (f32[8,32,512]{2,1,0:T(8,128)}, f32[4,16,256]{2,1,0:T(8,128)}, f32[2,8,128]{2,1,0:T(8,128)}) custom-call(f32[5,32,512]{2,1,0:T(8,128)S(1)} %constant_dynamic-slice_fusion.2.first, f32[3,32,512]{2,1,0:T(8,128)S(1)} %constant_dynamic-slice_fusion.1.last, f32[112,384]{1,0:T(8,128)S(1)} %get-tuple-element.29.fine_ref, ...), custom_call_target="tpu_custom_call" | custom-call | flops 200000000 | bytes 2151424 | tf_op jit(solution)/shard_map/pallas_call | solution.py:636
  (3 shorter events, 0.1 us)
Async XLA Ops:
  0.6 1.0 %copy-start = (f32[8,32,512]{2,1,0:T(8,128)S(1)}, f32[8,32,512]{2,1,0:T(8,128)}, u32[]{:S(2)}) copy-start(f32[8,32,512]{2,1,0:T(8,128)} %param.6) | copy-start | bytes 1572868
  1.7 1.7 %collective-permute-start = (f32[8,32,128]{2,1,0:T(8,128)S(1)}, f32[8,32,128]{2,1,0:T(8,128)S(1)}, u32[]{:S(2)}, u32[]{:S(2)}) collective-permute-start(f32[8,32,128]{2,1,0:T(8,128)S(1)} %constant_dynamic-slice_fusion), channel_id=1, source_target_pairs={{0,1},{1,0},{2,3},{3,2},{4,5},{5,4},{6,7},{7,6},{8,9},{9,8},{10,11... | collective-permute-start | bytes 393224 | tf_op jit(solution)/shard_map/ppermute | solution.py:630
  2.5 15.4 %copy-start.1 = (bf16[384,512]{1,0:T(8,128)(2,1)S(1)}, bf16[384,512]{1,0:T(8,128)(2,1)}, u32[]{:S(2)}) copy-start(bf16[384,512]{1,0:T(8,128)(2,1)} %constant.22.clone.refs_4_) | copy-start | bytes 1179652
  2.6 15.4 %copy-start.2 = (bf16[256,256]{1,0:T(8,128)(2,1)S(1)}, bf16[256,256]{1,0:T(8,128)(2,1)}, u32[]{:S(2)}) copy-start(bf16[256,256]{1,0:T(8,128)(2,1)} %constant.24.clone.refs_6_) | copy-start | bytes 393220
  2.6 15.4 %copy-start.3 = (bf16[256,112]{1,0:T(8,128)(2,1)S(1)}, bf16[256,112]{1,0:T(8,128)(2,1)}, u32[]{:S(2)}) copy-start(bf16[256,112]{1,0:T(8,128)(2,1)} %constant.23.clone.refs_5_) | copy-start | bytes 172036
  2.6 15.4 %copy-start.4 = (bf16[64,40]{1,0:T(8,128)(2,1)S(1)}, bf16[64,40]{1,0:T(8,128)(2,1)}, u32[]{:S(2)}) copy-start(bf16[64,40]{1,0:T(8,128)(2,1)} %constant.25.clone.refs_7_) | copy-start | bytes 15364
  3.9 5.1 %collective-permute-start.1 = (f32[112,128]{1,0:T(8,128)S(1)}, f32[112,128]{1,0:T(8,128)S(1)}, u32[]{:S(2)}, u32[]{:S(2)}) collective-permute-start(f32[112,128]{1,0:T(8,128)S(1)} %shard_map.88), channel_id=1, source_target_pairs={{0,2},{2,0},{1,3},{3,1},{4,6},{6,4},{5,7},{7,5},{8,10},{10,8},{9,1... | collective-permute-start | bytes 172040 | tf_op jit(solution)/shard_map/ppermute | solution.py:630
  9.6 8.3 %collective-permute-start.2 = (f32[192,128]{1,0:T(8,128)S(1)}, f32[192,128]{1,0:T(8,128)S(1)}, u32[]{:S(2)}, u32[]{:S(2)}) collective-permute-start(f32[192,128]{1,0:T(8,128)S(1)} %get-tuple-element.31), channel_id=1, source_target_pairs={{0,1},{1,0},{4,8},{5,9},{8,4},{9,5},{12,13},{13,12},{2,3},{3,2},{6... | collective-permute-start | bytes 294920 | tf_op jit(solution)/shard_map/ppermute | solution.py:796
  9.7 8.3 %collective-permute-start.3 = (f32[192,128]{1,0:T(8,128)S(1)}, f32[192,128]{1,0:T(8,128)S(1)}, u32[]{:S(2)}, u32[]{:S(2)}) collective-permute-start(f32[192,128]{1,0:T(8,128)S(1)} %get-tuple-element.32), channel_id=1, source_target_pairs={{0,4},{1,5},{4,0},{5,1},{8,12},{9,13},{12,8},{13,9},{2,6},{3,7},{6... | collective-permute-start | bytes 294920 | tf_op jit(solution)/shard_map/ppermute | solution.py:796
  13.1 4.8 %collective-permute-start.4 = (f32[40,128]{1,0:T(8,128)S(1)}, f32[40,128]{1,0:T(8,128)S(1)}, u32[]{:S(2)}, u32[]{:S(2)}) collective-permute-start(f32[40,128]{1,0:T(8,128)S(1)} %get-tuple-element.33), channel_id=1, source_target_pairs={{0,8},{1,9},{4,12},{5,13},{8,0},{9,1},{12,4},{13,5},{2,10},{3,11},... | collective-permute-start | bytes 61448 | tf_op jit(solution)/shard_map/ppermute | solution.py:796
  14.2 3.7 %collective-permute-start.5 = (f32[24,128]{1,0:T(8,128)S(1)}, f32[24,128]{1,0:T(8,128)S(1)}, u32[]{:S(2)}, u32[]{:S(2)}) collective-permute-start(f32[24,128]{1,0:T(8,128)S(1)} %get-tuple-element.34), channel_id=1, source_target_pairs={{0,12},{1,13},{4,0},{5,1},{8,4},{9,5},{12,8},{13,9},{2,14},{3,15},... | collective-permute-start | bytes 36872 | tf_op jit(solution)/shard_map/ppermute | solution.py:796

commit v5 on v4

--- a/solution.py
+++ b/solution.py
@@ -11,6 +11,7 @@
 from jax.sharding import PartitionSpec as P
 
 LANES = 128
+STACK = 128
 f32 = jnp.float32
 bf16 = jnp.bfloat16
 
@@ -73,6 +74,17 @@
     high = matrix.astype(np.float32).astype(ml_dtypes.bfloat16)
     low = (matrix - high.astype(np.float64)).astype(np.float32).astype(ml_dtypes.bfloat16)
     return np.stack([high, low])
+
+
+def stack_columns(matrix, counts):
+    blocks, at = [], 0
+    for count in counts:
+        high, low = split(matrix[:, at : at + count])
+        stacked = np.concatenate([high, high, low], 1)
+        assert stacked.shape[1] <= STACK
+        blocks.append(np.pad(stacked, ((0, 0), (0, STACK - stacked.shape[1]))))
+        at += count
+    return np.concatenate(blocks, 1)[None]
 
 
 def pad_to(matrix, rows, cols):
@@ -217,7 +229,7 @@
     rest = [(z, y, 0) for z in range(depth) for y in range(height) if (z, y, 0) not in own]
     cut = round_up(len(rest) // 2, 8)
     slots = rest[:cut] + own + rest[cut:]
-    return slots + [None] * (-len(slots) % 8), cut, len(own)
+    return slots + [None] * (-len(slots) % 16), cut, len(own)
 
 
 class Move:
@@ -310,10 +322,6 @@
     return mm(a[0], b[0]) + (mm(a[0], b[1]) + mm(a[1], b[0]))
 
 
-def mm2(a, b):
-    return mm(a, b[0]) + mm(a, b[1])
-
-
 def pack(tiles):
     total = tiles[0]
     for j in range(1, len(tiles)):
@@ -376,13 +384,13 @@
         self.lanes, self.blocks, self.count = lanes, [], 0
 
     def add(self, tables):
-        places, two, rows, cols = tables.shape
+        places, parts, rows, cols = tables.shape
         assert rows % 16 == 0 and cols <= self.lanes
-        flat = tables.reshape(places * two * rows, cols)
+        flat = tables.reshape(places * parts * rows, cols)
         self.blocks.append(np.pad(flat, ((0, 0), (0, self.lanes - cols))))
         start = self.count
         self.count += len(flat)
-        return start, two * rows, cols
+        return start, parts * rows, cols
 
     def whole(self):
         return jnp.asarray(np.concatenate(self.blocks))
@@ -557,11 +565,8 @@
     slabs, (table, fine, coarse, gf_got, gc_got, gf, gc, sems) = refs[:n_slabs], refs[n_slabs:]
     z_places, y_places = places
     place = choose(z_places, lax.axis_index("sec")) * (max(y_places) + 1) + choose(y_places, lax.axis_index("tile"))
-    cells = total.shape[0]
-    copies = []
-    for i, (spot, own, got) in enumerate(zip(spots, (gf, gc), (gf_got, gc_got))):
-        copies.append(fetch(table, spot, place, own, sems.at[2 * i]))
-        copies.append(fetch(table, spot, place, got, sems.at[2 * i + 1], cells))
+    outs = (gf, gf_got, gc, gc_got)
+    copies = [fetch(table, spot, place, out, sems.at[i]) for i, (spot, out) in enumerate(zip(spots, outs))]
     side = mm3(side_columns(first, last, slabs), halved(wside))
     x = halves(total[...] + scatter(side))
     copies[0].wait()
@@ -579,10 +584,10 @@
     at = 0
     for packing, ref in zip(plans_in, got):
         for level, (g, part) in enumerate(zip((gf, gc), packing.load(ref, True))):
-            half, rows = g.shape[0] // 2, part.shape[0]
-            w = g[:half, at : at + rows], g[half:, at : at + rows]
-            sums[level] = sums[level] + mm3(w, halves(part))
-        at += LANES
+            high, low = halves(part)
+            stacked = jnp.concatenate([high, low, high], 0)
+            sums[level] = sums[level] + mm(g[:, at : at + stacked.shape[0]], stacked)
+        at += STACK
     fine, coarse = sums
     fine_out[...] = fine[:fine_own]
     coarse_out[...] = coarse[:coarse_own]
@@ -607,18 +612,14 @@
             level[pl.ds(at, move.fine)] += more
         at = pl.multiple_of(choose(move.coarse_at, z), 8)
         coarse[pl.ds(at, move.coarse)] += less
-    wide = halves(mm2_right(halves(level[...]), ex[...]))
-    zero_out[...] = (sections((first, last)) - mm2(ezy[...], wide)).reshape(zero_out.shape)
-    narrow = halves(mm2_right(halves(coarse[...]), fx[...]))
+    wide = jnp.concatenate(halves(mm(jnp.concatenate(halves(level[...]), 1), ex[...])), 0)
+    zero_out[...] = (sections((first, last)) - mm(ezy[...], wide)).reshape(zero_out.shape)
+    narrow = jnp.concatenate(halves(mm(jnp.concatenate(halves(coarse[...]), 1), fx[...])), 0)
     start, count = fine_at
     own = level[start : start + count, : tiles * LANES]
-    one_out[...] = (own - mm2(fzy[...], narrow)).reshape(one_out.shape)
+    one_out[...] = (own - mm(fzy[...], narrow)).reshape(one_out.shape)
     start, count = coarse_at
     coarse_out[...] = coarse[start : start + count, LANES:].reshape(coarse_out.shape)
-
-
-def mm2_right(a, b):
-    return mm(a[0], b) + mm(a[1], b)
 
 
 def cost(flops, moved):
@@ -688,10 +689,10 @@
         slabs = [shifted(volume[:, :, width - LANES :], "xt", 1), shifted(volume[:, :, :LANES], "xt", -1)]
 
     rowplan = RowPlan(yaxis, depth)
-    row_packs = []
+    row_packs, row_counts = [], []
     for shift in yaxis.shifts:
-        fine_count, coarse_count = (p[3] for p in rowplan.parts if p[0] == shift)
-        row_packs.append(Packing(depth * fine_count, depth * coarse_count, tiles))
+        row_counts.append([depth * p[3] for p in rowplan.parts if p[0] == shift])
+        row_packs.append(Packing(*row_counts[-1], tiles))
     sends = [(level, rowplan.centres(yaxis, shift, level), count) for shift, level, _, count in rowplan.parts]
 
     fslots, ffirst, fcount = fine_slots(zaxis, yaxis)
@@ -704,7 +705,7 @@
             blocks = [slot_matrix(slots, zb, (yaxis.fine, yaxis.coarse)[level][ty, ty], t - s)]
             for shift in yaxis.shifts:
                 m = slot_matrix(slots, zb, rowplan.place(yaxis, ty, shift, level), t - s)
-                blocks.append(pad_to(m, len(slots), LANES))
+                blocks.append(m)
             out.append(np.concatenate(blocks, 1))
         return out
 
@@ -728,15 +729,17 @@
         return tuple(out)
 
     z_kept, z_places = unique([z_key(s) for s in range(zaxis.parts)])
-    gf, gc = [], []
+    own_tables, got_tables = ([], []), ([], [])
     for s in z_kept:
         for ty in y_kept:
-            for level, out in enumerate((gf, gc)):
+            for level in range(2):
                 rows = matrices(s, s, ty)[level]
                 blocks = [pad_to(rows, round_up(rows.shape[0], 16), rows.shape[1])]
                 blocks += [m.rows(s, level, lambda t: matrices(s, t, ty)[level]) for m in moves]
-                out.append(split(np.concatenate(blocks)))
-    gf, gc = np.stack(gf), np.stack(gc)
+                rows = np.concatenate(blocks)
+                own_tables[level].append(split(rows[:, :cells]))
+                got_tables[level].append(stack_columns(rows[:, cells:], [p[level] for p in row_counts]))
+    own_tables, got_tables = ([np.stack(t) for t in pair] for pair in (own_tables, got_tables))
 
     own = width // 2
     one = expand(own)
@@ -748,12 +751,14 @@
     fx[HALO[1][0]], fx[HALO[1][1]], fx[LANES:] = one[:, 0], one[:, -1], one[:, 1:-1].T
     ezy = slot_expand(fslots, depth // 2, height // 2)
     fzy = slot_expand(cslots, depth // 4, height // 4)
-    constants = [jnp.asarray(m.astype(ml_dtypes.bfloat16)) for m in (ex, ezy, fx, fzy)]
+    twice = [np.concatenate([m, m], dim) for m, dim in ((ex, 0), (ezy, 1), (fx, 0), (fzy, 1))]
+    constants = [jnp.asarray(m.astype(ml_dtypes.bfloat16)) for m in twice]
 
     n = (tiles + 1 + 1) * LANES
     shape = jax.ShapeDtypeStruct
-    tables = Tables(max(t.shape[-1] for t in (gf, gc)))
-    f_spot, c_spot = (tables.add(t) for t in (gf, gc))
+    every = [t for pair in zip(own_tables, got_tables) for t in pair]
+    tables = Tables(max(t.shape[-1] for t in every))
+    spots = [tables.add(t) for t in every]
     table = tables.whole()
     sent_rows = sum(round_up(depth * count, 16) for _, _, count in sends)
     own = width // 2
@@ -774,17 +779,17 @@
         [fine, coarse, wy, wside, first, last, *slabs],
     )
     got = [shifted(a, "tile", k) for a, k in zip(sent, yaxis.shifts)]
-    (_, f_rows, f_cols), (_, c_rows, c_cols) = f_spot, c_spot
+    f_own, f_got, c_own, c_got = (spot[1:] for spot in spots)
     fine, coarse, gf, gc = call(
-        functools.partial(own_rows, tiles, (z_places, y_places), (f_spot, c_spot)),
+        functools.partial(own_rows, tiles, (z_places, y_places), spots),
         [
-            shape((f_rows // 2, (tiles + 1) * LANES), f32),
-            shape((c_rows // 2, 2 * LANES), f32),
-            shape((f_rows, f_cols - cells), bf16),
-            shape((c_rows, c_cols - cells), bf16),
+            shape((f_got[0], (tiles + 1) * LANES), f32),
+            shape((c_got[0], 2 * LANES), f32),
+            shape(f_got, bf16),
+            shape(c_got, bf16),
         ],
         [total, wside, first, last, *slabs, table],
-        [pltpu.VMEM((f_rows, cells), bf16), pltpu.VMEM((c_rows, cells), bf16), pltpu.SemaphoreType.DMA((4,))],
+        [pltpu.VMEM(f_own, bf16), pltpu.VMEM(c_own, bf16), pltpu.SemaphoreType.DMA((4,))],
         fetched=1,
     )
     fine, coarse, *sent = call(

time: 19.6 us -> 19.4 us (0.990)
  waiting for transfers between devices: 3.16 us -> 2.95 us
    ppermute x2, waiting for transfers between devices: 0.68 us -> 0.47 us  [shifted(): return lax.ppermute(x, axis, [(i, (i + shift) % n) for i in range(n)])]
  transfers between devices with their start and end apart: 6 -> 6, of which waited for: 2 -> 2; matrix products, arithmetic and copies ran while one was open for 0% -> 0% of each run, Pallas kernels for 14% -> 16%
where the time goes in v5:
time: 19.4 us; the launch traced here: 19.2 us
  starting transfers between devices  9.08 us (47%)
  Pallas kernels  5.26 us (27%)
  waiting for transfers between devices  2.95 us (15%)
  local copies, waits for them, and re-layouts  1.13 us (6%)
  between operations  0.78 us (4%)
    ppermute x4, starting transfers between devices, shards(): got = [lax.ppermute(a, ('sec', 'xt'), m.pairs) for a, m in zip(sent, moves)]  5.84 us
    pallas_call x6, Pallas kernels, call(): pl.pallas_call(body, out_shape=outs, in_specs=[vmem] * (len(args) - fetch...  5.26 us
    ppermute x2, starting transfers between devices, shifted(): return lax.ppermute(x, axis, [(i, (i + shift) % n) for i in range(n)])  3.24 us
    ppermute x4, waiting for transfers between devices, shards(): got = [lax.ppermute(a, ('sec', 'xt'), m.pairs) for a, m in zip(sent, moves)]  2.48 us
    unnamed x10, local copies, waits for them, and re-layouts  1.06 us
    ppermute x2, waiting for transfers between devices, shifted(): return lax.ppermute(x, axis, [(i, (i + shift) % n) for i in range(n)])  0.47 us
  transfers between devices with their start and end apart: 6, of which 2 were waited for; matrix products, arithmetic and copies ran while one was open for 0% of the time, Pallas kernels for 16%

profile of v5, /device:TPU:0, one launch (start us, length us, event | category | flops | bytes accessed | tf_op | source)
XLA Modules:
  0.0 19.2 jit_solution(10161676244888884164)
XLA Ops:
  0.6 0.0 copy-start
  0.6 1.0 %copy-done = f32[8,32,512]{2,1,0:T(8,128)S(1)} copy-done((f32[8,32,512]{2,1,0:T(8,128)S(1)}, f32[8,32,512]{2,1,0:T(8,128)}, u32[]{:S(2)}) %copy-start) | copy-done | bytes 524312
  1.7 0.5 %collective-permute-start = (f32[8,32,128]{2,1,0:T(8,128)S(1)}, f32[8,32,128]{2,1,0:T(8,128)S(1)}, u32[]{:S(2)}, u32[]{:S(2)}) collective-permute-start(f32[8,32,128]{2,1,0:T(8,128)S(1)} %constant_dynamic-slice_fusion), channel_id=1, source_target_pairs={{0,1},{1,0},{2,3},{3,2},{4,5},{5,4},{6,7},{7,6},{8,9},{9,8},{10,11... | collective-permute-start | bytes 393224 | tf_op jit(solution)/shard_map/ppermute | solution.py:631
  2.2 0.3 %shard_map.85 = (bf16[4,256,256]{2,1,0:T(8,128)(2,1)S(1)}, bf16[160,256]{1,0:T(8,128)(2,1)S(1)}, bf16[512,128]{1,0:T(8,128)(2,1)S(1)}) custom-call(), custom_call_target="tpu_custom_call" | custom-call | flops 200000000 | bytes 737280 | tf_op jit(solution)/shard_map/pallas_call | solution.py:637
  2.5 0.0 copy-start.1
  2.6 0.0 copy-start.2
  2.6 0.0 copy-start.3
  2.6 0.0 copy-start.4
  2.7 0.7 %shard_map.86 = (f32[256,512]{1,0:T(8,128)S(1)}, f32[80,384]{1,0:T(8,128)S(1)}, f32[80,256]{1,0:T(8,128)S(1)}) custom-call(f32[5,32,512]{2,1,0:T(8,128)S(1)} %constant_dynamic-slice_fusion.2.first, f32[3,32,512]{2,1,0:T(8,128)S(1)} %constant_dynamic-slice_fusion.1.last, bf16[4,256,256]{2,1,0:T(8,128)(2,1)S(1)} %get-tuple-element.19.wx, ...), custom_call_target="tpu_custom_call" | custom-call | flops 200000000 | bytes 1859584 | tf_op jit(solution)/shard_map/pallas_call | solution.py:637
  3.4 0.0 collective-permute-done.refs_0_
  3.4 0.6 %shard_map.88 = f32[112,128]{1,0:T(8,128)S(1)} custom-call(f32[80,384]{1,0:T(8,128)S(1)} %get-tuple-element.27.fine_ref, f32[80,256]{1,0:T(8,128)S(1)} %get-tuple-element.28.coarse_ref, bf16[160,256]{1,0:T(8,128)(2,1)S(1)} %get-tuple-element.20.wy, bf16[512,128]{1,0:T(8,128)(2,1)S(1)} %get-tuple-element.22.wside, ...), custom_call_target="tpu_custom_call" | custom-call | flops 200000000 | bytes 1130496 | tf_op jit(solution)/shard_map/pallas_call | solution.py:637
  4.0 2.7 %collective-permute-start.1 = (f32[112,128]{1,0:T(8,128)S(1)}, f32[112,128]{1,0:T(8,128)S(1)}, u32[]{:S(2)}, u32[]{:S(2)}) collective-permute-start(f32[112,128]{1,0:T(8,128)S(1)} %shard_map.88), channel_id=1, source_target_pairs={{0,2},{2,0},{1,3},{3,1},{4,6},{6,4},{5,7},{7,5},{8,10},{10,8},{9,1... | collective-permute-start | bytes 172040 | tf_op jit(solution)/shard_map/ppermute | solution.py:631
  6.7 1.9 %shard_map.87 = (f32[272,384]{1,0:T(8,128)S(1)}, f32[192,256]{1,0:T(8,128)S(1)}, bf16[272,128]{1,0:T(8,128)(2,1)S(1)}, bf16[192,128]{1,0:T(8,128)(2,1)S(1)}) custom-call(f32[256,512]{1,0:T(8,128)S(1)} %get-tuple-element.21.total, bf16[512,128]{1,0:T(8,128)(2,1)S(1)} %get-tuple-element.22.wside, f32[5,32,512]{2,1,0:T(8,128)S(1)} %constant_dynamic-slice_fusion.2.first, ...), custom_call_target="tpu_custom_call" | custom-call | flops 200000000 | bytes 7745536 | tf_op jit(solution)/shard_map/pallas_call | solution.py:637
  8.6 0.5 %collective-permute-done.1.refs_0_ = f32[112,128]{1,0:T(8,128)S(1)} collective-permute-done((f32[112,128]{1,0:T(8,128)S(1)}, f32[112,128]{1,0:T(8,128)S(1)}, u32[]{:S(2)}, u32[]{:S(2)}) %collective-permute-start.1) | collective-permute-done | bytes 57376 | tf_op jit(solution)/shard_map/ppermute | solution.py:631
  9.1 0.3 %shard_map.89 = (f32[112,384]{1,0:T(8,128)S(1)}, f32[48,256]{1,0:T(8,128)S(1)}, f32[192,128]{1,0:T(8,128)S(1)}, f32[192,128]{1,0:T(8,128)S(1)}, f32[40,128]{1,0:T(8,128)S(1)}, /*index=5*/f32[24,128]{1,0:T(8,128)S(1)}) custom-call(f32[272,384]{1,0:T(8,128)S(1)} %get-tuple-element.23.fine_made, f32[192,256]{1,0:T(8,128)S(1)} %get-tuple-element.24.coarse_made, ...), custom_call_target="tpu_custom_call" | custom-call | flops 200000000 | bytes 1241088 | tf_op jit(solution)/shard_map/pallas_call | solution.py:637
  9.4 0.1 collective-permute-start.2
  9.5 3.4 %collective-permute-start.3 = (f32[192,128]{1,0:T(8,128)S(1)}, f32[192,128]{1,0:T(8,128)S(1)}, u32[]{:S(2)}, u32[]{:S(2)}) collective-permute-start(f32[192,128]{1,0:T(8,128)S(1)} %get-tuple-element.32), channel_id=1, source_target_pairs={{0,4},{1,5},{4,0},{5,1},{8,12},{9,13},{12,8},{13,9},{2,6},{3,7},{6... | collective-permute-start | bytes 294920 | tf_op jit(solution)/shard_map/ppermute | solution.py:801
  12.9 1.1 %collective-permute-start.4 = (f32[40,128]{1,0:T(8,128)S(1)}, f32[40,128]{1,0:T(8,128)S(1)}, u32[]{:S(2)}, u32[]{:S(2)}) collective-permute-start(f32[40,128]{1,0:T(8,128)S(1)} %get-tuple-element.33), channel_id=1, source_target_pairs={{0,8},{1,9},{4,12},{5,13},{8,0},{9,1},{12,4},{13,5},{2,10},{3,11},... | collective-permute-start | bytes 61448 | tf_op jit(solution)/shard_map/ppermute | solution.py:801
  14.0 1.3 %collective-permute-start.5 = (f32[24,128]{1,0:T(8,128)S(1)}, f32[24,128]{1,0:T(8,128)S(1)}, u32[]{:S(2)}, u32[]{:S(2)}) collective-permute-start(f32[24,128]{1,0:T(8,128)S(1)} %get-tuple-element.34), channel_id=1, source_target_pairs={{0,12},{1,13},{4,0},{5,1},{8,4},{9,5},{12,8},{13,9},{2,14},{3,15},... | collective-permute-start | bytes 36872 | tf_op jit(solution)/shard_map/ppermute | solution.py:801
  15.3 2.5 %collective-permute-done.5.refs_3_ = f32[24,128]{1,0:T(8,128)S(1)} collective-permute-done((f32[24,128]{1,0:T(8,128)S(1)}, f32[24,128]{1,0:T(8,128)S(1)}, u32[]{:S(2)}, u32[]{:S(2)}) %collective-permute-start.5) | collective-permute-done | bytes 12320 | tf_op jit(solution)/shard_map/ppermute | solution.py:801
  17.8 0.0 collective-permute-done.4.refs_2_
  17.8 0.0 collective-permute-done.2.refs_0_
  17.8 0.0 collective-permute-done.3.refs_1_
  17.8 0.0 copy-done.1
  17.8 0.0 copy-done.2
  17.8 0.0 copy-done.3
  17.8 0.0 copy-done.4
  17.8 1.4 %shard_map.90 = (f32[8,32,512]{2,1,0:T(8,128)}, f32[4,16,256]{2,1,0:T(8,128)}, f32[2,8,128]{2,1,0:T(8,128)}) custom-call(f32[5,32,512]{2,1,0:T(8,128)S(1)} %constant_dynamic-slice_fusion.2.first, f32[3,32,512]{2,1,0:T(8,128)S(1)} %constant_dynamic-slice_fusion.1.last, f32[112,384]{1,0:T(8,128)S(1)} %get-tuple-element.29.fine_ref, ...), custom_call_target="tpu_custom_call" | custom-call | flops 200000000 | bytes 2748416 | tf_op jit(solution)/shard_map/pallas_call | solution.py:637
  (3 shorter events, 0.1 us)
Async XLA Ops:
  0.6 1.0 %copy-start = (f32[8,32,512]{2,1,0:T(8,128)S(1)}, f32[8,32,512]{2,1,0:T(8,128)}, u32[]{:S(2)}) copy-start(f32[8,32,512]{2,1,0:T(8,128)} %param.6) | copy-start | bytes 1572868
  1.7 1.7 %collective-permute-start = (f32[8,32,128]{2,1,0:T(8,128)S(1)}, f32[8,32,128]{2,1,0:T(8,128)S(1)}, u32[]{:S(2)}, u32[]{:S(2)}) collective-permute-start(f32[8,32,128]{2,1,0:T(8,128)S(1)} %constant_dynamic-slice_fusion), channel_id=1, source_target_pairs={{0,1},{1,0},{2,3},{3,2},{4,5},{5,4},{6,7},{7,6},{8,9},{9,8},{10,11... | collective-permute-start | bytes 393224 | tf_op jit(solution)/shard_map/ppermute | solution.py:631
  2.5 15.2 %copy-start.1 = (bf16[768,512]{1,0:T(8,128)(2,1)S(1)}, bf16[768,512]{1,0:T(8,128)(2,1)}, u32[]{:S(2)}) copy-start(bf16[768,512]{1,0:T(8,128)(2,1)} %constant.22.clone.refs_4_) | copy-start | bytes 2359300
  2.6 15.2 %copy-start.2 = (bf16[512,256]{1,0:T(8,128)(2,1)S(1)}, bf16[512,256]{1,0:T(8,128)(2,1)}, u32[]{:S(2)}) copy-start(bf16[512,256]{1,0:T(8,128)(2,1)} %constant.24.clone.refs_6_) | copy-start | bytes 786436
  2.6 15.2 %copy-start.3 = (bf16[256,224]{1,0:T(8,128)(2,1)S(1)}, bf16[256,224]{1,0:T(8,128)(2,1)}, u32[]{:S(2)}) copy-start(bf16[256,224]{1,0:T(8,128)(2,1)} %constant.23.clone.refs_5_) | copy-start | bytes 344068
  2.6 15.2 %copy-start.4 = (bf16[64,96]{1,0:T(8,128)(2,1)S(1)}, bf16[64,96]{1,0:T(8,128)(2,1)}, u32[]{:S(2)}) copy-start(bf16[64,96]{1,0:T(8,128)(2,1)} %constant.25.clone.refs_7_) | copy-start | bytes 36868
  4.0 5.1 %collective-permute-start.1 = (f32[112,128]{1,0:T(8,128)S(1)}, f32[112,128]{1,0:T(8,128)S(1)}, u32[]{:S(2)}, u32[]{:S(2)}) collective-permute-start(f32[112,128]{1,0:T(8,128)S(1)} %shard_map.88), channel_id=1, source_target_pairs={{0,2},{2,0},{1,3},{3,1},{4,6},{6,4},{5,7},{7,5},{8,10},{10,8},{9,1... | collective-permute-start | bytes 172040 | tf_op jit(solution)/shard_map/ppermute | solution.py:631
  9.4 8.3 %collective-permute-start.2 = (f32[192,128]{1,0:T(8,128)S(1)}, f32[192,128]{1,0:T(8,128)S(1)}, u32[]{:S(2)}, u32[]{:S(2)}) collective-permute-start(f32[192,128]{1,0:T(8,128)S(1)} %get-tuple-element.31), channel_id=1, source_target_pairs={{0,1},{1,0},{4,8},{5,9},{8,4},{9,5},{12,13},{13,12},{2,3},{3,2},{6... | collective-permute-start | bytes 294920 | tf_op jit(solution)/shard_map/ppermute | solution.py:801
  9.5 8.3 %collective-permute-start.3 = (f32[192,128]{1,0:T(8,128)S(1)}, f32[192,128]{1,0:T(8,128)S(1)}, u32[]{:S(2)}, u32[]{:S(2)}) collective-permute-start(f32[192,128]{1,0:T(8,128)S(1)} %get-tuple-element.32), channel_id=1, source_target_pairs={{0,4},{1,5},{4,0},{5,1},{8,12},{9,13},{12,8},{13,9},{2,6},{3,7},{6... | collective-permute-start | bytes 294920 | tf_op jit(solution)/shard_map/ppermute | solution.py:801
  12.9 4.8 %collective-permute-start.4 = (f32[40,128]{1,0:T(8,128)S(1)}, f32[40,128]{1,0:T(8,128)S(1)}, u32[]{:S(2)}, u32[]{:S(2)}) collective-permute-start(f32[40,128]{1,0:T(8,128)S(1)} %get-tuple-element.33), channel_id=1, source_target_pairs={{0,8},{1,9},{4,12},{5,13},{8,0},{9,1},{12,4},{13,5},{2,10},{3,11},... | collective-permute-start | bytes 61448 | tf_op jit(solution)/shard_map/ppermute | solution.py:801
  14.0 3.7 %collective-permute-start.5 = (f32[24,128]{1,0:T(8,128)S(1)}, f32[24,128]{1,0:T(8,128)S(1)}, u32[]{:S(2)}, u32[]{:S(2)}) collective-permute-start(f32[24,128]{1,0:T(8,128)S(1)} %get-tuple-element.34), channel_id=1, source_target_pairs={{0,12},{1,13},{4,0},{5,1},{8,4},{9,5},{12,8},{13,9},{2,14},{3,15},... | collective-permute-start | bytes 36872 | tf_op jit(solution)/shard_map/ppermute | solution.py:801

commit v6 on v5

--- a/solution.py
+++ b/solution.py
@@ -286,6 +286,11 @@
         if used:
             moves.append(Move(used, pairs(to)))
     if near:
+        if n == 4:
+            rounds = [{0: 1, 1: 2, 2: 0}, {3: 2, 2: 1, 1: 3}, {0: 2, 2: 3, 3: 1, 1: 0}]
+            apart = [m for m in moves if abs(m.to.get(0, 0)) == 3]
+            first, *rest = [Move(to, pairs(to)) for to in rounds]
+            return [first, *apart, *rest][::-1]
         even = {s: s ^ 1 for s in range(n)}
         odd = {s: ((s - 1) ^ 1) + 1 for s in range(1, n - 1)}
         moves += [Move(to, pairs(to)) for to in (even, odd)]

time: 19.4 us -> 19.2 us (0.990)
  waiting for transfers between devices: 2.95 us -> 2.32 us
  starting transfers between devices: 9.08 us -> 9.37 us
    ppermute x4, waiting for transfers between devices: 2.48 us -> 2.06 us  [shards(): got = [lax.ppermute(a, ('sec', 'xt'), m.pairs) for a, m in zip(sent, moves)]]
    ppermute x4, starting transfers between devices: 5.84 us -> 6.07 us  [shards(): got = [lax.ppermute(a, ('sec', 'xt'), m.pairs) for a, m in zip(sent, moves)]]
    ppermute x2, waiting for transfers between devices: 0.47 us -> 0.26 us  [shifted(): return lax.ppermute(x, axis, [(i, (i + shift) % n) for i in range(n)])]
where the time goes in v6:
time: 19.2 us; the launch traced here: 19 us
  starting transfers between devices  9.37 us (49%)
  Pallas kernels  5.41 us (28%)
  waiting for transfers between devices  2.32 us (12%)
  local copies, waits for them, and re-layouts  1.13 us (6%)
  between operations  0.74 us (4%)
    ppermute x4, starting transfers between devices, shards(): got = [lax.ppermute(a, ('sec', 'xt'), m.pairs) for a, m in zip(sent, moves)]  6.07 us
    pallas_call x6, Pallas kernels, call(): pl.pallas_call(body, out_shape=outs, in_specs=[vmem] * (len(args) - fetch...  5.41 us
    ppermute x2, starting transfers between devices, shifted(): return lax.ppermute(x, axis, [(i, (i + shift) % n) for i in range(n)])  3.3 us
    ppermute x4, waiting for transfers between devices, shards(): got = [lax.ppermute(a, ('sec', 'xt'), m.pairs) for a, m in zip(sent, moves)]  2.06 us
    unnamed x10, local copies, waits for them, and re-layouts  1.05 us
  transfers between devices with their start and end apart: 6, of which 2 were waited for; matrix products, arithmetic and copies ran while one was open for 0% of the time, Pallas kernels for 16%

profile of v6, /device:TPU:0, one launch (start us, length us, event | category | flops | bytes accessed | tf_op | source)
XLA Modules:
  0.0 19.0 jit_solution(2057606049241314578)
XLA Ops:
  0.6 0.0 copy-start
  0.6 1.0 %copy-done = f32[8,32,512]{2,1,0:T(8,128)S(1)} copy-done((f32[8,32,512]{2,1,0:T(8,128)S(1)}, f32[8,32,512]{2,1,0:T(8,128)}, u32[]{:S(2)}) %copy-start) | copy-done | bytes 524312
  1.7 0.0 copy-start.1
  1.7 0.0 copy-start.2
  1.7 0.0 copy-start.3
  1.7 0.0 copy-start.4
  1.7 0.5 %collective-permute-start = (f32[8,32,128]{2,1,0:T(8,128)S(1)}, f32[8,32,128]{2,1,0:T(8,128)S(1)}, u32[]{:S(2)}, u32[]{:S(2)}) collective-permute-start(f32[8,32,128]{2,1,0:T(8,128)S(1)} %constant_dynamic-slice_fusion), channel_id=1, source_target_pairs={{0,1},{1,0},{2,3},{3,2},{4,5},{5,4},{6,7},{7,6},{8,9},{9,8},{10,11... | collective-permute-start | bytes 393224 | tf_op jit(solution)/shard_map/ppermute | solution.py:636
  2.2 0.3 %shard_map.85 = (bf16[4,256,256]{2,1,0:T(8,128)(2,1)S(1)}, bf16[160,256]{1,0:T(8,128)(2,1)S(1)}, bf16[512,128]{1,0:T(8,128)(2,1)S(1)}) custom-call(), custom_call_target="tpu_custom_call" | custom-call | flops 200000000 | bytes 737280 | tf_op jit(solution)/shard_map/pallas_call | solution.py:642
  2.6 0.7 %shard_map.86 = (f32[256,512]{1,0:T(8,128)S(1)}, f32[80,384]{1,0:T(8,128)S(1)}, f32[80,256]{1,0:T(8,128)S(1)}) custom-call(f32[5,32,512]{2,1,0:T(8,128)S(1)} %constant_dynamic-slice_fusion.2.first, f32[3,32,512]{2,1,0:T(8,128)S(1)} %constant_dynamic-slice_fusion.1.last, bf16[4,256,256]{2,1,0:T(8,128)(2,1)S(1)} %get-tuple-element.19.wx, ...), custom_call_target="tpu_custom_call" | custom-call | flops 200000000 | bytes 1859584 | tf_op jit(solution)/shard_map/pallas_call | solution.py:642
  3.3 0.0 collective-permute-done.refs_0_
  3.3 0.6 %shard_map.88 = f32[112,128]{1,0:T(8,128)S(1)} custom-call(f32[80,384]{1,0:T(8,128)S(1)} %get-tuple-element.27.fine_ref, f32[80,256]{1,0:T(8,128)S(1)} %get-tuple-element.28.coarse_ref, bf16[160,256]{1,0:T(8,128)(2,1)S(1)} %get-tuple-element.20.wy, bf16[512,128]{1,0:T(8,128)(2,1)S(1)} %get-tuple-element.22.wside, ...), custom_call_target="tpu_custom_call" | custom-call | flops 200000000 | bytes 1130496 | tf_op jit(solution)/shard_map/pallas_call | solution.py:642
  3.9 2.8 %collective-permute-start.1 = (f32[112,128]{1,0:T(8,128)S(1)}, f32[112,128]{1,0:T(8,128)S(1)}, u32[]{:S(2)}, u32[]{:S(2)}) collective-permute-start(f32[112,128]{1,0:T(8,128)S(1)} %shard_map.88), channel_id=1, source_target_pairs={{0,2},{2,0},{1,3},{3,1},{4,6},{6,4},{5,7},{7,5},{8,10},{10,8},{9,1... | collective-permute-start | bytes 172040 | tf_op jit(solution)/shard_map/ppermute | solution.py:636
  6.7 2.1 %shard_map.87 = (f32[336,384]{1,0:T(8,128)S(1)}, f32[192,256]{1,0:T(8,128)S(1)}, bf16[336,128]{1,0:T(8,128)(2,1)S(1)}, bf16[192,128]{1,0:T(8,128)(2,1)S(1)}) custom-call(f32[256,512]{1,0:T(8,128)S(1)} %get-tuple-element.21.total, bf16[512,128]{1,0:T(8,128)(2,1)S(1)} %get-tuple-element.22.wside, f32[5,32,512]{2,1,0:T(8,128)S(1)} %constant_dynamic-slice_fusion.2.first, ...), custom_call_target="tpu_custom_call" | custom-call | flops 200000000 | bytes 8646656 | tf_op jit(solution)/shard_map/pallas_call | solution.py:642
  8.8 0.3 %collective-permute-done.1.refs_0_ = f32[112,128]{1,0:T(8,128)S(1)} collective-permute-done((f32[112,128]{1,0:T(8,128)S(1)}, f32[112,128]{1,0:T(8,128)S(1)}, u32[]{:S(2)}, u32[]{:S(2)}) %collective-permute-start.1) | collective-permute-done | bytes 57376 | tf_op jit(solution)/shard_map/ppermute | solution.py:636
  9.1 0.4 %shard_map.89 = (f32[112,384]{1,0:T(8,128)S(1)}, f32[48,256]{1,0:T(8,128)S(1)}, f32[184,128]{1,0:T(8,128)S(1)}, f32[160,128]{1,0:T(8,128)S(1)}, f32[24,128]{1,0:T(8,128)S(1)}, /*index=5*/f32[192,128]{1,0:T(8,128)S(1)}) custom-call(f32[336,384]{1,0:T(8,128)S(1)} %get-tuple-element.23.fine_made, f32[192,256]{1,0:T(8,128)S(1)} %get-tuple-element.24.coarse_made, ...), custom_call_target="tpu_custom_call" | custom-call | flops 200000000 | bytes 1413120 | tf_op jit(solution)/shard_map/pallas_call | solution.py:642
  9.4 2.0 %collective-permute-start.5 = (f32[192,128]{1,0:T(8,128)S(1)}, f32[192,128]{1,0:T(8,128)S(1)}, u32[]{:S(2)}, u32[]{:S(2)}) collective-permute-start(f32[192,128]{1,0:T(8,128)S(1)} %get-tuple-element.34), channel_id=1, source_target_pairs={{0,4},{1,5},{4,8},{5,9},{8,0},{9,1},{12,13},{13,12},{2,6},{3,7},{6... | collective-permute-start | bytes 294920 | tf_op jit(solution)/shard_map/ppermute | solution.py:806
  11.4 1.1 %collective-permute-start.2 = (f32[184,128]{1,0:T(8,128)S(1)}, f32[184,128]{1,0:T(8,128)S(1)}, u32[]{:S(2)}, u32[]{:S(2)}) collective-permute-start(f32[184,128]{1,0:T(8,128)S(1)} %get-tuple-element.31), channel_id=1, source_target_pairs={{0,8},{1,9},{4,0},{5,1},{8,12},{9,13},{12,4},{13,5},{2,10},{3,11},... | collective-permute-start | bytes 282632 | tf_op jit(solution)/shard_map/ppermute | solution.py:806
  12.5 0.0 collective-permute-start.3
  12.5 3.0 %collective-permute-start.4 = (f32[24,128]{1,0:T(8,128)S(1)}, f32[24,128]{1,0:T(8,128)S(1)}, u32[]{:S(2)}, u32[]{:S(2)}) collective-permute-start(f32[24,128]{1,0:T(8,128)S(1)} %get-tuple-element.33), channel_id=1, source_target_pairs={{0,12},{1,13},{4,0},{5,1},{8,4},{9,5},{12,8},{13,9},{2,14},{3,15},... | collective-permute-start | bytes 36872 | tf_op jit(solution)/shard_map/ppermute | solution.py:806
  15.5 2.1 %collective-permute-done.4.refs_2_ = f32[24,128]{1,0:T(8,128)S(1)} collective-permute-done((f32[24,128]{1,0:T(8,128)S(1)}, f32[24,128]{1,0:T(8,128)S(1)}, u32[]{:S(2)}, u32[]{:S(2)}) %collective-permute-start.4) | collective-permute-done | bytes 12320 | tf_op jit(solution)/shard_map/ppermute | solution.py:806
  17.6 0.0 collective-permute-done.3.refs_1_
  17.6 0.0 collective-permute-done.2.refs_0_
  17.6 0.0 collective-permute-done.5.refs_3_
  17.6 0.0 copy-done.1
  17.6 0.0 copy-done.2
  17.6 0.0 copy-done.3
  17.6 0.0 copy-done.4
  17.6 1.4 %shard_map.90 = (f32[8,32,512]{2,1,0:T(8,128)}, f32[4,16,256]{2,1,0:T(8,128)}, f32[2,8,128]{2,1,0:T(8,128)}) custom-call(f32[5,32,512]{2,1,0:T(8,128)S(1)} %constant_dynamic-slice_fusion.2.first, f32[3,32,512]{2,1,0:T(8,128)S(1)} %constant_dynamic-slice_fusion.1.last, f32[112,384]{1,0:T(8,128)S(1)} %get-tuple-element.29.fine_ref, ...), custom_call_target="tpu_custom_call" | custom-call | flops 200000000 | bytes 2805760 | tf_op jit(solution)/shard_map/pallas_call | solution.py:642
  (3 shorter events, 0.1 us)
Async XLA Ops:
  0.6 1.0 %copy-start = (f32[8,32,512]{2,1,0:T(8,128)S(1)}, f32[8,32,512]{2,1,0:T(8,128)}, u32[]{:S(2)}) copy-start(f32[8,32,512]{2,1,0:T(8,128)} %param.6) | copy-start | bytes 1572868
  1.7 15.9 %copy-start.1 = (bf16[768,512]{1,0:T(8,128)(2,1)S(1)}, bf16[768,512]{1,0:T(8,128)(2,1)}, u32[]{:S(2)}) copy-start(bf16[768,512]{1,0:T(8,128)(2,1)} %constant.22.clone.refs_4_) | copy-start | bytes 2359300
  1.7 15.9 %copy-start.2 = (bf16[512,256]{1,0:T(8,128)(2,1)S(1)}, bf16[512,256]{1,0:T(8,128)(2,1)}, u32[]{:S(2)}) copy-start(bf16[512,256]{1,0:T(8,128)(2,1)} %constant.24.clone.refs_6_) | copy-start | bytes 786436
  1.7 15.9 %copy-start.3 = (bf16[256,224]{1,0:T(8,128)(2,1)S(1)}, bf16[256,224]{1,0:T(8,128)(2,1)}, u32[]{:S(2)}) copy-start(bf16[256,224]{1,0:T(8,128)(2,1)} %constant.23.clone.refs_5_) | copy-start | bytes 344068
  1.7 15.9 %copy-start.4 = (bf16[64,96]{1,0:T(8,128)(2,1)S(1)}, bf16[64,96]{1,0:T(8,128)(2,1)}, u32[]{:S(2)}) copy-start(bf16[64,96]{1,0:T(8,128)(2,1)} %constant.25.clone.refs_7_) | copy-start | bytes 36868
  1.7 1.6 %collective-permute-start = (f32[8,32,128]{2,1,0:T(8,128)S(1)}, f32[8,32,128]{2,1,0:T(8,128)S(1)}, u32[]{:S(2)}, u32[]{:S(2)}) collective-permute-start(f32[8,32,128]{2,1,0:T(8,128)S(1)} %constant_dynamic-slice_fusion), channel_id=1, source_target_pairs={{0,1},{1,0},{2,3},{3,2},{4,5},{5,4},{6,7},{7,6},{8,9},{9,8},{10,11... | collective-permute-start | bytes 393224 | tf_op jit(solution)/shard_map/ppermute | solution.py:636
  3.9 5.1 %collective-permute-start.1 = (f32[112,128]{1,0:T(8,128)S(1)}, f32[112,128]{1,0:T(8,128)S(1)}, u32[]{:S(2)}, u32[]{:S(2)}) collective-permute-start(f32[112,128]{1,0:T(8,128)S(1)} %shard_map.88), channel_id=1, source_target_pairs={{0,2},{2,0},{1,3},{3,1},{4,6},{6,4},{5,7},{7,5},{8,10},{10,8},{9,1... | collective-permute-start | bytes 172040 | tf_op jit(solution)/shard_map/ppermute | solution.py:636
  9.4 8.1 %collective-permute-start.5 = (f32[192,128]{1,0:T(8,128)S(1)}, f32[192,128]{1,0:T(8,128)S(1)}, u32[]{:S(2)}, u32[]{:S(2)}) collective-permute-start(f32[192,128]{1,0:T(8,128)S(1)} %get-tuple-element.34), channel_id=1, source_target_pairs={{0,4},{1,5},{4,8},{5,9},{8,0},{9,1},{12,13},{13,12},{2,6},{3,7},{6... | collective-permute-start | bytes 294920 | tf_op jit(solution)/shard_map/ppermute | solution.py:806
  11.4 6.2 %collective-permute-start.2 = (f32[184,128]{1,0:T(8,128)S(1)}, f32[184,128]{1,0:T(8,128)S(1)}, u32[]{:S(2)}, u32[]{:S(2)}) collective-permute-start(f32[184,128]{1,0:T(8,128)S(1)} %get-tuple-element.31), channel_id=1, source_target_pairs={{0,8},{1,9},{4,0},{5,1},{8,12},{9,13},{12,4},{13,5},{2,10},{3,11},... | collective-permute-start | bytes 282632 | tf_op jit(solution)/shard_map/ppermute | solution.py:806
  12.5 5.1 %collective-permute-start.3 = (f32[160,128]{1,0:T(8,128)S(1)}, f32[160,128]{1,0:T(8,128)S(1)}, u32[]{:S(2)}, u32[]{:S(2)}) collective-permute-start(f32[160,128]{1,0:T(8,128)S(1)} %get-tuple-element.32), channel_id=1, source_target_pairs={{0,1},{1,0},{4,12},{5,13},{8,4},{9,5},{12,8},{13,9},{2,3},{3,2},{6... | collective-permute-start | bytes 245768 | tf_op jit(solution)/shard_map/ppermute | solution.py:806
  12.5 5.1 %collective-permute-start.4 = (f32[24,128]{1,0:T(8,128)S(1)}, f32[24,128]{1,0:T(8,128)S(1)}, u32[]{:S(2)}, u32[]{:S(2)}) collective-permute-start(f32[24,128]{1,0:T(8,128)S(1)} %get-tuple-element.33), channel_id=1, source_target_pairs={{0,12},{1,13},{4,0},{5,1},{8,4},{9,5},{12,8},{13,9},{2,14},{3,15},... | collective-permute-start | bytes 36872 | tf_op jit(solution)/shard_map/ppermute | solution.py:806

commit v7 on v6

--- a/solution.py
+++ b/solution.py
@@ -554,8 +554,12 @@
 def over_columns(tiles, plans, fine_ref, coarse_ref, wy, wside, first, last, *refs):
     n_slabs = wside.shape[0] // 2 // LANES - 1
     slabs, sent = refs[:n_slabs], refs[n_slabs:]
-    rows = mm3(halved(wy), side_columns(first, last, slabs))
-    rows = scatter(mm3(halves(rows), halved(wside)))
+    edge, sends = side_columns(first, last, slabs), halved(wy)
+    rows = mm(jnp.concatenate([sends[0], sends[1]], 0), edge[0])
+    rows = rows[: sends[0].shape[0]] + rows[sends[0].shape[0] :] + mm(sends[0], edge[1])
+    parts, w = halves(rows), halved(wside)
+    rows = mm(jnp.concatenate(parts, 0), w[0])
+    rows = scatter(rows[: parts[0].shape[0]] + rows[parts[0].shape[0] :] + mm(parts[0], w[1]))
     fine = fine_ref[...] + rows[:, : (tiles + 1) * LANES]
     coarse = coarse_ref[...] + rows[:, tiles * LANES :]
     at = 0

time: 19.2 us -> 19.1 us (level)
  transfers between devices with their start and end apart: 6 -> 6, of which waited for: 2 -> 2; matrix products, arithmetic and copies ran while one was open for 0% -> 0% of each run, Pallas kernels for 16% -> 17%
where the time goes in v7:
time: 19.1 us; the launch traced here: 18.9 us
  starting transfers between devices  9.36 us (49%)
  Pallas kernels  5.38 us (28%)
  waiting for transfers between devices  2.33 us (12%)
  local copies, waits for them, and re-layouts  1.13 us (6%)
  between operations  0.74 us (4%)
    ppermute x4, starting transfers between devices, shards(): got = [lax.ppermute(a, ('sec', 'xt'), m.pairs) for a, m in zip(sent, moves)]  6.06 us
    pallas_call x6, Pallas kernels, call(): pl.pallas_call(body, out_shape=outs, in_specs=[vmem] * (len(args) - fetch...  5.38 us
    ppermute x2, starting transfers between devices, shifted(): return lax.ppermute(x, axis, [(i, (i + shift) % n) for i in range(n)])  3.3 us
    ppermute x4, waiting for transfers between devices, shards(): got = [lax.ppermute(a, ('sec', 'xt'), m.pairs) for a, m in zip(sent, moves)]  2.06 us
    unnamed x10, local copies, waits for them, and re-layouts  1.05 us
  transfers between devices with their start and end apart: 6, of which 2 were waited for; matrix products, arithmetic and copies ran while one was open for 0% of the time, Pallas kernels for 17%

profile of v7, /device:TPU:0, one launch (start us, length us, event | category | flops | bytes accessed | tf_op | source)
XLA Modules:
  0.0 18.9 jit_solution(5554847422006391370)
XLA Ops:
  0.6 0.0 copy-start
  0.6 1.0 %copy-done = f32[8,32,512]{2,1,0:T(8,128)S(1)} copy-done((f32[8,32,512]{2,1,0:T(8,128)S(1)}, f32[8,32,512]{2,1,0:T(8,128)}, u32[]{:S(2)}) %copy-start) | copy-done | bytes 524312
  1.7 0.0 copy-start.1
  1.7 0.0 copy-start.2
  1.7 0.0 copy-start.3
  1.7 0.0 copy-start.4
  1.7 0.5 %collective-permute-start = (f32[8,32,128]{2,1,0:T(8,128)S(1)}, f32[8,32,128]{2,1,0:T(8,128)S(1)}, u32[]{:S(2)}, u32[]{:S(2)}) collective-permute-start(f32[8,32,128]{2,1,0:T(8,128)S(1)} %constant_dynamic-slice_fusion), channel_id=1, source_target_pairs={{0,1},{1,0},{2,3},{3,2},{4,5},{5,4},{6,7},{7,6},{8,9},{9,8},{10,11... | collective-permute-start | bytes 393224 | tf_op jit(solution)/shard_map/ppermute | solution.py:640
  2.2 0.3 %shard_map.85 = (bf16[4,256,256]{2,1,0:T(8,128)(2,1)S(1)}, bf16[160,256]{1,0:T(8,128)(2,1)S(1)}, bf16[512,128]{1,0:T(8,128)(2,1)S(1)}) custom-call(), custom_call_target="tpu_custom_call" | custom-call | flops 200000000 | bytes 737280 | tf_op jit(solution)/shard_map/pallas_call | solution.py:646
  2.6 0.7 %shard_map.86 = (f32[256,512]{1,0:T(8,128)S(1)}, f32[80,384]{1,0:T(8,128)S(1)}, f32[80,256]{1,0:T(8,128)S(1)}) custom-call(f32[5,32,512]{2,1,0:T(8,128)S(1)} %constant_dynamic-slice_fusion.2.first, f32[3,32,512]{2,1,0:T(8,128)S(1)} %constant_dynamic-slice_fusion.1.last, bf16[4,256,256]{2,1,0:T(8,128)(2,1)S(1)} %get-tuple-element.19.wx, ...), custom_call_target="tpu_custom_call" | custom-call | flops 200000000 | bytes 1859584 | tf_op jit(solution)/shard_map/pallas_call | solution.py:646
  3.3 0.0 collective-permute-done.refs_0_
  3.3 0.5 %shard_map.88 = f32[112,128]{1,0:T(8,128)S(1)} custom-call(f32[80,384]{1,0:T(8,128)S(1)} %get-tuple-element.27.fine_ref, f32[80,256]{1,0:T(8,128)S(1)} %get-tuple-element.28.coarse_ref, bf16[160,256]{1,0:T(8,128)(2,1)S(1)} %get-tuple-element.20.wy, bf16[512,128]{1,0:T(8,128)(2,1)S(1)} %get-tuple-element.22.wside, ...), custom_call_target="tpu_custom_call" | custom-call | flops 200000000 | bytes 1130496 | tf_op jit(solution)/shard_map/pallas_call | solution.py:646
  3.9 2.8 %collective-permute-start.1 = (f32[112,128]{1,0:T(8,128)S(1)}, f32[112,128]{1,0:T(8,128)S(1)}, u32[]{:S(2)}, u32[]{:S(2)}) collective-permute-start(f32[112,128]{1,0:T(8,128)S(1)} %shard_map.88), channel_id=1, source_target_pairs={{0,2},{2,0},{1,3},{3,1},{4,6},{6,4},{5,7},{7,5},{8,10},{10,8},{9,1... | collective-permute-start | bytes 172040 | tf_op jit(solution)/shard_map/ppermute | solution.py:640
  6.7 2.1 %shard_map.87 = (f32[336,384]{1,0:T(8,128)S(1)}, f32[192,256]{1,0:T(8,128)S(1)}, bf16[336,128]{1,0:T(8,128)(2,1)S(1)}, bf16[192,128]{1,0:T(8,128)(2,1)S(1)}) custom-call(f32[256,512]{1,0:T(8,128)S(1)} %get-tuple-element.21.total, bf16[512,128]{1,0:T(8,128)(2,1)S(1)} %get-tuple-element.22.wside, f32[5,32,512]{2,1,0:T(8,128)S(1)} %constant_dynamic-slice_fusion.2.first, ...), custom_call_target="tpu_custom_call" | custom-call | flops 200000000 | bytes 8646656 | tf_op jit(solution)/shard_map/pallas_call | solution.py:646
  8.8 0.3 %collective-permute-done.1.refs_0_ = f32[112,128]{1,0:T(8,128)S(1)} collective-permute-done((f32[112,128]{1,0:T(8,128)S(1)}, f32[112,128]{1,0:T(8,128)S(1)}, u32[]{:S(2)}, u32[]{:S(2)}) %collective-permute-start.1) | collective-permute-done | bytes 57376 | tf_op jit(solution)/shard_map/ppermute | solution.py:640
  9.0 0.4 %shard_map.89 = (f32[112,384]{1,0:T(8,128)S(1)}, f32[48,256]{1,0:T(8,128)S(1)}, f32[184,128]{1,0:T(8,128)S(1)}, f32[160,128]{1,0:T(8,128)S(1)}, f32[24,128]{1,0:T(8,128)S(1)}, /*index=5*/f32[192,128]{1,0:T(8,128)S(1)}) custom-call(f32[336,384]{1,0:T(8,128)S(1)} %get-tuple-element.23.fine_made, f32[192,256]{1,0:T(8,128)S(1)} %get-tuple-element.24.coarse_made, ...), custom_call_target="tpu_custom_call" | custom-call | flops 200000000 | bytes 1413120 | tf_op jit(solution)/shard_map/pallas_call | solution.py:646
  9.4 2.0 %collective-permute-start.5 = (f32[192,128]{1,0:T(8,128)S(1)}, f32[192,128]{1,0:T(8,128)S(1)}, u32[]{:S(2)}, u32[]{:S(2)}) collective-permute-start(f32[192,128]{1,0:T(8,128)S(1)} %get-tuple-element.34), channel_id=1, source_target_pairs={{0,4},{1,5},{4,8},{5,9},{8,0},{9,1},{12,13},{13,12},{2,6},{3,7},{6... | collective-permute-start | bytes 294920 | tf_op jit(solution)/shard_map/ppermute | solution.py:810
  11.3 1.1 %collective-permute-start.2 = (f32[184,128]{1,0:T(8,128)S(1)}, f32[184,128]{1,0:T(8,128)S(1)}, u32[]{:S(2)}, u32[]{:S(2)}) collective-permute-start(f32[184,128]{1,0:T(8,128)S(1)} %get-tuple-element.31), channel_id=1, source_target_pairs={{0,8},{1,9},{4,0},{5,1},{8,12},{9,13},{12,4},{13,5},{2,10},{3,11},... | collective-permute-start | bytes 282632 | tf_op jit(solution)/shard_map/ppermute | solution.py:810
  12.4 0.0 collective-permute-start.3
  12.4 3.0 %collective-permute-start.4 = (f32[24,128]{1,0:T(8,128)S(1)}, f32[24,128]{1,0:T(8,128)S(1)}, u32[]{:S(2)}, u32[]{:S(2)}) collective-permute-start(f32[24,128]{1,0:T(8,128)S(1)} %get-tuple-element.33), channel_id=1, source_target_pairs={{0,12},{1,13},{4,0},{5,1},{8,4},{9,5},{12,8},{13,9},{2,14},{3,15},... | collective-permute-start | bytes 36872 | tf_op jit(solution)/shard_map/ppermute | solution.py:810
  15.5 2.1 %collective-permute-done.4.refs_2_ = f32[24,128]{1,0:T(8,128)S(1)} collective-permute-done((f32[24,128]{1,0:T(8,128)S(1)}, f32[24,128]{1,0:T(8,128)S(1)}, u32[]{:S(2)}, u32[]{:S(2)}) %collective-permute-start.4) | collective-permute-done | bytes 12320 | tf_op jit(solution)/shard_map/ppermute | solution.py:810
  17.5 0.0 collective-permute-done.3.refs_1_
  17.5 0.0 collective-permute-done.2.refs_0_
  17.5 0.0 collective-permute-done.5.refs_3_
  17.5 0.0 copy-done.1
  17.5 0.0 copy-done.2
  17.5 0.0 copy-done.3
  17.6 0.0 copy-done.4
  17.6 1.4 %shard_map.90 = (f32[8,32,512]{2,1,0:T(8,128)}, f32[4,16,256]{2,1,0:T(8,128)}, f32[2,8,128]{2,1,0:T(8,128)}) custom-call(f32[5,32,512]{2,1,0:T(8,128)S(1)} %constant_dynamic-slice_fusion.2.first, f32[3,32,512]{2,1,0:T(8,128)S(1)} %constant_dynamic-slice_fusion.1.last, f32[112,384]{1,0:T(8,128)S(1)} %get-tuple-element.29.fine_ref, ...), custom_call_target="tpu_custom_call" | custom-call | flops 200000000 | bytes 2805760 | tf_op jit(solution)/shard_map/pallas_call | solution.py:646
  (3 shorter events, 0.1 us)
Async XLA Ops:
  0.6 1.0 %copy-start = (f32[8,32,512]{2,1,0:T(8,128)S(1)}, f32[8,32,512]{2,1,0:T(8,128)}, u32[]{:S(2)}) copy-start(f32[8,32,512]{2,1,0:T(8,128)} %param.6) | copy-start | bytes 1572868
  1.7 15.9 %copy-start.1 = (bf16[768,512]{1,0:T(8,128)(2,1)S(1)}, bf16[768,512]{1,0:T(8,128)(2,1)}, u32[]{:S(2)}) copy-start(bf16[768,512]{1,0:T(8,128)(2,1)} %constant.22.clone.refs_4_) | copy-start | bytes 2359300
  1.7 15.9 %copy-start.2 = (bf16[512,256]{1,0:T(8,128)(2,1)S(1)}, bf16[512,256]{1,0:T(8,128)(2,1)}, u32[]{:S(2)}) copy-start(bf16[512,256]{1,0:T(8,128)(2,1)} %constant.24.clone.refs_6_) | copy-start | bytes 786436
  1.7 15.9 %copy-start.3 = (bf16[256,224]{1,0:T(8,128)(2,1)S(1)}, bf16[256,224]{1,0:T(8,128)(2,1)}, u32[]{:S(2)}) copy-start(bf16[256,224]{1,0:T(8,128)(2,1)} %constant.23.clone.refs_5_) | copy-start | bytes 344068
  1.7 15.9 %copy-start.4 = (bf16[64,96]{1,0:T(8,128)(2,1)S(1)}, bf16[64,96]{1,0:T(8,128)(2,1)}, u32[]{:S(2)}) copy-start(bf16[64,96]{1,0:T(8,128)(2,1)} %constant.25.clone.refs_7_) | copy-start | bytes 36868
  1.7 1.6 %collective-permute-start = (f32[8,32,128]{2,1,0:T(8,128)S(1)}, f32[8,32,128]{2,1,0:T(8,128)S(1)}, u32[]{:S(2)}, u32[]{:S(2)}) collective-permute-start(f32[8,32,128]{2,1,0:T(8,128)S(1)} %constant_dynamic-slice_fusion), channel_id=1, source_target_pairs={{0,1},{1,0},{2,3},{3,2},{4,5},{5,4},{6,7},{7,6},{8,9},{9,8},{10,11... | collective-permute-start | bytes 393224 | tf_op jit(solution)/shard_map/ppermute | solution.py:640
  3.9 5.1 %collective-permute-start.1 = (f32[112,128]{1,0:T(8,128)S(1)}, f32[112,128]{1,0:T(8,128)S(1)}, u32[]{:S(2)}, u32[]{:S(2)}) collective-permute-start(f32[112,128]{1,0:T(8,128)S(1)} %shard_map.88), channel_id=1, source_target_pairs={{0,2},{2,0},{1,3},{3,1},{4,6},{6,4},{5,7},{7,5},{8,10},{10,8},{9,1... | collective-permute-start | bytes 172040 | tf_op jit(solution)/shard_map/ppermute | solution.py:640
  9.4 8.1 %collective-permute-start.5 = (f32[192,128]{1,0:T(8,128)S(1)}, f32[192,128]{1,0:T(8,128)S(1)}, u32[]{:S(2)}, u32[]{:S(2)}) collective-permute-start(f32[192,128]{1,0:T(8,128)S(1)} %get-tuple-element.34), channel_id=1, source_target_pairs={{0,4},{1,5},{4,8},{5,9},{8,0},{9,1},{12,13},{13,12},{2,6},{3,7},{6... | collective-permute-start | bytes 294920 | tf_op jit(solution)/shard_map/ppermute | solution.py:810
  11.3 6.2 %collective-permute-start.2 = (f32[184,128]{1,0:T(8,128)S(1)}, f32[184,128]{1,0:T(8,128)S(1)}, u32[]{:S(2)}, u32[]{:S(2)}) collective-permute-start(f32[184,128]{1,0:T(8,128)S(1)} %get-tuple-element.31), channel_id=1, source_target_pairs={{0,8},{1,9},{4,0},{5,1},{8,12},{9,13},{12,4},{13,5},{2,10},{3,11},... | collective-permute-start | bytes 282632 | tf_op jit(solution)/shard_map/ppermute | solution.py:810
  12.4 5.1 %collective-permute-start.3 = (f32[160,128]{1,0:T(8,128)S(1)}, f32[160,128]{1,0:T(8,128)S(1)}, u32[]{:S(2)}, u32[]{:S(2)}) collective-permute-start(f32[160,128]{1,0:T(8,128)S(1)} %get-tuple-element.32), channel_id=1, source_target_pairs={{0,1},{1,0},{4,12},{5,13},{8,4},{9,5},{12,8},{13,9},{2,3},{3,2},{6... | collective-permute-start | bytes 245768 | tf_op jit(solution)/shard_map/ppermute | solution.py:810
  12.4 5.1 %collective-permute-start.4 = (f32[24,128]{1,0:T(8,128)S(1)}, f32[24,128]{1,0:T(8,128)S(1)}, u32[]{:S(2)}, u32[]{:S(2)}) collective-permute-start(f32[24,128]{1,0:T(8,128)S(1)} %get-tuple-element.33), channel_id=1, source_target_pairs={{0,12},{1,13},{4,0},{5,1},{8,4},{9,5},{12,8},{13,9},{2,14},{3,15},... | collective-permute-start | bytes 36872 | tf_op jit(solution)/shard_map/ppermute | solution.py:810
